TPU v7x, 32 devices: a whole 2x2x4 slice. The times are simulated.
32 devices in a mesh: dp: 16 (over z, y, x), mp: 2 (over core).
Axes of the slice: x: 2, y: 2, z: 4, core: 2. Of those that a mesh axis runs over, the one named last changes fastest.
Arguments:
- history: bfloat16 [8, 16384, 768], P(None, ('dp', 'mp')), may hold values from -6 to 6
- depth_weights: float32 [8], replicated, may hold values from -0.6 to 0.6
- gain_attn: float32 [768], replicated, may hold values from 0.25 to 1.75
- gain_mlp: float32 [768], replicated, may hold values from 0.25 to 1.75
- qkv_weight: bfloat16 [3, 768, 768], P(None, None, 'mp'), may hold values from -0.21875 to 0.21875
- out_weight: bfloat16 [768, 768], P('mp'), may hold values from -0.875 to 0.875
- up_weight: bfloat16 [768, 3072], P(None, 'mp'), may hold values from -0.21875 to 0.21875
- down_weight: bfloat16 [3072, 768], P('mp'), may hold values from -0.109375 to 0.109375
- cotangent: bfloat16 [16384, 768], P(('dp', 'mp')), may hold values from -6 to 6
Outputs:
- block_out: bfloat16 [16384, 768], P(('dp', 'mp'))
- grad_history: bfloat16 [8, 16384, 768], P(None, ('dp', 'mp'))
- grad_depth: float32 [8], replicated
- grad_gain_attn: float32 [768], replicated
- grad_gain_mlp: float32 [768], replicated
- grad_qkv: float32 [3, 768, 768], P(None, None, 'mp')
- grad_out_proj: float32 [768, 768], P('mp')
- grad_up: float32 [768, 3072], P(None, 'mp')
- grad_down: float32 [3072, 768], P('mp')
All inputs are finite; a program needn't handle non-finite values.
Results may differ from a plain program's by a relative error of at most 0.018.
Values may be sent and summed in bfloat16 or wider, within the bound.
No kernel may reach another device: no remote copies, remote signals or barrier semaphores. Data moves between devices by JAX's collectives and lax.ppermute only.
A program may use at most 192 MiB of HBM per device.

v0:
```python
import jax
import jax.numpy as jnp
from jax import lax
from jax.sharding import PartitionSpec as P

HEAD_DIM = 64
SEQ_LEN = 1024


EPSILON = 1e-05
SQRT_HALF = 0.7071067811865476
INV_ROOT_TWO_PI = 0.3989422804014327


def layer_norm(inputs, gain_row):
    row_mean = jnp.mean(inputs, axis=-1, keepdims=True)
    centered = inputs - row_mean
    variance = jnp.mean(centered * centered, axis=-1, keepdims=True)
    inv_scale = lax.rsqrt(variance + EPSILON)
    normed = centered * inv_scale
    return (normed * gain_row, normed, inv_scale)


def norm_back(grad_rows, gain_row, normed, inv_scale):
    scaled = grad_rows * gain_row
    first_mean = jnp.mean(scaled, axis=-1, keepdims=True)
    second_mean = jnp.mean(scaled * normed, axis=-1, keepdims=True)
    return (
        inv_scale * (scaled - first_mean - normed * second_mean),
        jnp.sum(grad_rows * normed, axis=0),
    )


def gelu_value(inputs):
    return 0.5 * inputs * (1.0 + lax.erf(inputs * SQRT_HALF))


def gelu_slope(inputs):
    normal_cdf = 0.5 * (1.0 + lax.erf(inputs * SQRT_HALF))
    return normal_cdf + inputs * jnp.exp(-0.5 * inputs * inputs) * INV_ROOT_TWO_PI


def masked_scores(queries, key_rows):
    length = queries.shape[0]
    scores = jnp.einsum(
        "qhe,khe->hqk", queries, key_rows, preferred_element_type=jnp.float32
    ) * HEAD_DIM ** (-0.5)
    row_ids = lax.broadcasted_iota(jnp.int32, (length, length), 0)
    col_ids = lax.broadcasted_iota(jnp.int32, (length, length), 1)
    return jnp.where((col_ids <= row_ids)[None], scores, -jnp.inf)


def attend_block(packed):
    queries, key_rows, value_rows = packed
    scores = masked_scores(queries, key_rows)
    row_max = jnp.max(scores, axis=-1, keepdims=True)
    exponent = jnp.exp(scores - row_max)
    row_total = jnp.sum(exponent, axis=-1, keepdims=True)
    attn_probs = (exponent / row_total).astype(jnp.bfloat16)
    attended = jnp.einsum(
        "hqk,khe->qhe", attn_probs, value_rows, preferred_element_type=jnp.float32
    )
    return (attended.astype(jnp.bfloat16), row_max + jnp.log(row_total))


def attend_back(packed):
    queries, key_rows, value_rows, grad_att, log_total = packed
    scale_factor = HEAD_DIM ** (-0.5)
    attn_probs = jnp.exp(masked_scores(queries, key_rows) - log_total)
    grad_values = jnp.einsum(
        "hqk,qhe->khe",
        attn_probs.astype(jnp.bfloat16),
        grad_att,
        preferred_element_type=jnp.float32,
    )
    grad_probs = jnp.einsum(
        "qhe,khe->hqk", grad_att, value_rows, preferred_element_type=jnp.float32
    )
    row_dot = jnp.sum(grad_probs * attn_probs, axis=-1, keepdims=True)
    grad_scores = (attn_probs * (grad_probs - row_dot)).astype(jnp.bfloat16)
    grad_queries = (
        jnp.einsum("hqk,khe->qhe", grad_scores, key_rows, preferred_element_type=jnp.float32)
        * scale_factor
    )
    grad_keys = (
        jnp.einsum("hqk,qhe->khe", grad_scores, queries, preferred_element_type=jnp.float32)
        * scale_factor
    )
    return (
        grad_queries.astype(jnp.bfloat16),
        grad_keys.astype(jnp.bfloat16),
        grad_values.astype(jnp.bfloat16),
    )


def shards(
    history,
    depth_weights,
    gain_attn,
    gain_mlp,
    qkv_weight,
    out_weight,
    up_weight,
    down_weight,
    cotangent,
):
    mixed_rows = depth_weights[0] * history[0].astype(jnp.float32)
    for layer_index in range(1, history.shape[0]):
        mixed_rows = mixed_rows + depth_weights[layer_index] * history[layer_index].astype(
            jnp.float32
        )
    first_out, first_normed, first_inv = layer_norm(mixed_rows, gain_attn)
    first_rows = lax.all_gather(first_out.astype(jnp.bfloat16), "mp", axis=0, tiled=True)
    all_rows = first_rows.shape[0]
    local_width = qkv_weight.shape[2]
    head_local = local_width // HEAD_DIM
    seq_count = all_rows // SEQ_LEN
    qkv_rows = jnp.einsum(
        "td,cde->cte", first_rows, qkv_weight, preferred_element_type=jnp.float32
    ).astype(jnp.bfloat16)
    shaped = qkv_rows.reshape(3, seq_count, SEQ_LEN, head_local, HEAD_DIM)
    attended, log_total = lax.map(attend_block, (shaped[0], shaped[1], shaped[2]))
    attended = attended.reshape(all_rows, local_width)

    def out_term():
        return jnp.dot(attended, out_weight, preferred_element_type=jnp.float32)

    branch = lax.psum_scatter(
        out_term().astype(jnp.bfloat16), "mp", scatter_dimension=0, tiled=True
    ).astype(jnp.float32)
    middle = mixed_rows + branch
    second_out, second_normed, second_inv = layer_norm(middle, gain_mlp)
    second_rows = lax.all_gather(second_out.astype(jnp.bfloat16), "mp", axis=0, tiled=True)
    pre_act = jnp.dot(second_rows, up_weight, preferred_element_type=jnp.float32)
    hidden = gelu_value(pre_act).astype(jnp.bfloat16)
    hidden_part = hidden
    block_out = (
        middle
        + lax.psum_scatter(
            jnp.dot(hidden_part, down_weight, preferred_element_type=jnp.float32).astype(
                jnp.bfloat16
            ),
            "mp",
            scatter_dimension=0,
            tiled=True,
        ).astype(jnp.float32)
    ).astype(jnp.bfloat16)
    branch_again = lax.psum_scatter(
        out_term().astype(jnp.bfloat16), "mp", scatter_dimension=0, tiled=True
    ).astype(jnp.float32)
    second_back, second_normed, second_inv = layer_norm(mixed_rows + branch_again, gain_mlp)
    second_rows = lax.all_gather(second_back.astype(jnp.bfloat16), "mp", axis=0, tiled=True)
    contract_rows = (((0,), (0,)), ((), ()))
    contract_cols = (((1,), (1,)), ((), ()))
    block_rows = lax.all_gather(cotangent, "mp", axis=0, tiled=True)
    hidden_part = hidden
    grad_down_w = lax.dot_general(
        hidden_part, block_rows, contract_rows, preferred_element_type=jnp.float32
    )
    hidden_rows = lax.dot_general(
        block_rows, down_weight, contract_cols, preferred_element_type=jnp.float32
    )
    grad_hidden = hidden_rows
    grad_down, grad_hidden = (grad_down_w, grad_hidden)
    grad_pre = (grad_hidden * gelu_slope(pre_act)).astype(jnp.bfloat16)
    grad_up = lax.dot_general(
        second_rows, grad_pre, contract_rows, preferred_element_type=jnp.float32
    )
    grad_second = lax.psum_scatter(
        lax.dot_general(
            grad_pre, up_weight, contract_cols, preferred_element_type=jnp.float32
        ).astype(jnp.bfloat16),
        "mp",
        scatter_dimension=0,
        tiled=True,
    ).astype(jnp.float32)
    middle_part, grad_gain_mlp = norm_back(grad_second, gain_mlp, second_normed, second_inv)
    grad_middle = cotangent.astype(jnp.float32) + middle_part
    block_rows = lax.all_gather(grad_middle.astype(jnp.bfloat16), "mp", axis=0, tiled=True)
    grad_out_w = lax.dot_general(
        attended, block_rows, contract_rows, preferred_element_type=jnp.float32
    )
    att_rows = lax.dot_general(
        block_rows, out_weight, contract_cols, preferred_element_type=jnp.float32
    )
    grad_att = att_rows
    grad_out_proj, grad_att = (grad_out_w, grad_att)
    grad_att = grad_att.astype(jnp.bfloat16).reshape(seq_count, SEQ_LEN, head_local, HEAD_DIM)
    attn_grads = lax.map(attend_back, (shaped[0], shaped[1], shaped[2], grad_att, log_total))
    grad_rows_qkv = jnp.stack(attn_grads).reshape(3, all_rows, local_width)
    grad_qkv = jnp.einsum(
        "td,cte->cde", first_rows, grad_rows_qkv, preferred_element_type=jnp.float32
    )
    grad_first = lax.psum_scatter(
        jnp.einsum(
            "cte,cde->td", grad_rows_qkv, qkv_weight, preferred_element_type=jnp.float32
        ).astype(jnp.bfloat16),
        "mp",
        scatter_dimension=0,
        tiled=True,
    ).astype(jnp.float32)
    mixed_part, grad_gain_attn = norm_back(grad_first, gain_attn, first_normed, first_inv)
    grad_mixed = grad_middle + mixed_part
    grad_history = (depth_weights[:, None, None] * grad_mixed[None]).astype(jnp.bfloat16)
    depth_terms = [
        jnp.sum(history[layer_index].astype(jnp.float32) * grad_mixed)
        for layer_index in range(history.shape[0])
    ]
    grad_depth = jnp.stack(depth_terms)
    grad_gain_attn, grad_gain_mlp, grad_depth = lax.psum(
        (grad_gain_attn, grad_gain_mlp, grad_depth), "mp"
    )
    grad_qkv, grad_out_proj, grad_up, grad_down, grad_gain_attn, grad_gain_mlp, grad_depth = (
        lax.psum(
            (
                grad_qkv,
                grad_out_proj,
                grad_up,
                grad_down,
                grad_gain_attn,
                grad_gain_mlp,
                grad_depth,
            ),
            "dp",
        )
    )
    return (
        block_out,
        grad_history,
        grad_depth,
        grad_gain_attn,
        grad_gain_mlp,
        grad_qkv,
        grad_out_proj,
        grad_up,
        grad_down,
    )


def solution(mesh):
    in_specs = (
        P(None, ("dp", "mp"), None),
        P(),
        P(),
        P(),
        P(None, None, "mp"),
        P("mp", None),
        P(None, "mp"),
        P("mp", None),
        P(("dp", "mp"), None),
    )
    out_specs = (
        P(("dp", "mp"), None),
        P(None, ("dp", "mp"), None),
        P(),
        P(),
        P(),
        P(None, None, "mp"),
        P("mp", None),
        P(None, "mp"),
        P("mp", None),
    )
    return jax.shard_map(shards, mesh=mesh, in_specs=in_specs, out_specs=out_specs, check_vma=False)
```

profile of v0, /device:TPU:0, one launch (start us, length us, event | category | flops | bytes accessed | tf_op | source)
XLA Modules:
  0.0 675.8 jit_solution(10533614835639184866)
XLA Ops:
  8.8 9.3 %fusion.55 = (f32[512]{0:T(512)S(1)}, f32[512,768]{1,0:T(8,128)S(1)}) fusion(bf16[8,512,768]{2,1,0:T(8,128)(2,1)} %param.9, f32[]{:T(128)} %bitcast.14, f32[]{:T(128)} %bitcast.12, f32[]{:T(128)} %bitcast.10, f32[]{:T(128)} %bitcast.8, f32[]{:T(128)} %bitcast.6, f32[]{:T(128)} %bitcast.4, f32[]{:T(128)} %bitcast.2, f32[]{:T(128)} %bitcast), kind=kLoop, calls=%fused_computation.108 | loop fusion | flops 9436672 | bytes 7866400 | tf_op jit(solution)/shard_map/reduce_sum | solution.py:16
  22.3 11.3 %all-gather.5.cloned.1.call-done = bf16[1024,768]{1,0:T(8,128)(2,1)} async-done(((bf16[512,768]{1,0:T(8,128)(2,1)}), bf16[1024,768]{1,0:T(8,128)(2,1)}) %all-gather.5.cloned.1.call-update) | async-done | bytes 1572880 | tf_op jit(solution)/shard_map/all_gather | solution.py:113
  33.6 4.0 convert_bitcast_fusion
  39.1 10.5 %fusion.59 = (f32[6,1024]{1,0:T(8,128)S(1)}, f32[6,1024,1024]{1,2,0:T(8,128)}) fusion(bf16[1024,6,64]{0,2,1:T(8,128)(2,1)S(1)} %bitcast.115, bf16[1024,6,64]{0,2,1:T(8,128)(2,1)S(1)} %bitcast.113, pred[1024,1024]{0,1:T(8,128)(4,1)S(1)} %copy-done.8), kind=kOutput, calls=%fused_computation.111 | convolution fusion | flops 824174592 | bytes 27811840 | tf_op jit(solution)/shard_map/while/body/eval_jaxpr/qhe,khe->hqk/dot_general | solution.py:45
  49.6 10.2 %fusion = f32[6,1024]{1,0:T(8,128)S(1)} fusion(f32[6,1024,1024]{1,2,0:T(8,128)} %get-tuple-element.107, f32[6,1024]{1,0:T(8,128)S(1)} %get-tuple-element.106), kind=kLoop, calls=%fused_computation.6 | loop fusion | flops 12576768 | bytes 25214976 | tf_op jit(solution)/shard_map/while/body/eval_jaxpr/reduce_sum | solution.py:58
  59.8 10.6 %fusion.48 = bf16[6,64,1024]{2,1,0:T(8,128)(2,1)S(1)} fusion(bf16[1024,6,64]{0,2,1:T(8,128)(2,1)S(1)} %bitcast.124, f32[6,1024,1024]{1,2,0:T(8,128)} %get-tuple-element.107, f32[6,1024]{1,0:T(8,128)S(1)} %fusion, f32[6,1024]{1,0:T(8,128)S(1)} %get-tuple-element.106), kind=kOutput, calls=%fused_computation.94 | convolution fusion | flops 824573952 | bytes 26787840 | tf_op jit(solution)/shard_map/while/body/eval_jaxpr/hqk,khe->qhe/dot_general | solution.py:60
  73.5 10.3 %reduce-scatter.5.cloned.1.call-done = bf16[512,768]{1,0:T(8,128)(2,1)} async-done(((bf16[1024,768]{1,0:T(8,128)(2,1)}), bf16[512,768]{1,0:T(8,128)(2,1)}) %reduce-scatter.5.cloned.1.call-update) | async-done | bytes 786448 | tf_op jit(solution)/shard_map/reduce_scatter | solution.py:128
  89.2 10.0 %all-gather.7.cloned.1.call-done = bf16[1024,768]{1,0:T(8,128)(2,1)} async-done(((bf16[512,768]{1,0:T(8,128)(2,1)}), bf16[1024,768]{1,0:T(8,128)(2,1)}) %all-gather.7.cloned.1.call-update) | async-done | bytes 1572880 | tf_op jit(solution)/shard_map/all_gather | solution.py:133
  99.2 6.7 multiply_convert_fusion.2
  105.9 5.8 all-gather.9.cloned.1.call-done
  111.7 6.6 fusion.11
  123.8 6.4 convolution_convert_fusion.2
  130.3 3.9 reduce-scatter.9.cloned.1.call-done
  136.1 11.0 %reduce-scatter.7.cloned.1.call-done = bf16[512,768]{1,0:T(8,128)(2,1)} async-done(((bf16[1024,768]{1,0:T(8,128)(2,1)}), bf16[512,768]{1,0:T(8,128)(2,1)}) %reduce-scatter.7.cloned.1.call-update) | async-done | bytes 786448 | tf_op jit(solution)/shard_map/reduce_scatter | solution.py:139
  147.1 3.8 fusion.52
  151.2 10.9 %all-gather.11.cloned.1.call-done = bf16[1024,768]{1,0:T(8,128)(2,1)} async-done(((bf16[512,768]{1,0:T(8,128)(2,1)}), bf16[1024,768]{1,0:T(8,128)(2,1)}) %all-gather.11.cloned.1.call-update) | async-done | bytes 1572880 | tf_op jit(solution)/shard_map/all_gather | solution.py:179
  164.4 10.4 %fusion.45 = bf16[6,64,1024]{2,1,0:T(8,128)(2,1)S(1)} fusion(bf16[1024,6,64]{0,2,1:T(8,128)(2,1)S(1)} %bitcast.120, f32[6,1024,1024]{1,2,0:T(8,128)} %get-tuple-element.107, f32[6,1024]{1,0:T(8,128)S(1)} %log_add_fusion), kind=kOutput, calls=%fused_computation.93 | convolution fusion | flops 818282496 | bytes 26763264 | tf_op jit(solution)/shard_map/while/body/eval_jaxpr/hqk,qhe->khe/dot_general | solution.py:70
  174.8 15.5 %multiply_reduce_fusion = (f32[6,1024]{1,0:T(8,128)S(1)}, f32[6,1024,1024]{1,2,0:T(8,128)}) fusion(f32[6,1024,1024]{1,2,0:T(8,128)} %get-tuple-element.107, f32[6,1024]{1,0:T(8,128)S(1)} %log_add_fusion, bf16[1024,6,64]{0,2,1:T(8,128)(2,1)S(1)} %bitcast.121, bf16[1024,6,64]{0,2,1:T(8,128)(2,1)S(1)} %bitcast.125), kind=kOutput, calls=%fused_computation.1 | convolution fusion | flops 824174592 | bytes 51953664 | tf_op jit(solution)/shard_map/while/body/eval_jaxpr/qhe,khe->hqk/dot_general | solution.py:76
  190.4 21.4 %multiply_convert_fusion = bf16[6,1024,1024]{1,2,0:T(8,128)(2,1)} fusion(f32[6,1024,1024]{1,2,0:T(8,128)} %get-tuple-element.111, f32[6,1024,1024]{1,2,0:T(8,128)} %get-tuple-element.107, f32[6,1024]{1,0:T(8,128)S(1)} %get-tuple-element.110, f32[6,1024]{1,0:T(8,128)S(1)} %log_add_fusion), kind=kLoop, calls=%fused_computation | loop fusion | flops 25165824 | bytes 62963712 | tf_op jit(solution)/shard_map/while/body/eval_jaxpr/convert_element_type | solution.py:80
  211.7 8.5 %multiply_convert_fusion.3 = bf16[6,64,1024]{2,1,0:T(8,128)(2,1)S(1)} fusion(bf16[1024,6,64]{0,2,1:T(8,128)(2,1)S(1)} %bitcast.116, bf16[6,1024,1024]{1,2,0:T(8,128)(2,1)} %multiply_convert_fusion), kind=kOutput, calls=%fused_computation.82 | convolution fusion | flops 806092800 | bytes 14155776 | tf_op jit(solution)/shard_map/while/body/eval_jaxpr/hqk,qhe->khe/dot_general | solution.py:86
  220.2 6.9 %multiply_convert_fusion.4 = bf16[6,64,1024]{2,1,0:T(8,128)(2,1)S(1)} fusion(bf16[1024,6,64]{0,2,1:T(8,128)(2,1)S(1)} %bitcast.114, bf16[6,1024,1024]{1,2,0:T(8,128)(2,1)} %multiply_convert_fusion), kind=kOutput, calls=%fused_computation.83 | convolution fusion | flops 806092800 | bytes 14155776 | tf_op jit(solution)/shard_map/while/body/eval_jaxpr/hqk,khe->qhe/dot_general | solution.py:82
  229.6 4.9 bitcast_convert_fusion
  235.9 6.5 fusion.61
  242.5 4.4 fusion.62
  249.1 3.9 convolution_bitcast_fusion
  256.6 6.5 fusion.42
  263.1 5.1 stack.51
  270.7 47.0 %all-reduce = (f32[8]{0:T(128)}, f32[768]{0:T(1024)}, f32[768]{0:T(1024)}) all-reduce(f32[8]{0:T(128)S(1)} %get-tuple-element.84, f32[768]{0:T(1024)S(1)} %get-tuple-element.85, f32[768]{0:T(1024)S(1)} %get-tuple-element.86), channel_id=1, replica_groups=mesh['dp'=16,'mp'=2] {'dp'}, use_global_device_ids=true, to_apply=%region_24.25 | all-reduce | flops 1544 | bytes 12352 | tf_op jit(solution)/shard_map/psum | solution.py:214
  317.7 6.0 multiply_convert_fusion.1
  323.7 330.1 %all-reduce.5.cloned.1.call-done = (f32[3,768,384]{1,2,0:T(8,128)}, f32[384,768]{1,0:T(8,128)}, f32[768,1536]{1,0:T(8,128)}, f32[1536,768]{1,0:T(8,128)}) async-done(((f32[3,768,384]{1,2,0:T(8,128)}, f32[384,768]{1,0:T(8,128)}, f32[768,1536]{1,0:T(8,128)}, f32[1536,768]{1,0:T(8,128)}), (f32[3,768,384]{1,2,0:T(8,128)}, f32[384,768]{1,0:T(8,128)}, f32[768,1536]{1,0:T(8,128)}, ...) | async-done | bytes 14155792 | tf_op jit(solution)/shard_map/psum | solution.py:214
  653.9 5.2 copy.27
  660.1 5.5 copy.39
  (124 shorter events, 42.1 us)
Async XLA Ops:
  7.2 92.0 %copy-start = (bf16[768,1536]{1,0:T(8,128)(2,1)S(1)}, bf16[768,1536]{1,0:T(8,128)(2,1)}, u32[]{:S(2)}) copy-start(bf16[768,1536]{1,0:T(8,128)(2,1)} %param.15) | copy-start | bytes 7077892
  7.2 26.4 %all-gather.5.cloned.1.call-start = ((), (), s32[]{:S(2)}) async-start(), calls=%async_computation.4 | async-start | bytes 2359296 | tf_op jit(solution)/shard_map/all_gather | solution.py:113
  18.1 1.7 copy-start.25
  21.0 62.8 %reduce-scatter.5.cloned.1.call-start = ((), (), s32[]{:S(2)}) async-start(), calls=%async_computation.5 | async-start | bytes 2359296 | tf_op jit(solution)/shard_map/reduce_scatter | solution.py:128
  37.9 11.7 %copy-start.6 = (bf16[1,1024,384]{1,2,0:T(8,128)(2,1)}, bf16[1,1024,384]{1,2,0:T(8,128)(2,1)S(1)}, u32[]{:S(2)}) copy-start(bf16[1,1024,384]{1,2,0:T(8,128)(2,1)S(1)} %get-tuple-element.95) | copy-start | bytes 2359300
  37.9 21.9 %copy-start.13 = (bf16[1,1024,384]{1,2,0:T(8,128)(2,1)}, bf16[1,1024,384]{1,2,0:T(8,128)(2,1)S(1)}, u32[]{:S(2)}) copy-start(bf16[1,1024,384]{1,2,0:T(8,128)(2,1)S(1)} %get-tuple-element.96) | copy-start | bytes 2359300
  59.8 11.5 %copy-start.32 = (bf16[384,768]{1,0:T(8,128)(2,1)S(1)}, bf16[384,768]{1,0:T(8,128)(2,1)}, u32[]{:S(2)}) copy-start(bf16[384,768]{1,0:T(8,128)(2,1)} %param.14) | copy-start | bytes 1769476
  73.4 25.8 %all-gather.7.cloned.1.call-start = ((), (), s32[]{:S(2)}) async-start(), calls=%async_computation.6 | async-start | bytes 2359296 | tf_op jit(solution)/shard_map/all_gather | solution.py:133
  88.1 23.6 %all-gather.9.cloned.1.call-start = ((), (), s32[]{:S(2)}) async-start(), calls=%async_computation.8 | async-start | bytes 2359296 | tf_op jit(solution)/shard_map/all_gather | solution.py:155
  88.6 45.5 %reduce-scatter.9.cloned.1.call-start = ((), (), s32[]{:S(2)}) async-start(), calls=%async_computation.9 | async-start | bytes 2359296 | tf_op jit(solution)/shard_map/reduce_scatter | solution.py:169
  123.8 23.4 %reduce-scatter.7.cloned.1.call-start = ((), (), s32[]{:S(2)}) async-start(), calls=%async_computation.7 | async-start | bytes 2359296 | tf_op jit(solution)/shard_map/reduce_scatter | solution.py:139
  130.2 4.0 copy-start.5
  130.2 16.9 %copy-start.12 = (bf16[512,768]{1,0:T(8,128)(2,1)S(1)}, bf16[512,768]{1,0:T(8,128)(2,1)}, u32[]{:S(2)}) copy-start(bf16[512,768]{1,0:T(8,128)(2,1)} %param.17) | copy-start | bytes 2359300
  130.2 31.9 %all-gather.11.cloned.1.call-start = ((), (), s32[]{:S(2)}) async-start(), calls=%async_computation.10 | async-start | bytes 2359296 | tf_op jit(solution)/shard_map/all_gather | solution.py:179
  150.9 102.1 %reduce-scatter.11.cloned.1.call-start = ((), (), s32[]{:S(2)}) async-start(), calls=%async_computation.11 | async-start | bytes 2359296 | tf_op jit(solution)/shard_map/reduce_scatter | solution.py:194
  164.4 10.4 %copy-start.14 = (bf16[1,1024,384]{1,2,0:T(8,128)(2,1)S(1)}, bf16[1,1024,384]{1,2,0:T(8,128)(2,1)}, u32[]{:S(2)}) copy-start(bf16[1,1024,384]{1,2,0:T(8,128)(2,1)} %copy-done.13) | copy-start | bytes 2359300
  190.4 21.4 %copy-start.7 = (bf16[1,1024,384]{1,2,0:T(8,128)(2,1)S(1)}, bf16[1,1024,384]{1,2,0:T(8,128)(2,1)}, u32[]{:S(2)}) copy-start(bf16[1,1024,384]{1,2,0:T(8,128)(2,1)} %copy-done.6) | copy-start | bytes 2359300
  234.6 419.3 %all-reduce.5.cloned.1.call-start = ((), (), s32[]{:S(2)}) async-start(), calls=%async_computation.12 | async-start | bytes 28311552 | tf_op jit(solution)/shard_map/psum | solution.py:214
  235.9 6.5 copy-start.30
  235.9 6.5 copy-start.35
  242.5 4.4 copy-start.31
  242.5 4.4 copy-start.34
  246.9 1.8 copy-start.18
  246.9 1.8 copy-start.20
  246.9 2.2 copy-start.29
  254.4 2.1 copy-start.9
  254.4 2.1 copy-start.10
  256.5 61.2 %copy-start.23 = (f32[8]{0:T(128)S(1)}, f32[8]{0:T(128)}, u32[]{:S(2)}) copy-start(f32[8]{0:T(128)} %param.10) | copy-start | bytes 100
  653.8 5.3 copy-start.16
  659.1 6.5 slice-start
  660.1 5.5 slice-start.1
  665.6 3.4 copy-start.1
  (15 other events, 18.1 us)
Sparse Core Ops, SparseCore 0:
  21.1 12.4 all-gather.4
  73.5 10.2 reduce-scatter.4
  88.2 10.9 all-gather.6
  100.7 10.9 all-gather.8
  123.9 10.2 reduce-scatter.8
  136.8 10.2 reduce-scatter.6
  151.1 10.9 all-gather.10
  234.7 10.2 reduce-scatter.10
  253.1 400.6 all-reduce.4
where the time goes:
time: 685 us; the launch traced here: 676 us
  waiting for transfers between devices  394 us (58%)
  matrix products  116 us (17%)
  other arithmetic  67.1 us (10%)
  blocking collectives  49.5 us (7%)
  local copies, waits for them, and re-layouts  33.6 us (5%)
  between operations  14.5 us (2%)
    psum x1, waiting for transfers between devices, shards(): lax.psum((grad_qkv, grad_out_proj, grad_up, grad_down, grad_gain_attn, gr...  330 us
    psum x1, blocking collectives, shards(): lax.psum((grad_qkv, grad_out_proj, grad_up, grad_down, grad_gain_attn, gr...  47 us
    unnamed x80, local copies, waits for them, and re-layouts  25.7 us
    convert_element_type x1, other arithmetic, attend_back(): grad_scores = (attn_probs * (grad_probs - row_dot)).astype(jnp.bfloat16)  21.4 us
    dot_general x1, matrix products, attend_back(): jnp.einsum('qhe,khe->hqk', grad_att, value_rows, preferred_element_type=j...  15.5 us
  transfers between devices with their start and end apart: 9, of which 8 were waited for; matrix products, arithmetic and copies ran while one was open for 8% of the time, Pallas kernels for 0%

commit v1 on v0

--- a/solution.py
+++ b/solution.py
@@ -91,6 +91,26 @@
         grad_keys.astype(jnp.bfloat16),
         grad_values.astype(jnp.bfloat16),
     )
+
+
+def mp_swap(rows):
+    return lax.ppermute(rows, "mp", [(0, 1), (1, 0)])
+
+
+def mp_gather(rows):
+    other = mp_swap(rows)
+    at_zero = lax.axis_index("mp") == 0
+    return jnp.concatenate(
+        [jnp.where(at_zero, rows, other), jnp.where(at_zero, other, rows)], axis=0
+    )
+
+
+def mp_scatter_sum(rows):
+    half = rows.shape[0] // 2
+    at = lax.axis_index("mp")
+    mine = lax.dynamic_slice_in_dim(rows, at * half, half, 0)
+    sent = lax.dynamic_slice_in_dim(rows, (1 - at) * half, half, 0).astype(jnp.bfloat16)
+    return mine + mp_swap(sent).astype(jnp.float32)
 
 
 def shards(
@@ -110,7 +130,7 @@
             jnp.float32
         )
     first_out, first_normed, first_inv = layer_norm(mixed_rows, gain_attn)
-    first_rows = lax.all_gather(first_out.astype(jnp.bfloat16), "mp", axis=0, tiled=True)
+    first_rows = mp_gather(first_out.astype(jnp.bfloat16))
     all_rows = first_rows.shape[0]
     local_width = qkv_weight.shape[2]
     head_local = local_width // HEAD_DIM
@@ -125,34 +145,20 @@
     def out_term():
         return jnp.dot(attended, out_weight, preferred_element_type=jnp.float32)
 
-    branch = lax.psum_scatter(
-        out_term().astype(jnp.bfloat16), "mp", scatter_dimension=0, tiled=True
-    ).astype(jnp.float32)
+    branch = mp_scatter_sum(out_term())
     middle = mixed_rows + branch
     second_out, second_normed, second_inv = layer_norm(middle, gain_mlp)
-    second_rows = lax.all_gather(second_out.astype(jnp.bfloat16), "mp", axis=0, tiled=True)
+    second_rows = mp_gather(second_out.astype(jnp.bfloat16))
     pre_act = jnp.dot(second_rows, up_weight, preferred_element_type=jnp.float32)
     hidden = gelu_value(pre_act).astype(jnp.bfloat16)
     hidden_part = hidden
     block_out = (
         middle
-        + lax.psum_scatter(
-            jnp.dot(hidden_part, down_weight, preferred_element_type=jnp.float32).astype(
-                jnp.bfloat16
-            ),
-            "mp",
-            scatter_dimension=0,
-            tiled=True,
-        ).astype(jnp.float32)
+        + mp_scatter_sum(jnp.dot(hidden_part, down_weight, preferred_element_type=jnp.float32))
     ).astype(jnp.bfloat16)
-    branch_again = lax.psum_scatter(
-        out_term().astype(jnp.bfloat16), "mp", scatter_dimension=0, tiled=True
-    ).astype(jnp.float32)
-    second_back, second_normed, second_inv = layer_norm(mixed_rows + branch_again, gain_mlp)
-    second_rows = lax.all_gather(second_back.astype(jnp.bfloat16), "mp", axis=0, tiled=True)
     contract_rows = (((0,), (0,)), ((), ()))
     contract_cols = (((1,), (1,)), ((), ()))
-    block_rows = lax.all_gather(cotangent, "mp", axis=0, tiled=True)
+    block_rows = mp_gather(cotangent)
     hidden_part = hidden
     grad_down_w = lax.dot_general(
         hidden_part, block_rows, contract_rows, preferred_element_type=jnp.float32
@@ -166,17 +172,12 @@
     grad_up = lax.dot_general(
         second_rows, grad_pre, contract_rows, preferred_element_type=jnp.float32
     )
-    grad_second = lax.psum_scatter(
-        lax.dot_general(
-            grad_pre, up_weight, contract_cols, preferred_element_type=jnp.float32
-        ).astype(jnp.bfloat16),
-        "mp",
-        scatter_dimension=0,
-        tiled=True,
-    ).astype(jnp.float32)
+    grad_second = mp_scatter_sum(
+        lax.dot_general(grad_pre, up_weight, contract_cols, preferred_element_type=jnp.float32)
+    )
     middle_part, grad_gain_mlp = norm_back(grad_second, gain_mlp, second_normed, second_inv)
     grad_middle = cotangent.astype(jnp.float32) + middle_part
-    block_rows = lax.all_gather(grad_middle.astype(jnp.bfloat16), "mp", axis=0, tiled=True)
+    block_rows = mp_gather(grad_middle.astype(jnp.bfloat16))
     grad_out_w = lax.dot_general(
         attended, block_rows, contract_rows, preferred_element_type=jnp.float32
     )
@@ -191,14 +192,9 @@
     grad_qkv = jnp.einsum(
         "td,cte->cde", first_rows, grad_rows_qkv, preferred_element_type=jnp.float32
     )
-    grad_first = lax.psum_scatter(
-        jnp.einsum(
-            "cte,cde->td", grad_rows_qkv, qkv_weight, preferred_element_type=jnp.float32
-        ).astype(jnp.bfloat16),
-        "mp",
-        scatter_dimension=0,
-        tiled=True,
-    ).astype(jnp.float32)
+    grad_first = mp_scatter_sum(
+        jnp.einsum("cte,cde->td", grad_rows_qkv, qkv_weight, preferred_element_type=jnp.float32)
+    )
     mixed_part, grad_gain_attn = norm_back(grad_first, gain_attn, first_normed, first_inv)
     grad_mixed = grad_middle + mixed_part
     grad_history = (depth_weights[:, None, None] * grad_mixed[None]).astype(jnp.bfloat16)
@@ -208,22 +204,16 @@
     ]
     grad_depth = jnp.stack(depth_terms)
     grad_gain_attn, grad_gain_mlp, grad_depth = lax.psum(
-        (grad_gain_attn, grad_gain_mlp, grad_depth), "mp"
-    )
-    grad_qkv, grad_out_proj, grad_up, grad_down, grad_gain_attn, grad_gain_mlp, grad_depth = (
-        lax.psum(
-            (
-                grad_qkv,
-                grad_out_proj,
-                grad_up,
-                grad_down,
-                grad_gain_attn,
-                grad_gain_mlp,
-                grad_depth,
-            ),
-            "dp",
-        )
-    )
+        (grad_gain_attn, grad_gain_mlp, grad_depth), ("dp", "mp")
+    )
+
+    def dp_sum(grad):
+        return lax.psum(grad.astype(jnp.bfloat16), "dp").astype(jnp.float32)
+
+    grad_down = dp_sum(grad_down)
+    grad_up = dp_sum(grad_up)
+    grad_out_proj = dp_sum(grad_out_proj)
+    grad_qkv = dp_sum(grad_qkv)
     return (
         block_out,
         grad_history,

time: 685 us -> 428 us (0.62)
  waiting for transfers between devices: 394 us -> 173 us
  matrix products: 116 us -> 97.3 us
  local copies, waits for them, and re-layouts: 33.6 us -> 16.8 us
  other arithmetic: 67.1 us -> 74.3 us
    psum x1, waiting for transfers between devices: 330 us -> 163 us  [dp_sum(): return lax.psum(grad.astype(jnp.bfloat16), 'dp').astype(jnp.float32)]
    all_gather x4 -> x0, waiting for transfers between devices: 38 us -> none  [the longest x1 11.3 us: shards(): lax.all_gather(first_out.astype(jnp.bfloat16), 'mp', axis=0, tiled=True)]
    reduce_scatter x4 -> x0, waiting for transfers between devices: 25.3 us -> none  [the longest x1 11 us: shards(): lax.psum_scatter(jnp.dot(hidden_part, down_weight, preferred_element_type...]
    unnamed x80 -> x65, local copies, waits for them, and re-layouts: 25.7 us -> 7.76 us
    ppermute x0 -> x8, waiting for transfers between devices: none -> 10.1 us  [mp_swap(): return lax.ppermute(rows, 'mp', [(0, 1), (1, 0)])]
    psum x2 -> x1, blocking collectives: 49.5 us -> 44 us  [shards(): lax.psum((grad_gain_attn, grad_gain_mlp, grad_depth), ('dp', 'mp'))]
  transfers between devices with their start and end apart: 9 -> 9, of which waited for: 8 -> 6; matrix products, arithmetic and copies ran while one was open for 8% -> 11% of each run, Pallas kernels for 0% -> 0%
where the time goes in v1:
time: 428 us; the launch traced here: 423 us
  waiting for transfers between devices  173 us (40%)
  matrix products  97.3 us (23%)
  other arithmetic  74.3 us (17%)
  blocking collectives  44 us (10%)
  local copies, waits for them, and re-layouts  16.8 us (4%)
  between operations  14.8 us (3%)
    psum x1, waiting for transfers between devices, dp_sum(): return lax.psum(grad.astype(jnp.bfloat16), 'dp').astype(jnp.float32)  163 us
    psum x1, blocking collectives, shards(): lax.psum((grad_gain_attn, grad_gain_mlp, grad_depth), ('dp', 'mp'))  44 us
    convert_element_type x1, other arithmetic, attend_back(): grad_scores = (attn_probs * (grad_probs - row_dot)).astype(jnp.bfloat16)  21.6 us
    dot_general x1, matrix products, attend_back(): jnp.einsum('qhe,khe->hqk', grad_att, value_rows, preferred_element_type=j...  15.5 us
    reduce_sum x2, other arithmetic, layer_norm(): row_mean = jnp.mean(inputs, axis=-1, keepdims=True)  11.7 us
    dot_general x1, matrix products, masked_scores(): jnp.einsum('qhe,khe->hqk', queries, key_rows, preferred_element_type=jnp....  10.7 us
    dot_general x1, matrix products, attend_block(): jnp.einsum('hqk,khe->qhe', attn_probs, value_rows, preferred_element_type...  10.5 us
    dot_general x1, matrix products, attend_back(): jnp.einsum('hqk,qhe->khe', attn_probs.astype(jnp.bfloat16), grad_att, pre...  10.4 us
  transfers between devices with their start and end apart: 9, of which 6 were waited for; matrix products, arithmetic and copies ran while one was open for 11% of the time, Pallas kernels for 0%

profile of v1, /device:TPU:0, one launch (start us, length us, event | category | flops | bytes accessed | tf_op | source)
XLA Modules:
  0.0 422.5 jit_solution(4503957997086827757)
XLA Ops:
  9.3 9.3 %fusion.43 = (f32[512]{0:T(512)S(1)}, f32[512,768]{1,0:T(8,128)S(1)}) fusion(bf16[8,512,768]{2,1,0:T(8,128)(2,1)} %param.9, f32[]{:T(128)} %bitcast.14, f32[]{:T(128)} %bitcast.12, f32[]{:T(128)} %bitcast.10, f32[]{:T(128)} %bitcast.8, f32[]{:T(128)} %bitcast.6, f32[]{:T(128)} %bitcast.4, f32[]{:T(128)} %bitcast.2, f32[]{:T(128)} %bitcast), kind=kLoop, calls=%fused_computation.120 | loop fusion | flops 9436672 | bytes 7866400 | tf_op jit(solution)/shard_map/reduce_sum | solution.py:16
  20.9 2.2 collective-permute-done
  23.1 3.5 broadcast_select_fusion.3
  28.9 10.7 %fusion.47 = (f32[6,1024]{1,0:T(8,128)S(1)}, f32[6,1024,1024]{1,2,0:T(8,128)}) fusion(bf16[1024,6,64]{0,2,1:T(8,128)(2,1)S(1)} %bitcast.110, bf16[1024,6,64]{0,2,1:T(8,128)(2,1)S(1)} %bitcast.108, pred[1024,1024]{0,1:T(8,128)(4,1)S(1)} %iota_compare_fusion), kind=kOutput, calls=%fused_computation.123 | convolution fusion | flops 824174592 | bytes 27811840 | tf_op jit(solution)/shard_map/while/body/eval_jaxpr/qhe,khe->hqk/dot_general | solution.py:45
  39.6 10.2 %fusion = f32[6,1024]{1,0:T(8,128)S(1)} fusion(f32[6,1024,1024]{1,2,0:T(8,128)} %get-tuple-element.112, f32[6,1024]{1,0:T(8,128)S(1)} %get-tuple-element.111), kind=kLoop, calls=%fused_computation.6 | loop fusion | flops 12576768 | bytes 25214976 | tf_op jit(solution)/shard_map/while/body/eval_jaxpr/reduce_sum | solution.py:58
  49.8 10.5 %fusion.30 = bf16[6,64,1024]{2,1,0:T(8,128)(2,1)S(1)} fusion(bf16[1024,6,64]{0,2,1:T(8,128)(2,1)S(1)} %bitcast.117, f32[6,1024,1024]{1,2,0:T(8,128)} %get-tuple-element.112, f32[6,1024]{1,0:T(8,128)S(1)} %fusion, f32[6,1024]{1,0:T(8,128)S(1)} %get-tuple-element.111), kind=kOutput, calls=%fused_computation.87 | convolution fusion | flops 824573952 | bytes 26787840 | tf_op jit(solution)/shard_map/while/body/eval_jaxpr/hqk,khe->qhe/dot_general | solution.py:60
  64.2 2.5 collective-permute-done.1
  66.7 2.4 fusion.42
  70.3 2.1 collective-permute-done.2
  72.9 2.8 multiply_convert_fusion.2
  75.7 5.0 %fusion.11 = bf16[1024,1536]{1,0:T(8,128)(2,1)S(1)} fusion(f32[1024,1536]{1,0:T(8,128)S(1)} %get-tuple-element.114, bf16[1536,768]{1,0:T(8,128)(2,1)S(1)} %copy-done.30, bf16[512,768]{1,0:T(8,128)(2,1)S(1)} %copy-done.17, bf16[512,768]{1,0:T(8,128)(2,1)S(1)} %copy-done.16), kind=kOutput, calls=%fused_computation.18 | convolution fusion | flops 2434793472 | bytes 13369344 | tf_op jit(solution)/shard_map/dot_general | solution.py:166
  80.7 2.6 fusion.50
  83.7 2.6 fusion.49
  88.7 2.2 fusion.41
  91.3 4.0 convolution_convert_fusion
  95.2 3.9 convolution_convert_fusion.1
  102.7 10.4 %fusion.27 = bf16[6,64,1024]{2,1,0:T(8,128)(2,1)S(1)} fusion(bf16[1024,6,64]{0,2,1:T(8,128)(2,1)S(1)} %bitcast.113, f32[6,1024,1024]{1,2,0:T(8,128)} %get-tuple-element.112, f32[6,1024]{1,0:T(8,128)S(1)} %log_add_fusion), kind=kOutput, calls=%fused_computation.86 | convolution fusion | flops 818282496 | bytes 26763264 | tf_op jit(solution)/shard_map/while/body/eval_jaxpr/hqk,qhe->khe/dot_general | solution.py:70
  113.1 15.5 %multiply_reduce_fusion = (f32[6,1024]{1,0:T(8,128)S(1)}, f32[6,1024,1024]{1,2,0:T(8,128)}) fusion(f32[6,1024,1024]{1,2,0:T(8,128)} %get-tuple-element.112, f32[6,1024]{1,0:T(8,128)S(1)} %log_add_fusion, bf16[1024,6,64]{0,2,1:T(8,128)(2,1)S(1)} %bitcast.114, bf16[1024,6,64]{0,2,1:T(8,128)(2,1)S(1)} %bitcast.118), kind=kOutput, calls=%fused_computation.1 | convolution fusion | flops 824174592 | bytes 51953664 | tf_op jit(solution)/shard_map/while/body/eval_jaxpr/qhe,khe->hqk/dot_general | solution.py:76
  128.6 21.6 %multiply_convert_fusion = bf16[6,1024,1024]{1,2,0:T(8,128)(2,1)} fusion(f32[6,1024,1024]{1,2,0:T(8,128)} %get-tuple-element.116, f32[6,1024,1024]{1,2,0:T(8,128)} %get-tuple-element.112, f32[6,1024]{1,0:T(8,128)S(1)} %get-tuple-element.115, f32[6,1024]{1,0:T(8,128)S(1)} %log_add_fusion), kind=kLoop, calls=%fused_computation | loop fusion | flops 25165824 | bytes 62963712 | tf_op jit(solution)/shard_map/while/body/eval_jaxpr/convert_element_type | solution.py:80
  150.2 8.5 %multiply_convert_fusion.3 = bf16[6,64,1024]{2,1,0:T(8,128)(2,1)S(1)} fusion(bf16[1024,6,64]{0,2,1:T(8,128)(2,1)S(1)} %bitcast.111, bf16[6,1024,1024]{1,2,0:T(8,128)(2,1)} %multiply_convert_fusion), kind=kOutput, calls=%fused_computation.69 | convolution fusion | flops 806092800 | bytes 14155776 | tf_op jit(solution)/shard_map/while/body/eval_jaxpr/hqk,qhe->khe/dot_general | solution.py:86
  158.7 6.9 %multiply_convert_fusion.4 = bf16[6,64,1024]{2,1,0:T(8,128)(2,1)S(1)} fusion(bf16[1024,6,64]{0,2,1:T(8,128)(2,1)S(1)} %bitcast.109, bf16[6,1024,1024]{1,2,0:T(8,128)(2,1)} %multiply_convert_fusion), kind=kOutput, calls=%fused_computation.70 | convolution fusion | flops 806092800 | bytes 14155776 | tf_op jit(solution)/shard_map/while/body/eval_jaxpr/hqk,khe->qhe/dot_general | solution.py:82
  166.7 4.7 %convert_bitcast_fusion.1 = bf16[3,768,384]{1,2,0:T(8,128)(2,1)} fusion(bf16[512,768]{1,0:T(8,128)(2,1)} %copy-done.14, bf16[512,768]{1,0:T(8,128)(2,1)} %copy-done.15, bf16[1,1024,384]{2,1,0:T(8,128)(2,1)S(1)} %copy.25, bf16[1,1024,384]{2,1,0:T(8,128)(2,1)S(1)} %copy.24, bf16[1,1024,384]{2,1,0:T(8,128)(2,1)S(1)} %copy.23), kind=kOutput, calls=%fused_computation.43 | convolution fusion | flops 1818329088 | bytes 5701632 | tf_op jit(solution)/shard_map/td,cte->cde/dot_general | solution.py:192
  171.4 3.7 convolution_bitcast_fusion
  178.4 7.2 %fusion.26 = (f32[]{:T(128)}, f32[]{:T(128)}, f32[]{:T(128)}, f32[]{:T(128)}, f32[]{:T(128)}, /*index=5*/f32[]{:T(128)}, f32[]{:T(128)}, f32[]{:T(128)}, f32[512,768]{1,0:T(8,128)}) fusion(bf16[8,512,768]{2,1,0:T(8,128)(2,1)} %param.9, f32[512,768]{1,0:T(8,128)S(1)} %copy-done.7, f32[512]{0:T(512)S(1)} %broadcast_multiply_fusion, ...), kind=kLoop, calls=%fused_computation.58 | loop fusion | flops 13369336 | bytes 13380644 | tf_op jit(solution)/shard_map/reduce_sum | solution.py:202
  185.7 5.0 %stack.51 = f32[8]{0:T(128)S(1)} concatenate(f32[1]{0:T(128)} %bitcast.34, f32[1]{0:T(128)} %bitcast.36, f32[1]{0:T(128)} %bitcast.38, f32[1]{0:T(128)} %bitcast.40, f32[1]{0:T(128)} %bitcast.42, f32[1]{0:T(128)} %bitcast.44, f32[1]{0:T(128)} %bitcast.46, f32[1]{0:T(128)} %bitcast.48), dimensions={0} | concatenate | bytes 64 | tf_op jit(solution)/shard_map/stack | solution.py:205
  190.7 44.0 %all-reduce = (f32[8]{0:T(128)}, f32[768]{0:T(1024)}, f32[768]{0:T(1024)}) all-reduce(f32[8]{0:T(128)S(1)} %stack.51, f32[768]{0:T(1024)S(1)} %get-tuple-element.73, f32[768]{0:T(1024)S(1)} %get-tuple-element.71), channel_id=1, replica_groups=mesh['dp'=16,'mp'=2] {'dp','mp'}, use_global_device_ids=true, to_apply=%region_19.20 | all-reduce | flops 1544 | bytes 12352 | tf_op jit(solution)/shard_map/psum | solution.py:206
  234.7 6.0 %multiply_convert_fusion.1 = bf16[8,512,768]{2,1,0:T(8,128)(2,1)} fusion(f32[512,768]{1,0:T(8,128)} %get-tuple-element.84, f32[8]{0:T(128)S(1)} %copy-done.29), kind=kLoop, calls=%fused_computation.9 | loop fusion | flops 6291456 | bytes 7864352 | tf_op jit(solution)/shard_map/convert_element_type | solution.py:200
  240.6 163.1 %all-reduce.4.cloned.1.call-done = (bf16[3,768,384]{1,2,0:T(8,128)(2,1)}, bf16[384,768]{1,0:T(8,128)(2,1)}, bf16[768,1536]{1,0:T(8,128)(2,1)}, bf16[1536,768]{1,0:T(8,128)(2,1)}) async-done(((bf16[3,768,384]{1,2,0:T(8,128)(2,1)}, bf16[384,768]{1,0:T(8,128)(2,1)}, bf16[768,1536]{1,0:T(8,128)(2,1)}, bf16[1536,768]{1,0:T(8,128)(2,1)}), (bf16[3,768,384]{1,2,0:T(8,128)(2,1)}, bf16[384,768]{1,0:T(8,128)(2,1)}, ...) | async-done | bytes 7077904 | tf_op jit(solution)/shard_map/psum | solution.py:211
  403.8 2.2 convert_element_type.230
  405.9 4.2 copy.29
  410.1 2.8 convert_element_type.232
  412.9 2.5 convert_element_type.234
  (110 shorter events, 23.0 us)
Async XLA Ops:
  7.2 65.7 %copy-start = (bf16[768,1536]{1,0:T(8,128)(2,1)S(1)}, bf16[768,1536]{1,0:T(8,128)(2,1)}, u32[]{:S(2)}) copy-start(bf16[768,1536]{1,0:T(8,128)(2,1)} %param.15) | copy-start | bytes 7077892
  7.2 396.6 %all-reduce.4.cloned.1.call-start = ((), (), s32[]{:S(2)}) async-start(), calls=%async_computation | async-start | bytes 14155776 | tf_op jit(solution)/shard_map/psum | solution.py:211
  7.2 13.6 %collective-permute-start.4 = (bf16[512,768]{1,0:T(8,128)(2,1)}, bf16[512,768]{1,0:T(8,128)(2,1)}, u32[]{:S(2)}, u32[]{:S(2)}) collective-permute-start(bf16[512,768]{1,0:T(8,128)(2,1)} %param.17), channel_id=1, source_target_pairs={{0,1},{1,0},{2,3},{3,2},{4,5},{5,4},{6,7},{7,6},{8,9},{9,8},{10,11... | collective-permute-start | bytes 2359304 | tf_op jit(solution)/shard_map/ppermute | solution.py:97
  18.6 4.5 %copy-start.22 = (f32[512]{0:T(512)}, f32[512]{0:T(512)S(1)}, u32[]{:S(2)}) copy-start(f32[512]{0:T(512)S(1)} %broadcast_multiply_fusion.5) | copy-start | bytes 6148
  19.3 3.8 copy-start.27
  19.3 3.8 copy-start.10
  20.5 2.6 collective-permute-start
  20.8 5.7 %copy-start.31 = (bf16[3,768,384]{2,1,0:T(8,128)(2,1)S(1)}, bf16[3,768,384]{2,1,0:T(8,128)(2,1)}, u32[]{:S(2)}) copy-start(bf16[3,768,384]{2,1,0:T(8,128)(2,1)} %param.13) | copy-start | bytes 5308420
  26.6 2.1 copy-start.15
  28.9 10.7 %copy-start.4 = (bf16[1,1024,384]{1,2,0:T(8,128)(2,1)}, bf16[1,1024,384]{1,2,0:T(8,128)(2,1)S(1)}, u32[]{:S(2)}) copy-start(bf16[1,1024,384]{1,2,0:T(8,128)(2,1)S(1)} %get-tuple-element.92) | copy-start | bytes 2359300
  28.9 20.9 %copy-start.8 = (bf16[1,1024,384]{1,2,0:T(8,128)(2,1)}, bf16[1,1024,384]{1,2,0:T(8,128)(2,1)S(1)}, u32[]{:S(2)}) copy-start(bf16[1,1024,384]{1,2,0:T(8,128)(2,1)S(1)} %get-tuple-element.93) | copy-start | bytes 2359300
  49.8 10.6 %copy-start.20 = (bf16[384,768]{1,0:T(8,128)(2,1)S(1)}, bf16[384,768]{1,0:T(8,128)(2,1)}, u32[]{:S(2)}) copy-start(bf16[384,768]{1,0:T(8,128)(2,1)} %param.14) | copy-start | bytes 1769476
  64.1 2.6 collective-permute-start.1
  70.1 2.4 collective-permute-start.2
  72.9 2.8 copy-start.16
  72.9 2.8 copy-start.17
  72.9 2.8 copy-start.30
  83.5 3.4 collective-permute-start.5
  86.4 2.4 collective-permute-start.3
  90.9 8.2 %collective-permute-start.6 = (bf16[512,768]{1,0:T(8,128)(2,1)S(1)}, bf16[512,768]{1,0:T(8,128)(2,1)S(1)}, u32[]{:S(2)}, u32[]{:S(2)}) collective-permute-start(bf16[512,768]{1,0:T(8,128)(2,1)S(1)} %get-tuple-element.85), channel_id=1, source_target_pairs={{0,1},{1,0},{2,3},{3,2},{4,5},{5,4},{6,7},{7,6},{8,9},{9,8},{10,11... | collective-permute-start | bytes 2359304 | tf_op jit(solution)/shard_map/ppermute | solution.py:97
  102.7 10.4 %copy-start.9 = (bf16[1,1024,384]{1,2,0:T(8,128)(2,1)S(1)}, bf16[1,1024,384]{1,2,0:T(8,128)(2,1)}, u32[]{:S(2)}) copy-start(bf16[1,1024,384]{1,2,0:T(8,128)(2,1)} %copy-done.8) | copy-start | bytes 2359300
  128.6 21.6 %copy-start.5 = (bf16[1,1024,384]{1,2,0:T(8,128)(2,1)S(1)}, bf16[1,1024,384]{1,2,0:T(8,128)(2,1)}, u32[]{:S(2)}) copy-start(bf16[1,1024,384]{1,2,0:T(8,128)(2,1)} %copy-done.4) | copy-start | bytes 2359300
  171.4 6.2 %copy-start.23 = (f32[512]{0:T(512)S(1)}, f32[512]{0:T(512)}, u32[]{:S(2)}) copy-start(f32[512]{0:T(512)} %copy-done.22) | copy-start | bytes 6148
  171.4 6.2 %copy-start.25 = (f32[768]{0:T(1024)S(1)}, f32[768]{0:T(1024)}, u32[]{:S(2)}) copy-start(f32[768]{0:T(1024)} %param.11) | copy-start | bytes 9220
  171.4 6.2 %copy-start.28 = (f32[512]{0:T(512)S(1)}, f32[512]{0:T(512)}, u32[]{:S(2)}) copy-start(f32[512]{0:T(512)} %copy-done.27) | copy-start | bytes 6148
  175.1 2.5 copy-start.3
  175.2 3.2 copy-start.7
  175.2 2.4 collective-permute-start.7
  178.4 56.2 %copy-start.29 = (f32[8]{0:T(128)S(1)}, f32[8]{0:T(128)}, u32[]{:S(2)}) copy-start(f32[8]{0:T(128)} %param.10) | copy-start | bytes 100
  405.9 4.2 copy-start.13
  410.1 2.8 copy-start.12
  412.9 2.5 copy-start.1
  (9 other events, 12.7 us)
Sparse Core Ops, SparseCore 0:
  171.5 232.2 all-reduce.3

commit v2 on v1

v2 whole, which is shorter than its diff:
```python
import functools

import jax
import jax.numpy as jnp
from jax import lax
from jax.experimental import pallas as pl
from jax.experimental.pallas import tpu as pltpu
from jax.sharding import PartitionSpec as P

HEAD_DIM = 64
EPSILON = 1e-05
SQRT_HALF = 0.7071067811865476
INV_ROOT_TWO_PI = 0.3989422804014327
LOG2E = 1.4426950408889634
NEG = -1e30
TILE = 256
ROW_BLOCK = 128
VMEM_BYTES = 32 * 2**20
SPLITS = 4
PAIR = 2 * HEAD_DIM
CHUNK = 512

PLAIN = (((1,), (0,)), ((), ()))
CONTRACT_COLS = (((1,), (1,)), ((), ()))
CONTRACT_ROWS = (((0,), (0,)), ((), ()))


def dot(lhs, rhs, dims=PLAIN):
    return lax.dot_general(lhs, rhs, dims, preferred_element_type=jnp.float32)


def cost(flops, moved, exps=0):
    return pl.CostEstimate(flops=flops, bytes_accessed=moved, transcendentals=exps)


def params():
    return pltpu.CompilerParams(vmem_limit_bytes=VMEM_BYTES)


def normalize(inputs):
    row_mean = jnp.mean(inputs, axis=-1, keepdims=True)
    centered = inputs - row_mean
    variance = jnp.mean(centered * centered, axis=-1, keepdims=True)
    inv_scale = lax.rsqrt(variance + EPSILON)
    return centered * inv_scale, inv_scale


def norm_back(grad_rows, gain_row, normed, inv_scale):
    scaled = grad_rows * gain_row
    first_mean = jnp.mean(scaled, axis=-1, keepdims=True)
    second_mean = jnp.mean(scaled * normed, axis=-1, keepdims=True)
    return inv_scale * (scaled - first_mean - normed * second_mean)


def gelu_value(inputs):
    return 0.5 * inputs * (1.0 + lax.erf(inputs * SQRT_HALF))


def gelu_slope(inputs):
    normal_cdf = 0.5 * (1.0 + lax.erf(inputs * SQRT_HALF))
    return normal_cdf + inputs * jnp.exp(-0.5 * inputs * inputs) * INV_ROOT_TWO_PI


def mix_kernel(weights_ref, history_ref, gain_ref, mixed_ref, first_ref):
    mixed = weights_ref[0] * history_ref[0].astype(jnp.float32)
    for layer in range(1, history_ref.shape[0]):
        mixed = mixed + weights_ref[layer] * history_ref[layer].astype(jnp.float32)
    mixed_ref[...] = mixed
    normed, _ = normalize(mixed)
    first_ref[...] = (normed * gain_ref[...]).astype(jnp.bfloat16)


def mix(weights, history, gain):
    layers, rows, width = history.shape
    return pl.pallas_call(
        mix_kernel,
        grid=(rows // ROW_BLOCK,),
        in_specs=[
            pl.BlockSpec(memory_space=pltpu.SMEM),
            pl.BlockSpec((layers, ROW_BLOCK, width), lambda i: (0, i, 0)),
            pl.BlockSpec((1, width), lambda i: (0, 0)),
        ],
        out_specs=[
            pl.BlockSpec((ROW_BLOCK, width), lambda i: (i, 0)),
            pl.BlockSpec((ROW_BLOCK, width), lambda i: (i, 0)),
        ],
        out_shape=[
            jax.ShapeDtypeStruct((rows, width), jnp.float32),
            jax.ShapeDtypeStruct((rows, width), jnp.bfloat16),
        ],
        compiler_params=params(),
        cost_estimate=cost(30 * rows * width, 22 * rows * width),
        name="mix",
    )(weights, history, gain[None])


def unmix_kernel(
    weights_ref, history_ref, gain_ref, mixed_ref, middle_ref, own_ref, other_ref, *refs
):
    grads_ref, gain_grad_ref, depth_ref = refs[-3:]
    grad_first = own_ref[...] + other_ref[...].astype(jnp.float32)
    normed, inv_scale = normalize(mixed_ref[...])
    grad_mixed = middle_ref[...] + norm_back(grad_first, gain_ref[...], normed, inv_scale)
    gain_term = jnp.sum(grad_first * normed, axis=0, keepdims=True)
    step = pl.program_id(0)

    @pl.when(step == 0)
    def _():
        gain_grad_ref[...] = jnp.zeros_like(gain_grad_ref)
        depth_ref[...] = jnp.zeros_like(depth_ref)

    gain_grad_ref[...] += gain_term
    for layer in range(history_ref.shape[0]):
        grads_ref[layer] = (weights_ref[layer] * grad_mixed).astype(jnp.bfloat16)
        product = history_ref[layer].astype(jnp.float32) * grad_mixed
        depth_ref[layer : layer + 1] += jnp.sum(product, axis=0, keepdims=True)


def unmix(weights, history, gain, mixed, grad_middle, own, other, after=()):
    layers, rows, width = history.shape
    row_spec = pl.BlockSpec((ROW_BLOCK, width), lambda i: (i, 0))
    layer_spec = pl.BlockSpec((layers, ROW_BLOCK, width), lambda i: (0, i, 0))
    return pl.pallas_call(
        unmix_kernel,
        grid=(rows // ROW_BLOCK,),
        in_specs=[
            pl.BlockSpec(memory_space=pltpu.SMEM),
            layer_spec,
            pl.BlockSpec((1, width), lambda i: (0, 0)),
            row_spec,
            row_spec,
            row_spec,
            row_spec,
        ]
        + [pl.BlockSpec(memory_space=pl.ANY)] * len(after),
        out_specs=[
            layer_spec,
            pl.BlockSpec((1, width), lambda i: (0, 0)),
            pl.BlockSpec((layers, width), lambda i: (0, 0)),
        ],
        out_shape=[
            jax.ShapeDtypeStruct(history.shape, jnp.bfloat16),
            jax.ShapeDtypeStruct((1, width), jnp.float32),
            jax.ShapeDtypeStruct((layers, width), jnp.float32),
        ],
        compiler_params=params(),
        cost_estimate=cost(1000, 1000),
        name="unmix",
    )(weights, history, gain[None], mixed, grad_middle, own, other, *after)


def head_mask(head):
    lanes = lax.broadcasted_iota(jnp.int32, (1, PAIR), 1)
    return (lanes // HEAD_DIM) == head


def future_mask():
    keys = lax.broadcasted_iota(jnp.int32, (TILE, TILE), 0)
    asks = lax.broadcasted_iota(jnp.int32, (TILE, TILE), 1)
    return keys > asks


def local_call(kernel, name, at, arrays, outs, after=(), scratch=()):
    in_vmem = pl.BlockSpec(memory_space=pltpu.VMEM)
    return pl.pallas_call(
        kernel,
        in_specs=[pl.BlockSpec(memory_space=pltpu.SMEM)]
        + [in_vmem] * len(arrays)
        + [pl.BlockSpec(memory_space=pl.ANY)] * len(after),
        out_specs=[in_vmem] * len(outs),
        out_shape=[jax.ShapeDtypeStruct(shape, dtype) for shape, dtype in outs],
        scratch_shapes=list(scratch),
        compiler_params=params(),
        cost_estimate=cost(1000, 1000),
        name=name,
    )(at, *arrays, *after)


def attend_kernel(
    at_ref, own_ref, other_ref, weight_ref, out_weight_ref,
    qkv_ref, att_ref, lse_ref, out_own_ref, out_other_ref,
):
    rows = own_ref.shape[0]
    tiles = rows // TILE
    first = at_ref[0]
    scale = HEAD_DIM ** (-0.5) * LOG2E
    places = (first, 1 - first)
    later = future_mask()

    def one_pair(pair, carry):
        lanes = pl.ds(pl.multiple_of(pair * PAIR, PAIR), PAIR)
        weight = jnp.concatenate([weight_ref[c, :, lanes] for c in range(3)], axis=1)
        for side, ref in enumerate((own_ref, other_ref)):
            made = dot(ref[...], weight).astype(jnp.bfloat16)
            for c in range(3):
                qkv_ref[c, side, :, lanes] = made[:, c * PAIR : (c + 1) * PAIR]
        half_keys = [qkv_ref[1, places[half], :, lanes] for half in range(2)]
        half_values = [qkv_ref[2, places[half], :, lanes].T for half in range(2)]
        for half in range(2):
            for tile in range(tiles):
                at_rows = pl.ds(tile * TILE, TILE)
                queries = qkv_ref[0, places[half], at_rows, lanes]
                outs = []
                for head in range(2):
                    asked = jnp.where(head_mask(head), queries, jnp.zeros_like(queries))
                    spans = []
                    if half == 1:
                        spans.append((0, 0, rows))
                    if tile > 0:
                        spans.append((half, 0, tile * TILE))
                    spans.append((half, tile * TILE, TILE))
                    scores = [
                        dot(half_keys[where][start : start + size], asked, CONTRACT_COLS)
                        for where, start, size in spans
                    ]
                    scores[-1] = jnp.where(later, NEG, scores[-1])
                    top = functools.reduce(
                        jnp.maximum, [jnp.max(part, axis=0, keepdims=True) for part in scores]
                    )
                    top = top * scale
                    total = 0.0
                    summed = 0.0
                    mine = slice(head * HEAD_DIM, (head + 1) * HEAD_DIM)
                    for part, (where, start, size) in zip(scores, spans):
                        weights = jnp.exp2(part * scale - top)
                        total = total + jnp.sum(weights, axis=0, keepdims=True)
                        summed = summed + dot(
                            half_values[where][mine, start : start + size],
                            weights.astype(jnp.bfloat16),
                        )
                    outs.append(summed / total)
                    lse_ref[pair, head, half, :, at_rows] = top + jnp.log2(total)
                joined = jnp.concatenate(outs, axis=0).T
                att_ref[places[half], at_rows, lanes] = joined.astype(jnp.bfloat16)
        return carry

    lax.fori_loop(0, att_ref.shape[2] // PAIR, one_pair, 0)
    out_other_ref[...] = dot(att_ref[1], out_weight_ref[...]).astype(jnp.bfloat16)
    out_own_ref[...] = dot(att_ref[0], out_weight_ref[...])


def attend(at, own, other, weight, out_weight):
    rows, width = own.shape
    local = weight.shape[2]
    return local_call(
        attend_kernel,
        "attend",
        at,
        [own, other, weight, out_weight],
        [
            ((3, 2, rows, local), jnp.bfloat16),
            ((2, rows, local), jnp.bfloat16),
            ((local // PAIR, 2, 2, 1, rows), jnp.float32),
            ((rows, width), jnp.float32),
            ((rows, width), jnp.bfloat16),
        ],
    )


def renorm_kernel(at_ref, mixed_ref, own_ref, other_ref, gain_ref, middle_ref, second_ref):
    middle = mixed_ref[...] + own_ref[...] + other_ref[...].astype(jnp.float32)
    middle_ref[...] = middle
    second_ref[...] = (normalize(middle)[0] * gain_ref[...]).astype(jnp.bfloat16)


def renorm(at, mixed, own, other, gain):
    return local_call(
        renorm_kernel,
        "renorm",
        at,
        [mixed, own, other, gain[None]],
        [(mixed.shape, jnp.float32), (mixed.shape, jnp.bfloat16)],
    )


def split_halves(bit, rows, top, bottom, keep_ref, send_ref):
    shape = (keep_ref.shape[0], -1, keep_ref.shape[2])
    top = top.astype(jnp.bfloat16).reshape(shape)
    bottom = bottom.astype(jnp.bfloat16).reshape(shape)
    keep_ref[:, rows, :] = jnp.where(bit == 0, top, bottom)
    send_ref[:, rows, :] = jnp.where(bit == 0, bottom, top)


def mlp_kernel(
    slots, at_ref, second_own_ref, second_other_ref, cot_own_ref, cot_other_ref, up_ref, down_ref,
    keep_a_ref, send_a_ref, keep_b_ref, send_b_ref, hidden_ref, grad_pre_ref,
):
    bf16 = jnp.bfloat16
    chunks = hidden_ref.shape[2] // CHUNK
    sides = ((second_own_ref, cot_own_ref), (second_other_ref, cot_other_ref))
    early = keep_a_ref.shape[1] * keep_a_ref.shape[0] // CHUNK
    unit = CHUNK // keep_a_ref.shape[0]

    def make(chunk):
        lanes = pl.ds(chunk * CHUNK, CHUNK)
        for side, (second_ref, cot_ref) in enumerate(sides):
            pre = dot(second_ref[...], up_ref[:, lanes])
            cdf = 0.5 * (1.0 + lax.erf(pre * SQRT_HALF))
            hidden_ref[side, :, lanes] = (pre * cdf).astype(bf16)
            slope = cdf + pre * jnp.exp(-0.5 * pre * pre) * INV_ROOT_TWO_PI
            grad_hidden = dot(cot_ref[...], down_ref[lanes, :], CONTRACT_COLS)
            grad_pre_ref[side, :, lanes] = (grad_hidden * slope).astype(bf16)

    def give(chunk):
        lanes = pl.ds(chunk * CHUNK, CHUNK)
        grad_up, grad_down = 0.0, 0.0
        for side, (second_ref, cot_ref) in enumerate(sides):
            grad_up = grad_up + dot(grad_pre_ref[side, :, lanes], second_ref[...], CONTRACT_ROWS)
            grad_down = grad_down + dot(hidden_ref[side, :, lanes], cot_ref[...], CONTRACT_ROWS)
        late = chunk >= early
        refs = (keep_b_ref, send_b_ref) if late else (keep_a_ref, send_a_ref)
        rows = pl.ds((chunk - early if late else chunk) * unit, unit)
        split_halves(at_ref[slots[late]], rows, grad_up, grad_down, *refs)

    make(0)
    for chunk in range(1, chunks):
        make(chunk)
        give(chunk - 1)
    give(chunks - 1)


def mlp(at, slots, second_own, second_other, cot_own, cot_other, up, down, after=()):
    rows, width = second_own.shape
    hidden = down.shape[0]
    blocks = 2 ** (SPLITS - 1)
    chunks = hidden // CHUNK
    early = 2 * chunks // 3
    unit = CHUNK // blocks
    pieces = [((blocks, count * unit, width), jnp.bfloat16) for count in (early, chunks - early)]
    return local_call(
        functools.partial(mlp_kernel, slots),
        "mlp",
        at,
        [second_own, second_other, cot_own, cot_other, up, down],
        [pieces[0], pieces[0], pieces[1], pieces[1]] + [((2, rows, hidden), jnp.bfloat16)] * 2,
        after,
    )


def rows_kernel(transposed, at_ref, rows_ref, weight_ref, *refs):
    own_ref, other_ref = refs[-2:]
    dims = CONTRACT_COLS if transposed else PLAIN
    other_ref[...] = dot(rows_ref[1], weight_ref[...], dims).astype(jnp.bfloat16)
    own_ref[...] = dot(rows_ref[0], weight_ref[...], dims)


def rows_times(at, name, rows, weight, transposed, after=()):
    shape = (rows.shape[1], weight.shape[0 if transposed else 1])
    return local_call(
        functools.partial(rows_kernel, transposed), name, at, [rows, weight],
        [(shape, jnp.float32), (shape, jnp.bfloat16)], after,
    )


def norm_back_kernel(at_ref, own_ref, other_ref, middle_ref, cot_ref, gain_ref, *refs):
    grad_ref, narrow_ref, gain_grad_ref = refs[-3:]
    grad_second = own_ref[...] + other_ref[...].astype(jnp.float32)
    normed, inv_scale = normalize(middle_ref[...])
    grad = cot_ref[...].astype(jnp.float32) + norm_back(
        grad_second, gain_ref[...], normed, inv_scale
    )
    grad_ref[...] = grad
    narrow_ref[...] = grad.astype(jnp.bfloat16)
    gain_grad_ref[...] = jnp.sum(grad_second * normed, axis=0, keepdims=True)


def norm_back_rows(at, own, other, middle, cotangent, gain, after=()):
    shape = own.shape
    return local_call(
        norm_back_kernel,
        "norm_back_rows",
        at,
        [own, other, middle, cotangent, gain[None]],
        [(shape, jnp.float32), (shape, jnp.bfloat16), ((1, shape[1]), jnp.float32)],
        after,
    )


def attend_back_kernel(
    slot, start, at_ref, qkv_ref, att_ref, lse_ref, grad_own_ref, grad_other_ref, out_weight_ref,
    first_own_ref, first_other_ref, *refs,
):
    keep_ref, send_ref, grad_rows_ref = refs[-3:]
    rows = grad_own_ref.shape[0]
    tiles = rows // TILE
    first = at_ref[0]
    plain = HEAD_DIM ** (-0.5)
    scale = plain * LOG2E
    places = (first, 1 - first)
    later = future_mask()
    bf16 = jnp.bfloat16
    sides = (grad_own_ref, grad_other_ref)
    firsts = (first_own_ref, first_other_ref)
    masked = [head_mask(head) for head in range(2)]
    unit = 4 * PAIR // (2 * keep_ref.shape[0])
    count = keep_ref.shape[1] // unit
    is_own = [places[half] == 0 for half in range(2)]
    chunks = [(half, tile) for half in range(2) for tile in range(tiles)]

    def only(head, part):
        return jnp.where(masked[head], part, jnp.zeros_like(part))

    def plus(old, term):
        return term if old is None else old + term

    for step in range(count):
        pair = start + step
        lanes = pl.ds(pair * PAIR, PAIR)
        outer = [
            dot(ref[...], out_weight_ref[lanes, :], CONTRACT_COLS).astype(bf16) for ref in sides
        ]
        grads = [jnp.where(is_own[half], outer[0], outer[1]) for half in range(2)]
        queries, keys, values = [
            [qkv_ref[c, places[half], :, lanes] for half in range(2)] for c in range(3)
        ]
        keys_t = [part.T for part in keys]
        deltas = []
        for half in range(2):
            attended = att_ref[places[half], :, lanes].astype(jnp.float32)
            product = (grads[half].astype(jnp.float32) * attended).T
            deltas.append([
                jnp.sum(product[head * HEAD_DIM : (head + 1) * HEAD_DIM], axis=0, keepdims=True)
                for head in range(2)
            ])
        key_grads = [None for _ in chunks]
        value_grads = [None for _ in chunks]
        query_grads = []
        for ask, (ask_half, ask_tile) in enumerate(chunks):
            ask_rows = slice(ask_tile * TILE, (ask_tile + 1) * TILE)
            sums_here = []
            for head in range(2):
                asked = only(head, queries[ask_half][ask_rows])
                grad = only(head, grads[ask_half][ask_rows])
                lse = lse_ref[pair, head, ask_half, :, ask_rows]
                delta = deltas[ask_half][head][:, ask_rows]
                query_grad = None
                for key in range(ask + 1):
                    key_half, key_tile = chunks[key]
                    key_rows = slice(key_tile * TILE, (key_tile + 1) * TILE)
                    scores = dot(keys[key_half][key_rows], asked, CONTRACT_COLS)
                    probs = jnp.exp2(scores * scale - lse)
                    if key == ask:
                        probs = jnp.where(later, 0.0, probs)
                    grad_probs = dot(values[key_half][key_rows], grad, CONTRACT_COLS)
                    grad_scores = (probs * (grad_probs - delta)).astype(bf16)
                    value_grads[key] = plus(value_grads[key], dot(probs.astype(bf16), grad))
                    key_grads[key] = plus(key_grads[key], dot(grad_scores, asked))
                    mine = slice(head * HEAD_DIM, (head + 1) * HEAD_DIM)
                    query_grad = plus(
                        query_grad, dot(keys_t[key_half][mine, key_rows], grad_scores)
                    )
                sums_here.append(query_grad)
            query_grads.append((jnp.concatenate(sums_here, axis=0) * plain).astype(bf16))
        turned = []
        for half in range(2):
            at_half = [i for i, (where, _) in enumerate(chunks) if where == half]
            query_t = jnp.concatenate([query_grads[i] for i in at_half], axis=1)
            key = jnp.concatenate([(key_grads[i] * plain).astype(bf16) for i in at_half], axis=0)
            value = jnp.concatenate([value_grads[i].astype(bf16) for i in at_half], axis=0)
            turned.append([query_t, key.T, value.T, att_ref[places[half], :, lanes].T])
            for c, part in enumerate((query_t.T, key, value)):
                grad_rows_ref[c, places[half], :, step * PAIR : (step + 1) * PAIR] = part
        top, bottom = 0.0, 0.0
        for side in range(2):
            mine = [jnp.where(is_own[side], a, b) for a, b in zip(turned[0], turned[1])]
            rows_here = firsts[side][...]
            top = top + dot(jnp.concatenate(mine[:2], axis=0), rows_here)
            bottom = bottom + jnp.concatenate(
                [dot(mine[2], rows_here), dot(mine[3], sides[side][...])], axis=0
            )
        split_halves(
            at_ref[slot], pl.ds(step * unit, unit), top, bottom, keep_ref, send_ref
        )


def attend_back(at, slot, start, count, qkv, att, lse, grad_own, grad_other, out_weight,
                first_own, first_other, after=()):
    rows, width = grad_own.shape
    blocks = 2 ** (SPLITS - 1)
    unit = 4 * PAIR // (2 * blocks)
    pieces = ((blocks, count * unit, width), jnp.bfloat16)
    return local_call(
        functools.partial(attend_back_kernel, slot, start),
        "attend_back",
        at,
        [qkv, att, lse, grad_own, grad_other, out_weight, first_own, first_other],
        [pieces, pieces, ((3, 2, rows, count * PAIR), jnp.bfloat16)],
        after,
    )


def first_back_kernel(at_ref, weight_ref, *refs):
    own_ref, other_ref = refs[-2:]
    groups = []
    start = 0
    for ref in refs[:-2]:
        if len(ref.shape) != 4:
            break
        groups.append((ref, start))
        start += ref.shape[3]
    for side, out_ref in ((1, other_ref), (0, own_ref)):
        total = 0.0
        for ref, begin in groups:
            for c in range(3):
                lanes = slice(begin, begin + ref.shape[3])
                total = total + dot(ref[c, side], weight_ref[c, :, lanes], CONTRACT_COLS)
        out_ref[...] = total.astype(out_ref.dtype)


def first_back(at, weight, groups, after=()):
    shape = (groups[0].shape[2], weight.shape[1])
    return local_call(
        first_back_kernel, "first_back", at, [weight, *groups],
        [(shape, jnp.float32), (shape, jnp.bfloat16)], after,
    )


def fold_kernel(slot, at_ref, kept_ref, came_ref, *refs):
    keep_ref, send_ref = refs[-2:]
    half = keep_ref.shape[0]
    bit = at_ref[slot]
    for target, start in ((send_ref, (1 - bit) * half), (keep_ref, bit * half)):
        for index in range(half):
            total = kept_ref[start + index].astype(jnp.float32) + came_ref[
                start + index
            ].astype(jnp.float32)
            target[index] = total.astype(jnp.bfloat16)


def add_kernel(at_ref, kept_ref, came_ref, *refs):
    total = kept_ref[...].astype(jnp.float32) + came_ref[...].astype(jnp.float32)
    refs[-1][...] = total.astype(jnp.bfloat16)


def join_kernel(slot, at_ref, mine_ref, came_ref, *refs):
    both_ref = refs[-1]
    half = mine_ref.shape[0]
    bit = at_ref[slot]
    for source, start in ((mine_ref, bit * half), (came_ref, (1 - bit) * half)):
        for index in range(half):
            both_ref[start + index] = source[index]


def fold(at, slot, kept, came, after=()):
    blocks, rows, width = kept.shape
    if blocks == 1:
        outs = [(kept.shape, jnp.bfloat16)]
        return local_call(add_kernel, "add", at, [kept, came], outs, after)[0]
    outs = [((blocks // 2, rows, width), jnp.bfloat16)] * 2
    return local_call(
        functools.partial(fold_kernel, slot), "fold", at, [kept, came], outs, after
    )


def join(at, slot, mine, came, after=()):
    blocks, rows, width = mine.shape
    outs = [((2 * blocks, rows, width), jnp.bfloat16)]
    return local_call(
        functools.partial(join_kernel, slot), "join", at, [mine, came], outs, after
    )[0]


def in_order(bit, mine, came):
    rows = mine.shape[0] * mine.shape[1]
    mine = mine.reshape(rows, -1).astype(jnp.float32)
    came = came.reshape(rows, -1).astype(jnp.float32)
    return jnp.where(bit == 0, mine, came), jnp.where(bit == 0, came, mine)


def finish_mlp_kernel(slot, at_ref, mine_ref, came_ref, *refs):
    up_ref, down_ref = refs[-2:]
    top, bottom = in_order(at_ref[slot], mine_ref[...], came_ref[...])
    up_ref[...] = top.T
    down_ref[...] = bottom


def finish_mlp(at, slot, start, mine, came, width, hidden, old=None, after=()):
    blocks, rows, _ = mine.shape
    unit = CHUNK // blocks
    part = pl.BlockSpec((blocks, unit, width), lambda i, at: (0, i, 0))
    return pl.pallas_call(
        functools.partial(finish_mlp_kernel, slot),
        grid_spec=pltpu.PrefetchScalarGridSpec(
            num_scalar_prefetch=1,
            grid=(rows // unit,),
            in_specs=[part, part]
            + [pl.BlockSpec(memory_space=pl.ANY)] * (len(old or []) + len(after)),
            out_specs=[
                pl.BlockSpec((width, CHUNK), lambda i, at: (0, start + i)),
                pl.BlockSpec((CHUNK, width), lambda i, at: (start + i, 0)),
            ],
        ),
        out_shape=[
            jax.ShapeDtypeStruct((width, hidden), jnp.float32),
            jax.ShapeDtypeStruct((hidden, width), jnp.float32),
        ],
        input_output_aliases={3: 0, 4: 1} if old else {},
        compiler_params=params(),
        cost_estimate=cost(1000, 1000),
        name="finish_mlp",
    )(at, mine, came, *(old or []), *after)


def finish_attend_kernel(slot, at_ref, mine_ref, came_ref, *refs):
    qkv_ref, out_ref = refs[-2:]
    top, bottom = in_order(at_ref[slot], mine_ref[...], came_ref[...])
    qkv_ref[0] = top[:PAIR].T
    qkv_ref[1] = top[PAIR:].T
    qkv_ref[2] = bottom[:PAIR].T
    out_ref[...] = bottom[PAIR:]


def finish_attend(at, slot, start, mine, came, width, local, old=None, after=()):
    blocks, rows, _ = mine.shape
    unit = 2 * PAIR // blocks
    part = pl.BlockSpec((blocks, unit, width), lambda i, at: (0, i, 0))
    return pl.pallas_call(
        functools.partial(finish_attend_kernel, slot),
        grid_spec=pltpu.PrefetchScalarGridSpec(
            num_scalar_prefetch=1,
            grid=(rows // unit,),
            in_specs=[part, part]
            + [pl.BlockSpec(memory_space=pl.ANY)] * (len(old or []) + len(after)),
            out_specs=[
                pl.BlockSpec((3, width, PAIR), lambda i, at: (0, 0, start + i)),
                pl.BlockSpec((PAIR, width), lambda i, at: (start + i, 0)),
            ],
        ),
        out_shape=[
            jax.ShapeDtypeStruct((3, width, local), jnp.float32),
            jax.ShapeDtypeStruct((local, width), jnp.float32),
        ],
        input_output_aliases={3: 0, 4: 1} if old else {},
        compiler_params=params(),
        cost_estimate=cost(1000, 1000),
        name="finish_attend",
    )(at, mine, came, *(old or []), *after)


def mp_swap(rows):
    return lax.ppermute(rows, "mp", [(0, 1), (1, 0)])


def dp_bits():
    return lax.axis_size("dp").bit_length() - 1


def orders(kind):
    if kind == 0:
        return (0, 1, 2, 3), (1, 0, 2, 3)
    return (2, 0, 1, 3), (2, 1, 0, 3)


def bit_swap(rows, bits):
    size, cores = lax.axis_size("dp"), lax.axis_size("mp")
    pairs = [
        (i * cores + core, (i ^ (1 << bits[core])) * cores + core)
        for i in range(size)
        for core in range(cores)
    ]
    return lax.ppermute(rows, ("dp", "mp"), pairs)


def step_bits(kind, step):
    return [order[step] for order in orders(kind)]


def slot_of(kind, step):
    return 1 + kind * SPLITS + step


def where_am_i():
    core, index = lax.axis_index("mp"), lax.axis_index("dp")
    values = [core]
    for kind in range(2):
        for step in range(SPLITS):
            bits = step_bits(kind, step)
            values.append((index >> jnp.where(core == 0, bits[0], bits[1])) & 1)
    return jnp.stack(values).astype(jnp.int32)


class Stream:
    def __init__(self, at, kind, kept, sent):
        self.at, self.kind, self.kept, self.step = at, kind, kept, 0
        self.came = bit_swap(sent, step_bits(kind, 0))

    def advance(self, after=()):
        step, kind = self.step, self.kind
        self.step += 1
        if step < SPLITS - 1:
            self.kept, sent = fold(
                self.at, slot_of(kind, step + 1), self.kept, self.came, after
            )
            self.came = bit_swap(sent, step_bits(kind, step + 1))
            return self.kept
        if step == SPLITS - 1:
            self.kept = fold(self.at, 0, self.kept, self.came, after)
            for bit in range(SPLITS, dp_bits()):
                other = bit_swap(self.kept, [bit, bit])
                self.kept = fold(self.at, 0, self.kept, other)
        else:
            bit_step = 2 * SPLITS - 1 - step
            self.kept = join(self.at, slot_of(kind, bit_step), self.kept, self.came, after)
        self.came = bit_swap(self.kept, step_bits(kind, 2 * SPLITS - 2 - step))
        return self.kept


def shards(
    history,
    depth_weights,
    gain_attn,
    gain_mlp,
    qkv_weight,
    out_weight,
    up_weight,
    down_weight,
    cotangent,
):
    width = cotangent.shape[1]
    local = out_weight.shape[0]
    hidden = down_weight.shape[0]
    pairs = local // PAIR
    chunks = hidden // CHUNK
    at = where_am_i()

    cot_other = mp_swap(cotangent)
    mixed, first = mix(depth_weights, history, gain_attn)
    first_other = mp_swap(first)
    qkv, att, lse, out_own, out_other = attend(at, first, first_other, qkv_weight, out_weight)
    middle, second = renorm(at, mixed, out_own, mp_swap(out_other), gain_mlp)
    second_other = mp_swap(second)
    early = 2 * chunks // 3
    kept_a, sent_a, kept_b, sent_b, hidden_rows, grad_pre = mlp(
        at, (slot_of(0, 0), slot_of(1, 0)), second, second_other, cotangent, cot_other,
        up_weight, down_weight,
    )
    mlp_a = Stream(at, 0, kept_a, sent_a)
    mlp_b = Stream(at, 1, kept_b, sent_b)
    grad_own, grad_other = rows_times(at, "second_back", grad_pre, up_weight, True)
    block_own, block_other = rows_times(
        at, "block", hidden_rows, down_weight, False, after=[grad_own]
    )
    grad_middle, narrow, gain_grad_mlp = norm_back_rows(
        at, grad_own, mp_swap(grad_other), middle, cotangent, gain_mlp, after=[block_own]
    )
    narrow_other = mp_swap(narrow)
    early_pairs = 2 * pairs // 3
    back_args = (qkv, att, lse, narrow, narrow_other, out_weight, first, first_other)
    kept, sent, early_rows = attend_back(at, slot_of(0, 0), 0, early_pairs, *back_args)
    att_a = Stream(at, 0, kept, sent)
    last = early_rows
    for stream in (mlp_a, mlp_b):
        last = stream.advance([last])
    kept, sent, late_rows = attend_back(
        at, slot_of(1, 0), early_pairs, pairs - early_pairs, *back_args, after=[last]
    )
    att_b = Stream(at, 1, kept, sent)
    first_own_grad, first_other_grad = first_back(at, qkv_weight, [early_rows, late_rows])
    first_came = mp_swap(first_other_grad)
    last = first_own_grad
    for stream in (mlp_b, mlp_a, att_a, att_b):
        last = stream.advance([last])
    grad_history, gain_grad_attn, depth_terms = unmix(
        depth_weights, history, gain_attn, mixed, grad_middle, first_own_grad, first_came,
        after=[last],
    )
    last = depth_terms
    block_out = (
        middle + block_own + mp_swap(block_other).astype(jnp.float32)
    ).astype(jnp.bfloat16)
    small = jnp.concatenate(
        [gain_grad_attn[0], gain_grad_mlp[0], jnp.sum(depth_terms, axis=1)]
    )
    small = small + mp_swap(small)
    for bit in range(dp_bits()):
        small = small + bit_swap(small, [bit, bit])
    gain_grad_attn, gain_grad_mlp, grad_depth = jnp.split(small, [width, 2 * width])

    streams = [mlp_b, mlp_a, att_b, att_a]
    while any(stream.step < 2 * SPLITS - 1 for stream in streams):
        for stream in streams:
            if stream.step < 2 * SPLITS - 1:
                last = stream.advance([last])
    grads = finish_mlp(
        at, slot_of(1, 0), early, mlp_b.kept, mlp_b.came, width, hidden, after=[last]
    )
    grad_up, grad_down = finish_mlp(
        at, slot_of(0, 0), 0, mlp_a.kept, mlp_a.came, width, hidden, grads
    )
    grads = finish_attend(
        at, slot_of(1, 0), early_pairs, att_b.kept, att_b.came, width, local, after=[grad_up]
    )
    grad_qkv, grad_out = finish_attend(
        at, slot_of(0, 0), 0, att_a.kept, att_a.came, width, local, grads
    )
    return (
        block_out,
        grad_history,
        grad_depth,
        gain_grad_attn,
        gain_grad_mlp,
        grad_qkv,
        grad_out,
        grad_up,
        grad_down,
    )


def solution(mesh):
    in_specs = (
        P(None, ("dp", "mp"), None),
        P(),
        P(),
        P(),
        P(None, None, "mp"),
        P("mp", None),
        P(None, "mp"),
        P("mp", None),
        P(("dp", "mp"), None),
    )
    out_specs = (
        P(("dp", "mp"), None),
        P(None, ("dp", "mp"), None),
        P(),
        P(),
        P(),
        P(None, None, "mp"),
        P("mp", None),
        P(None, "mp"),
        P("mp", None),
    )
    return jax.shard_map(shards, mesh=mesh, in_specs=in_specs, out_specs=out_specs, check_vma=False)
```

time: 428 us -> 254 us (0.59)
  matrix products: 97.3 us -> 0 us
  Pallas kernels: 0 us -> 96.7 us
  waiting for transfers between devices: 173 us -> 87.2 us
  other arithmetic: 74.3 us -> 4.4 us
  starting transfers between devices: 2.16 us -> 49.5 us
  blocking collectives: 44 us -> 0 us
  between operations: 14.8 us -> 1.45 us
  local copies, waits for them, and re-layouts: 16.8 us -> 11.1 us
    psum x1 -> x0, waiting for transfers between devices: 163 us -> none  [dp_sum(): return lax.psum(grad.astype(jnp.bfloat16), 'dp').astype(jnp.float32)]
    dot_general x18 -> x0, matrix products: 97.3 us -> none  [the longest x1 15.5 us: attend_back(): jnp.einsum('qhe,khe->hqk', grad_att, value_rows, preferred_element_type=j...]
    pallas_call x0 -> x43, Pallas kernels: none -> 96.7 us  [the longest x37 76.4 us: local_call(): pl.pallas_call(kernel, in_specs=[pl.BlockSpec(memory_space=pltpu.SMEM)] +...]
    ppermute x0 -> x36, waiting for transfers between devices: none -> 81.2 us  [bit_swap(): return lax.ppermute(rows, ('dp', 'mp'), pairs)]
    ppermute x0 -> x36, starting transfers between devices: none -> 47.2 us  [bit_swap(): return lax.ppermute(rows, ('dp', 'mp'), pairs)]
    psum x1 -> x0, blocking collectives: 44 us -> none  [shards(): lax.psum((grad_gain_attn, grad_gain_mlp, grad_depth), ('dp', 'mp'))]
    convert_element_type x8 -> x1, other arithmetic: 38.7 us -> 2.32 us  [shards(): block_out = (middle + block_own + mp_swap(block_other).astype(jnp.float32...]
    reduce_sum x8 -> x1, other arithmetic: 31.2 us -> 1.37 us  [shards(): jnp.sum(depth_terms, axis=1)]
  transfers between devices with their start and end apart: 9 -> 45, of which waited for: 6 -> 20; matrix products, arithmetic and copies ran while one was open for 11% -> 2% of each run, Pallas kernels for 0% -> 24%
where the time goes in v2:
time: 254 us; the launch traced here: 250 us
  Pallas kernels  96.7 us (38%)
  waiting for transfers between devices  87.2 us (34%)
  starting transfers between devices  49.5 us (19%)
  local copies, waits for them, and re-layouts  11.1 us (4%)
  other arithmetic  4.4 us (2%)
    ppermute x36, waiting for transfers between devices, bit_swap(): return lax.ppermute(rows, ('dp', 'mp'), pairs)  81.2 us
    pallas_call x37, Pallas kernels, local_call(): pl.pallas_call(kernel, in_specs=[pl.BlockSpec(memory_space=pltpu.SMEM)] +...  76.4 us
    ppermute x36, starting transfers between devices, bit_swap(): return lax.ppermute(rows, ('dp', 'mp'), pairs)  47.2 us
    unnamed x54, local copies, waits for them, and re-layouts  9.21 us
    pallas_call x2, Pallas kernels, finish_mlp(): pl.pallas_call(functools.partial(finish_mlp_kernel, slot), grid_spec=pltp...  7.21 us
    ppermute x9, waiting for transfers between devices, mp_swap(): return lax.ppermute(rows, 'mp', [(0, 1), (1, 0)])  6.08 us
    pallas_call x1, Pallas kernels, unmix(): pl.pallas_call(unmix_kernel, grid=(rows // ROW_BLOCK,), in_specs=[pl.Bloc...  6.05 us
  transfers between devices with their start and end apart: 45, of which 20 were waited for; matrix products, arithmetic and copies ran while one was open for 2% of the time, Pallas kernels for 24%

profile of v2, /device:TPU:0, one launch (start us, length us, event | category | flops | bytes accessed | tf_op | source)
XLA Modules:
  0.0 250.4 jit_solution(6946565958610885711)
XLA Ops:
  1.3 2.8 %copy-done = bf16[8,512,768]{2,1,0:T(8,128)(2,1)S(1)} copy-done((bf16[8,512,768]{2,1,0:T(8,128)(2,1)S(1)}, bf16[8,512,768]{2,1,0:T(8,128)(2,1)}, u32[]{:S(2)}) %copy-start) | copy-done | bytes 6291480
  4.8 2.8 %mix.1 = (f32[512,768]{1,0:T(8,128)S(1)}, bf16[512,768]{1,0:T(8,128)(2,1)S(1)}) custom-call(f32[8]{0:T(128)S(1)} %copy-done.21, bf16[8,512,768]{2,1,0:T(8,128)(2,1)S(1)} %copy-done, f32[1,768]{1,0:T(1,128)S(1)} %broadcast_in_dim.8.gain_ref), custom_call_target="tpu_custom_call" | custom-call | flops 11796480 | bytes 8650752 | tf_op jit(solution)/shard_map/mix/pallas_call | solution.py:75
  12.2 14.6 %attend.1 = (bf16[3,2,512,384]{3,2,1,0:T(8,128)(2,1)S(1)}, bf16[2,512,384]{2,1,0:T(8,128)(2,1)S(1)}, f32[3,2,2,1,512]{4,3,2,1,0:T(1,128)S(1)}, f32[512,768]{1,0:T(8,128)S(1)}, bf16[512,768]{1,0:T(8,128)(2,1)S(1)}) custom-call(s32[9]{0:T(128)S(1)} %stack.27.at_ref, bf16[512,768]{1,0:T(8,128)(2,1)S(1)} %get-tuple-element.75.own_ref.first_own_ref, ...), custom_call_target="tpu_custom_call" | custom-call | flops 1000 | bytes 1000 | tf_op jit(solution)/shard_map/attend/pallas_call | solution.py:165
  32.7 12.0 %mlp.1 = (bf16[8,128,768]{2,1,0:T(8,128)(2,1)S(1)}, bf16[8,128,768]{2,1,0:T(8,128)(2,1)S(1)}, bf16[8,64,768]{2,1,0:T(8,128)(2,1)S(1)}, bf16[8,64,768]{2,1,0:T(8,...) custom-call(s32[9]{0:T(128)S(1)} %stack.27.at_ref, ...), custom_call_target="tpu_custom_call" | custom-call | flops 1000 | bytes 1000 | tf_op jit(solution)/shard_map/mlp/pallas_call | solution.py:165
  45.8 3.4 %second_back.1 = (f32[512,768]{1,0:T(8,128)S(1)}, bf16[512,768]{1,0:T(8,128)(2,1)S(1)}) custom-call(s32[9]{0:T(128)S(1)} %stack.27.at_ref, bf16[2,512,1536]{2,1,0:T(8,128)(2,1)S(1)} %get-tuple-element.81.rows_ref, bf16[768,1536]{1,0:T(8,128)(2,1)S(1)} %copy-done.3), custom_call_target="tpu_custom_call" | custom-call | flops 1000 | bytes 1000 | tf_op jit(solution)/shard_map/second_back/pallas_call | solution.py:165
  49.7 2.6 %collective-permute-start.8 = (bf16[8,128,768]{2,1,0:T(8,128)(2,1)S(1)}, bf16[8,128,768]{2,1,0:T(8,128)(2,1)S(1)}, u32[]{:S(2)}, u32[]{:S(2)}) collective-permute-start(bf16[8,128,768]{2,1,0:T(8,128)(2,1)S(1)} %get-tuple-element.95), channel_id=1, source_target_pairs={{0,2},{1,5},{2,0},{3,7},{4,6},{5,1},{6,4},{7,3},{8,10},{9,13},{10,... | collective-permute-start | bytes 4718600 | tf_op jit(solution)/shard_map/ppermute | solution.py:661
  52.3 3.2 %block.1 = (f32[512,768]{1,0:T(8,128)S(1)}, bf16[512,768]{1,0:T(8,128)(2,1)}) custom-call(s32[9]{0:T(128)S(1)} %stack.27.at_ref, bf16[2,512,1536]{2,1,0:T(8,128)(2,1)S(1)} %get-tuple-element.80.rows_ref, bf16[1536,768]{1,0:T(8,128)(2,1)S(1)} %copy-done.2, f32[512,768]{1,0:T(8,128)S(1)} %get-tuple-element.82.refs_0_.own_ref), custom_call_target="tpu_custom_call" | custom-call | flops 1000 | bytes 1000 | tf_op jit(solution)/shard_map/block/pallas_call | solution.py:165
  59.6 13.2 %attend_back.2 = (bf16[8,64,768]{2,1,0:T(8,128)(2,1)S(1)}, bf16[8,64,768]{2,1,0:T(8,128)(2,1)S(1)}, bf16[3,2,512,256]{3,2,1,0:T(8,128)(2,1)S(1)}) custom-call(s32[9]{0:T(128)S(1)} %stack.27.at_ref, bf16[3,2,512,384]{3,2,1,0:T(8,128)(2,1)S(1)} %get-tuple-element.87.qkv_ref, bf16[2,512,384]{2,1,0:T(8,128)(2,1)S(1)} %copy-done.17, ...), custom_call_target="tpu_custom_call" | custom-call | flops 1000 | bytes 1000 | tf_op jit(solution)/shard_map/attend_back/pallas_call | solution.py:165
  79.3 6.7 %attend_back.3 = (bf16[8,32,768]{2,1,0:T(8,128)(2,1)S(1)}, bf16[8,32,768]{2,1,0:T(8,128)(2,1)S(1)}, bf16[3,2,512,128]{3,2,1,0:T(8,128)(2,1)S(1)}) custom-call(s32[9]{0:T(128)S(1)} %stack.27.at_ref, bf16[3,2,512,384]{3,2,1,0:T(8,128)(2,1)S(1)} %get-tuple-element.87.qkv_ref, bf16[2,512,384]{2,1,0:T(8,128)(2,1)S(1)} %copy-done.17, ...), custom_call_target="tpu_custom_call" | custom-call | flops 1000 | bytes 1000 | tf_op jit(solution)/shard_map/attend_back/pallas_call | solution.py:165
  86.0 3.2 %first_back.1 = (f32[512,768]{1,0:T(8,128)S(1)}, bf16[512,768]{1,0:T(8,128)(2,1)S(1)}) custom-call(s32[9]{0:T(128)S(1)} %stack.27.at_ref, bf16[3,768,384]{2,1,0:T(8,128)(2,1)S(1)} %copy-done.4, bf16[3,2,512,256]{3,2,1,0:T(8,128)(2,1)S(1)} %get-tuple-element.91.refs_0_, bf16[3,2,512,128]{3,2,1,0:T(8,128)(2,1)S(1)} %get-tuple-element.98.refs_1_), custom_call_target="tpu_custom_call" | custom-call | flops 1000 | bytes 1000 | tf_op jit(solution)/shard_map/first_back/pallas_call | solution.py:165
  90.9 6.7 %collective-permute-done.13.came_ref = bf16[4,64,768]{2,1,0:T(8,128)(2,1)S(1)} collective-permute-done((bf16[4,64,768]{2,1,0:T(8,128)(2,1)S(1)}, bf16[4,64,768]{2,1,0:T(8,128)(2,1)S(1)}, u32[]{:S(2)}, u32[]{:S(2)}) %collective-permute-start.13) | collective-permute-done | bytes 393248 | tf_op jit(solution)/shard_map/ppermute | solution.py:661
  105.9 6.1 %unmix.1 = (bf16[8,512,768]{2,1,0:T(8,128)(2,1)}, f32[1,768]{1,0:T(1,128)S(1)}, f32[8,768]{1,0:T(8,128)S(1)}) custom-call(f32[8]{0:T(128)S(1)} %copy-done.22, bf16[8,512,768]{2,1,0:T(8,128)(2,1)S(1)} %bitcast.6, f32[1,768]{1,0:T(1,128)S(1)} %broadcast_in_dim.8.gain_ref, f32[512,768]{1,0:T(8,128)S(1)} %copy-done.11, ...), custom_call_target="tpu_custom_call" | custom-call | flops 1000 | bytes 1000 | tf_op jit(solution)/shard_map/unmix/pallas_call | solution.py:123
  114.7 2.7 %collective-permute-start.25 = (bf16[1,128,768]{2,1,0:T(8,128)(2,1)S(1)}, bf16[1,128,768]{2,1,0:T(8,128)(2,1)S(1)}, u32[]{:S(2)}, u32[]{:S(2)}) collective-permute-start(bf16[1,128,768]{2,1,0:T(8,128)(2,1)S(1)} %get-tuple-element.125), channel_id=1, source_target_pairs={{0,16},{1,17},{2,18},{3,19},{4,20},{5,21},{6,22},{7,23},{8,24},{9,... | collective-permute-start | bytes 589832 | tf_op jit(solution)/shard_map/ppermute | solution.py:661
  119.5 11.2 %collective-permute-done.26.came_ref = bf16[1,64,768]{2,1,0:T(8,128)(2,1)S(1)} collective-permute-done((bf16[1,64,768]{2,1,0:T(8,128)(2,1)S(1)}, bf16[1,64,768]{2,1,0:T(8,128)(2,1)S(1)}, u32[]{:S(2)}, u32[]{:S(2)}) %collective-permute-start.26) | collective-permute-done | bytes 98336 | tf_op jit(solution)/shard_map/ppermute | solution.py:661
  133.0 2.8 %collective-permute-start.30 = (bf16[1,64,768]{2,1,0:T(8,128)(2,1)S(1)}, bf16[1,64,768]{2,1,0:T(8,128)(2,1)S(1)}, u32[]{:S(2)}, u32[]{:S(2)}) collective-permute-start(bf16[1,64,768]{2,1,0:T(8,128)(2,1)S(1)} %add.37.refs_0_.mine_ref), channel_id=1, source_target_pairs={{0,16},{1,17},{2,18},{3,19},{4,20},{5,21},{6,22},{7,23},{8,24},{9,... | collective-permute-start | bytes 294920 | tf_op jit(solution)/shard_map/ppermute | solution.py:661
  137.8 9.1 %collective-permute-done.30.came_ref = bf16[1,64,768]{2,1,0:T(8,128)(2,1)S(1)} collective-permute-done((bf16[1,64,768]{2,1,0:T(8,128)(2,1)S(1)}, bf16[1,64,768]{2,1,0:T(8,128)(2,1)S(1)}, u32[]{:S(2)}, u32[]{:S(2)}) %collective-permute-start.30) | collective-permute-done | bytes 98336 | tf_op jit(solution)/shard_map/ppermute | solution.py:661
  149.1 2.8 %collective-permute-start.27 = (bf16[1,64,768]{2,1,0:T(8,128)(2,1)S(1)}, bf16[1,64,768]{2,1,0:T(8,128)(2,1)S(1)}, u32[]{:S(2)}, u32[]{:S(2)}) collective-permute-start(bf16[1,64,768]{2,1,0:T(8,128)(2,1)S(1)} %get-tuple-element.129), channel_id=1, source_target_pairs={{0,16},{1,17},{2,18},{3,19},{4,20},{5,21},{6,22},{7,23},{8,24},{9,... | collective-permute-start | bytes 294920 | tf_op jit(solution)/shard_map/ppermute | solution.py:661
  152.0 8.1 %collective-permute-done.28.came_ref = bf16[1,32,768]{2,1,0:T(8,128)(2,1)S(1)} collective-permute-done((bf16[1,32,768]{2,1,0:T(8,128)(2,1)S(1)}, bf16[1,32,768]{2,1,0:T(8,128)(2,1)S(1)}, u32[]{:S(2)}, u32[]{:S(2)}) %collective-permute-start.28) | collective-permute-done | bytes 49184 | tf_op jit(solution)/shard_map/ppermute | solution.py:661
  165.1 2.9 %collective-permute-start.31 = (bf16[1,64,768]{2,1,0:T(8,128)(2,1)S(1)}, bf16[1,64,768]{2,1,0:T(8,128)(2,1)S(1)}, u32[]{:S(2)}, u32[]{:S(2)}) collective-permute-start(bf16[1,64,768]{2,1,0:T(8,128)(2,1)S(1)} %add.40.refs_0_.mine_ref), channel_id=1, source_target_pairs={{0,16},{1,17},{2,18},{3,19},{4,20},{5,21},{6,22},{7,23},{8,24},{9,... | collective-permute-start | bytes 294920 | tf_op jit(solution)/shard_map/ppermute | solution.py:661
  168.0 6.8 %collective-permute-done.32.came_ref = bf16[1,32,768]{2,1,0:T(8,128)(2,1)S(1)} collective-permute-done((bf16[1,32,768]{2,1,0:T(8,128)(2,1)S(1)}, bf16[1,32,768]{2,1,0:T(8,128)(2,1)S(1)}, u32[]{:S(2)}, u32[]{:S(2)}) %collective-permute-start.32) | collective-permute-done | bytes 49184 | tf_op jit(solution)/shard_map/ppermute | solution.py:661
  179.9 3.2 %collective-permute-start.35 = (bf16[2,64,768]{2,1,0:T(8,128)(2,1)S(1)}, bf16[2,64,768]{2,1,0:T(8,128)(2,1)S(1)}, u32[]{:S(2)}, u32[]{:S(2)}) collective-permute-start(bf16[2,64,768]{2,1,0:T(8,128)(2,1)S(1)} %join.17.refs_0_.mine_ref), channel_id=1, source_target_pairs={{0,8},{1,9},{2,10},{3,11},{4,12},{5,13},{6,14},{7,15},{8,0},{9,1},... | collective-permute-start | bytes 589832 | tf_op jit(solution)/shard_map/ppermute | solution.py:661
  184.0 4.8 %collective-permute-done.36.came_ref = bf16[2,32,768]{2,1,0:T(8,128)(2,1)S(1)} collective-permute-done((bf16[2,32,768]{2,1,0:T(8,128)(2,1)S(1)}, bf16[2,32,768]{2,1,0:T(8,128)(2,1)S(1)}, u32[]{:S(2)}, u32[]{:S(2)}) %collective-permute-start.36) | collective-permute-done | bytes 98336 | tf_op jit(solution)/shard_map/ppermute | solution.py:661
  194.3 12.2 %collective-permute-done.40.came_ref = bf16[4,32,768]{2,1,0:T(8,128)(2,1)S(1)} collective-permute-done((bf16[4,32,768]{2,1,0:T(8,128)(2,1)S(1)}, bf16[4,32,768]{2,1,0:T(8,128)(2,1)S(1)}, u32[]{:S(2)}, u32[]{:S(2)}) %collective-permute-start.40) | collective-permute-done | bytes 196640 | tf_op jit(solution)/shard_map/ppermute | solution.py:661
  206.5 3.3 %collective-permute-start.44 = (bf16[8,64,768]{2,1,0:T(8,128)(2,1)S(1)}, bf16[8,64,768]{2,1,0:T(8,128)(2,1)S(1)}, u32[]{:S(2)}, u32[]{:S(2)}) collective-permute-start(bf16[8,64,768]{2,1,0:T(8,128)(2,1)S(1)} %join.18.refs_0_.mine_ref), channel_id=1, source_target_pairs={{0,8},{1,9},{2,10},{3,11},{4,12},{5,13},{6,14},{7,15},{8,0},{9,1},... | collective-permute-start | bytes 2359304 | tf_op jit(solution)/shard_map/ppermute | solution.py:661
  213.1 10.0 %collective-permute-done.15 = f32[1544]{0:T(1024)S(1)} collective-permute-done((f32[1544]{0:T(1024)S(1)}, f32[1544]{0:T(1024)S(1)}, u32[]{:S(2)}, u32[]{:S(2)}) %collective-permute-start.15) | collective-permute-done | bytes 6208 | tf_op jit(solution)/shard_map/ppermute | solution.py:661
  224.2 2.5 %collective-permute-done.16 = f32[1544]{0:T(1024)S(1)} collective-permute-done((f32[1544]{0:T(1024)S(1)}, f32[1544]{0:T(1024)S(1)}, u32[]{:S(2)}, u32[]{:S(2)}) %collective-permute-start.16) | collective-permute-done | bytes 6208 | tf_op jit(solution)/shard_map/ppermute | solution.py:661
  226.7 3.8 %collective-permute-done.17 = f32[1544]{0:T(1024)S(1)} collective-permute-done((f32[1544]{0:T(1024)S(1)}, f32[1544]{0:T(1024)S(1)}, u32[]{:S(2)}, u32[]{:S(2)}) %collective-permute-start.17) | collective-permute-done | bytes 6208 | tf_op jit(solution)/shard_map/ppermute | solution.py:661
  232.6 2.3 add_convert_fusion
  236.3 2.5 finish_mlp.2
  238.8 4.7 %finish_mlp.3 = (f32[768,1536]{1,0:T(8,128)}, f32[1536,768]{1,0:T(8,128)}) custom-call(s32[9]{0:T(128)S(1)} %stack.27.at_ref, bf16[8,128,768]{2,1,0:T(8,128)(2,1)S(1)} %join.19.refs_0_.mine_ref, bf16[8,128,768]{2,1,0:T(8,128)(2,1)} %collective-permute-done.43.came_ref, ...), custom_call_target="tpu_custom_call", output_to_operand_aliasing={{0}: (3, {}), {1}: (4, {})} | custom-call | flops 1000 | bytes 1000 | tf_op jit(solution)/shard_map/finish_mlp/pallas_call | solution.py:581
  243.6 2.3 copy-done.1
  247.7 2.5 finish_attend.3
  (171 shorter events, 71.2 us)
Async XLA Ops:
  49.7 23.2 %collective-permute-start.8 = (bf16[8,128,768]{2,1,0:T(8,128)(2,1)S(1)}, bf16[8,128,768]{2,1,0:T(8,128)(2,1)S(1)}, u32[]{:S(2)}, u32[]{:S(2)}) collective-permute-start(bf16[8,128,768]{2,1,0:T(8,128)(2,1)S(1)} %get-tuple-element.95), channel_id=1, source_target_pairs={{0,2},{1,5},{2,0},{3,7},{4,6},{5,1},{6,4},{7,3},{8,10},{9,13},{10,... | collective-permute-start | bytes 4718600 | tf_op jit(solution)/shard_map/ppermute | solution.py:661
  57.5 19.8 %collective-permute-start.7 = (bf16[8,64,768]{2,1,0:T(8,128)(2,1)S(1)}, bf16[8,64,768]{2,1,0:T(8,128)(2,1)S(1)}, u32[]{:S(2)}, u32[]{:S(2)}) collective-permute-start(bf16[8,64,768]{2,1,0:T(8,128)(2,1)S(1)} %get-tuple-element.93), channel_id=1, source_target_pairs={{0,8},{1,9},{2,10},{3,11},{4,12},{5,13},{6,14},{7,15},{8,0},{9,1},... | collective-permute-start | bytes 2359304 | tf_op jit(solution)/shard_map/ppermute | solution.py:661
  73.7 24.5 %collective-permute-start.12 = (bf16[4,128,768]{2,1,0:T(8,128)(2,1)S(1)}, bf16[4,128,768]{2,1,0:T(8,128)(2,1)S(1)}, u32[]{:S(2)}, u32[]{:S(2)}) collective-permute-start(bf16[4,128,768]{2,1,0:T(8,128)(2,1)S(1)} %get-tuple-element.105), channel_id=1, source_target_pairs={{0,4},{1,3},{2,6},{3,1},{4,0},{5,7},{6,2},{7,5},{8,12},{9,11},{10,... | collective-permute-start | bytes 2359304 | tf_op jit(solution)/shard_map/ppermute | solution.py:661
  75.4 25.3 %collective-permute-start.11 = (bf16[8,64,768]{2,1,0:T(8,128)(2,1)S(1)}, bf16[8,64,768]{2,1,0:T(8,128)(2,1)S(1)}, u32[]{:S(2)}, u32[]{:S(2)}) collective-permute-start(bf16[8,64,768]{2,1,0:T(8,128)(2,1)S(1)} %get-tuple-element.104), channel_id=1, source_target_pairs={{0,2},{1,5},{2,0},{3,7},{4,6},{5,1},{6,4},{7,3},{8,10},{9,13},{10,... | collective-permute-start | bytes 2359304 | tf_op jit(solution)/shard_map/ppermute | solution.py:661
  78.0 19.6 %collective-permute-start.13 = (bf16[4,64,768]{2,1,0:T(8,128)(2,1)S(1)}, bf16[4,64,768]{2,1,0:T(8,128)(2,1)S(1)}, u32[]{:S(2)}, u32[]{:S(2)}) collective-permute-start(bf16[4,64,768]{2,1,0:T(8,128)(2,1)S(1)} %get-tuple-element.106), channel_id=1, source_target_pairs={{0,2},{1,5},{2,0},{3,7},{4,6},{5,1},{6,4},{7,3},{8,10},{9,13},{10,... | collective-permute-start | bytes 1179656 | tf_op jit(solution)/shard_map/ppermute | solution.py:661
  89.2 16.6 %collective-permute-start.9 = (bf16[512,768]{1,0:T(8,128)(2,1)S(1)}, bf16[512,768]{1,0:T(8,128)(2,1)S(1)}, u32[]{:S(2)}, u32[]{:S(2)}) collective-permute-start(bf16[512,768]{1,0:T(8,128)(2,1)S(1)} %get-tuple-element.100), channel_id=1, source_target_pairs={{0,1},{1,0},{2,3},{3,2},{4,5},{5,4},{6,7},{7,6},{8,9},{9,8},{10,11... | collective-permute-start | bytes 2359304 | tf_op jit(solution)/shard_map/ppermute | solution.py:641
  89.3 14.2 %collective-permute-start.10 = (bf16[8,32,768]{2,1,0:T(8,128)(2,1)S(1)}, bf16[8,32,768]{2,1,0:T(8,128)(2,1)S(1)}, u32[]{:S(2)}, u32[]{:S(2)}) collective-permute-start(bf16[8,32,768]{2,1,0:T(8,128)(2,1)S(1)} %get-tuple-element.102), channel_id=1, source_target_pairs={{0,8},{1,9},{2,10},{3,11},{4,12},{5,13},{6,14},{7,15},{8,0},{9,1},... | collective-permute-start | bytes 1179656 | tf_op jit(solution)/shard_map/ppermute | solution.py:661
  99.0 15.0 %collective-permute-start.21 = (bf16[2,128,768]{2,1,0:T(8,128)(2,1)S(1)}, bf16[2,128,768]{2,1,0:T(8,128)(2,1)S(1)}, u32[]{:S(2)}, u32[]{:S(2)}) collective-permute-start(bf16[2,128,768]{2,1,0:T(8,128)(2,1)S(1)} %get-tuple-element.117), channel_id=1, source_target_pairs={{0,8},{1,9},{2,10},{3,11},{4,12},{5,13},{6,14},{7,15},{8,0},{9,1},... | collective-permute-start | bytes 1179656 | tf_op jit(solution)/shard_map/ppermute | solution.py:661
  101.4 16.9 %collective-permute-start.19 = (bf16[4,64,768]{2,1,0:T(8,128)(2,1)S(1)}, bf16[4,64,768]{2,1,0:T(8,128)(2,1)S(1)}, u32[]{:S(2)}, u32[]{:S(2)}) collective-permute-start(bf16[4,64,768]{2,1,0:T(8,128)(2,1)S(1)} %get-tuple-element.115), channel_id=1, source_target_pairs={{0,4},{1,3},{2,6},{3,1},{4,0},{5,7},{6,2},{7,5},{8,12},{9,11},{10,... | collective-permute-start | bytes 1179656 | tf_op jit(solution)/shard_map/ppermute | solution.py:661
  103.0 10.5 %collective-permute-start.22 = (bf16[2,64,768]{2,1,0:T(8,128)(2,1)S(1)}, bf16[2,64,768]{2,1,0:T(8,128)(2,1)S(1)}, u32[]{:S(2)}, u32[]{:S(2)}) collective-permute-start(bf16[2,64,768]{2,1,0:T(8,128)(2,1)S(1)} %get-tuple-element.118), channel_id=1, source_target_pairs={{0,4},{1,3},{2,6},{3,1},{4,0},{5,7},{6,2},{7,5},{8,12},{9,11},{10,... | collective-permute-start | bytes 589832 | tf_op jit(solution)/shard_map/ppermute | solution.py:661
  104.1 13.6 %collective-permute-start.20 = (bf16[4,32,768]{2,1,0:T(8,128)(2,1)S(1)}, bf16[4,32,768]{2,1,0:T(8,128)(2,1)S(1)}, u32[]{:S(2)}, u32[]{:S(2)}) collective-permute-start(bf16[4,32,768]{2,1,0:T(8,128)(2,1)S(1)} %get-tuple-element.116), channel_id=1, source_target_pairs={{0,2},{1,5},{2,0},{3,7},{4,6},{5,1},{6,4},{7,3},{8,10},{9,13},{10,... | collective-permute-start | bytes 589832 | tf_op jit(solution)/shard_map/ppermute | solution.py:661
  114.7 16.6 %collective-permute-start.25 = (bf16[1,128,768]{2,1,0:T(8,128)(2,1)S(1)}, bf16[1,128,768]{2,1,0:T(8,128)(2,1)S(1)}, u32[]{:S(2)}, u32[]{:S(2)}) collective-permute-start(bf16[1,128,768]{2,1,0:T(8,128)(2,1)S(1)} %get-tuple-element.125), channel_id=1, source_target_pairs={{0,16},{1,17},{2,18},{3,19},{4,20},{5,21},{6,22},{7,23},{8,24},{9,... | collective-permute-start | bytes 589832 | tf_op jit(solution)/shard_map/ppermute | solution.py:661
  117.3 13.4 %collective-permute-start.26 = (bf16[1,64,768]{2,1,0:T(8,128)(2,1)S(1)}, bf16[1,64,768]{2,1,0:T(8,128)(2,1)S(1)}, u32[]{:S(2)}, u32[]{:S(2)}) collective-permute-start(bf16[1,64,768]{2,1,0:T(8,128)(2,1)S(1)} %get-tuple-element.126), channel_id=1, source_target_pairs={{0,16},{1,17},{2,18},{3,19},{4,20},{5,21},{6,22},{7,23},{8,24},{9,... | collective-permute-start | bytes 294920 | tf_op jit(solution)/shard_map/ppermute | solution.py:661
  118.9 18.3 %collective-permute-start.23 = (bf16[2,64,768]{2,1,0:T(8,128)(2,1)S(1)}, bf16[2,64,768]{2,1,0:T(8,128)(2,1)S(1)}, u32[]{:S(2)}, u32[]{:S(2)}) collective-permute-start(bf16[2,64,768]{2,1,0:T(8,128)(2,1)S(1)} %get-tuple-element.123), channel_id=1, source_target_pairs={{0,8},{1,9},{2,10},{3,11},{4,12},{5,13},{6,14},{7,15},{8,0},{9,1},... | collective-permute-start | bytes 589832 | tf_op jit(solution)/shard_map/ppermute | solution.py:661
  131.9 15.6 %collective-permute-start.29 = (bf16[1,128,768]{2,1,0:T(8,128)(2,1)S(1)}, bf16[1,128,768]{2,1,0:T(8,128)(2,1)S(1)}, u32[]{:S(2)}, u32[]{:S(2)}) collective-permute-start(bf16[1,128,768]{2,1,0:T(8,128)(2,1)S(1)} %add.38.refs_0_.mine_ref), channel_id=1, source_target_pairs={{0,16},{1,17},{2,18},{3,19},{4,20},{5,21},{6,22},{7,23},{8,24},{9,... | collective-permute-start | bytes 589832 | tf_op jit(solution)/shard_map/ppermute | solution.py:661
  133.0 13.9 %collective-permute-start.30 = (bf16[1,64,768]{2,1,0:T(8,128)(2,1)S(1)}, bf16[1,64,768]{2,1,0:T(8,128)(2,1)S(1)}, u32[]{:S(2)}, u32[]{:S(2)}) collective-permute-start(bf16[1,64,768]{2,1,0:T(8,128)(2,1)S(1)} %add.37.refs_0_.mine_ref), channel_id=1, source_target_pairs={{0,16},{1,17},{2,18},{3,19},{4,20},{5,21},{6,22},{7,23},{8,24},{9,... | collective-permute-start | bytes 294920 | tf_op jit(solution)/shard_map/ppermute | solution.py:661
  148.1 14.3 %collective-permute-start.33 = (bf16[2,128,768]{2,1,0:T(8,128)(2,1)S(1)}, bf16[2,128,768]{2,1,0:T(8,128)(2,1)S(1)}, u32[]{:S(2)}, u32[]{:S(2)}) collective-permute-start(bf16[2,128,768]{2,1,0:T(8,128)(2,1)S(1)} %join.13.refs_0_.mine_ref), channel_id=1, source_target_pairs={{0,8},{1,9},{2,10},{3,11},{4,12},{5,13},{6,14},{7,15},{8,0},{9,1},... | collective-permute-start | bytes 1179656 | tf_op jit(solution)/shard_map/ppermute | solution.py:661
  148.1 13.1 %collective-permute-start.34 = (bf16[2,64,768]{2,1,0:T(8,128)(2,1)S(1)}, bf16[2,64,768]{2,1,0:T(8,128)(2,1)S(1)}, u32[]{:S(2)}, u32[]{:S(2)}) collective-permute-start(bf16[2,64,768]{2,1,0:T(8,128)(2,1)S(1)} %join.12.refs_0_.mine_ref), channel_id=1, source_target_pairs={{0,4},{1,3},{2,6},{3,1},{4,0},{5,7},{6,2},{7,5},{8,12},{9,11},{10,... | collective-permute-start | bytes 589832 | tf_op jit(solution)/shard_map/ppermute | solution.py:661
  149.1 11.6 %collective-permute-start.27 = (bf16[1,64,768]{2,1,0:T(8,128)(2,1)S(1)}, bf16[1,64,768]{2,1,0:T(8,128)(2,1)S(1)}, u32[]{:S(2)}, u32[]{:S(2)}) collective-permute-start(bf16[1,64,768]{2,1,0:T(8,128)(2,1)S(1)} %get-tuple-element.129), channel_id=1, source_target_pairs={{0,16},{1,17},{2,18},{3,19},{4,20},{5,21},{6,22},{7,23},{8,24},{9,... | collective-permute-start | bytes 294920 | tf_op jit(solution)/shard_map/ppermute | solution.py:661
  162.9 15.0 %collective-permute-start.37 = (bf16[4,128,768]{2,1,0:T(8,128)(2,1)S(1)}, bf16[4,128,768]{2,1,0:T(8,128)(2,1)S(1)}, u32[]{:S(2)}, u32[]{:S(2)}) collective-permute-start(bf16[4,128,768]{2,1,0:T(8,128)(2,1)S(1)} %join.15.refs_0_.mine_ref), channel_id=1, source_target_pairs={{0,4},{1,3},{2,6},{3,1},{4,0},{5,7},{6,2},{7,5},{8,12},{9,11},{10,... | collective-permute-start | bytes 2359304 | tf_op jit(solution)/shard_map/ppermute | solution.py:661
  163.9 12.1 %collective-permute-start.38 = (bf16[4,64,768]{2,1,0:T(8,128)(2,1)S(1)}, bf16[4,64,768]{2,1,0:T(8,128)(2,1)S(1)}, u32[]{:S(2)}, u32[]{:S(2)}) collective-permute-start(bf16[4,64,768]{2,1,0:T(8,128)(2,1)S(1)} %join.14.refs_0_.mine_ref), channel_id=1, source_target_pairs={{0,2},{1,5},{2,0},{3,7},{4,6},{5,1},{6,4},{7,3},{8,10},{9,13},{10,... | collective-permute-start | bytes 1179656 | tf_op jit(solution)/shard_map/ppermute | solution.py:661
  165.1 10.3 %collective-permute-start.31 = (bf16[1,64,768]{2,1,0:T(8,128)(2,1)S(1)}, bf16[1,64,768]{2,1,0:T(8,128)(2,1)S(1)}, u32[]{:S(2)}, u32[]{:S(2)}) collective-permute-start(bf16[1,64,768]{2,1,0:T(8,128)(2,1)S(1)} %add.40.refs_0_.mine_ref), channel_id=1, source_target_pairs={{0,16},{1,17},{2,18},{3,19},{4,20},{5,21},{6,22},{7,23},{8,24},{9,... | collective-permute-start | bytes 294920 | tf_op jit(solution)/shard_map/ppermute | solution.py:661
  178.6 60.2 %collective-permute-start.43 = (bf16[8,128,768]{2,1,0:T(8,128)(2,1)S(1)}, bf16[8,128,768]{2,1,0:T(8,128)(2,1)}, u32[]{:S(2)}, u32[]{:S(2)}) collective-permute-start(bf16[8,128,768]{2,1,0:T(8,128)(2,1)S(1)} %join.19.refs_0_.mine_ref), channel_id=1, source_target_pairs={{0,2},{1,5},{2,0},{3,7},{4,6},{5,1},{6,4},{7,3},{8,10},{9,13},{10,... | collective-permute-start | bytes 4718600 | tf_op jit(solution)/shard_map/ppermute | solution.py:661
  179.9 9.5 %collective-permute-start.35 = (bf16[2,64,768]{2,1,0:T(8,128)(2,1)S(1)}, bf16[2,64,768]{2,1,0:T(8,128)(2,1)S(1)}, u32[]{:S(2)}, u32[]{:S(2)}) collective-permute-start(bf16[2,64,768]{2,1,0:T(8,128)(2,1)S(1)} %join.17.refs_0_.mine_ref), channel_id=1, source_target_pairs={{0,8},{1,9},{2,10},{3,11},{4,12},{5,13},{6,14},{7,15},{8,0},{9,1},... | collective-permute-start | bytes 589832 | tf_op jit(solution)/shard_map/ppermute | solution.py:661
  183.1 47.5 %collective-permute-start.4 = (bf16[512,768]{1,0:T(8,128)(2,1)}, bf16[512,768]{1,0:T(8,128)(2,1)}, u32[]{:S(2)}, u32[]{:S(2)}) collective-permute-start(bf16[512,768]{1,0:T(8,128)(2,1)} %get-tuple-element.84), channel_id=1, source_target_pairs={{0,1},{1,0},{2,3},{3,2},{4,5},{5,4},{6,7},{7,6},{8,9},{9,8},{10,11... | collective-permute-start | bytes 2359304 | tf_op jit(solution)/shard_map/ppermute | solution.py:641
  190.0 20.4 %collective-permute-start.39 = (bf16[4,64,768]{2,1,0:T(8,128)(2,1)S(1)}, bf16[4,64,768]{2,1,0:T(8,128)(2,1)S(1)}, u32[]{:S(2)}, u32[]{:S(2)}) collective-permute-start(bf16[4,64,768]{2,1,0:T(8,128)(2,1)S(1)} %join.21.refs_0_.mine_ref), channel_id=1, source_target_pairs={{0,4},{1,3},{2,6},{3,1},{4,0},{5,7},{6,2},{7,5},{8,12},{9,11},{10,... | collective-permute-start | bytes 1179656 | tf_op jit(solution)/shard_map/ppermute | solution.py:661
  191.0 15.5 %collective-permute-start.40 = (bf16[4,32,768]{2,1,0:T(8,128)(2,1)S(1)}, bf16[4,32,768]{2,1,0:T(8,128)(2,1)S(1)}, u32[]{:S(2)}, u32[]{:S(2)}) collective-permute-start(bf16[4,32,768]{2,1,0:T(8,128)(2,1)S(1)} %join.20.refs_0_.mine_ref), channel_id=1, source_target_pairs={{0,2},{1,5},{2,0},{3,7},{4,6},{5,1},{6,4},{7,3},{8,10},{9,13},{10,... | collective-permute-start | bytes 589832 | tf_op jit(solution)/shard_map/ppermute | solution.py:661
  194.2 17.9 %collective-permute-start.14 = (f32[1544]{0:T(1024)S(1)}, f32[1544]{0:T(1024)S(1)}, u32[]{:S(2)}, u32[]{:S(2)}) collective-permute-start(f32[1544]{0:T(1024)S(1)} %pad_maximum_fusion), channel_id=1, source_target_pairs={{0,1},{1,0},{2,3},{3,2},{4,5},{5,4},{6,7},{7,6},{8,9},{9,8},{10,11... | collective-permute-start | bytes 18536 | tf_op jit(solution)/shard_map/ppermute | solution.py:641
  206.5 29.8 %collective-permute-start.44 = (bf16[8,64,768]{2,1,0:T(8,128)(2,1)S(1)}, bf16[8,64,768]{2,1,0:T(8,128)(2,1)S(1)}, u32[]{:S(2)}, u32[]{:S(2)}) collective-permute-start(bf16[8,64,768]{2,1,0:T(8,128)(2,1)S(1)} %join.18.refs_0_.mine_ref), channel_id=1, source_target_pairs={{0,8},{1,9},{2,10},{3,11},{4,12},{5,13},{6,14},{7,15},{8,0},{9,1},... | collective-permute-start | bytes 2359304 | tf_op jit(solution)/shard_map/ppermute | solution.py:661
  210.9 36.8 %collective-permute-start.41 = (bf16[8,64,768]{2,1,0:T(8,128)(2,1)S(1)}, bf16[8,64,768]{2,1,0:T(8,128)(2,1)S(1)}, u32[]{:S(2)}, u32[]{:S(2)}) collective-permute-start(bf16[8,64,768]{2,1,0:T(8,128)(2,1)S(1)} %join.23.refs_0_.mine_ref), channel_id=1, source_target_pairs={{0,2},{1,5},{2,0},{3,7},{4,6},{5,1},{6,4},{7,3},{8,10},{9,13},{10,... | collective-permute-start | bytes 2359304 | tf_op jit(solution)/shard_map/ppermute | solution.py:661
  212.1 10.9 %collective-permute-start.15 = (f32[1544]{0:T(1024)S(1)}, f32[1544]{0:T(1024)S(1)}, u32[]{:S(2)}, u32[]{:S(2)}) collective-permute-start(f32[1544]{0:T(1024)S(1)} %fusion.1), channel_id=1, source_target_pairs={{0,2},{1,3},{2,0},{3,1},{4,6},{5,7},{6,4},{7,5},{8,10},{9,11},{10,... | collective-permute-start | bytes 18536 | tf_op jit(solution)/shard_map/ppermute | solution.py:661
  230.6 13.0 %collective-permute-start.42 = (bf16[8,32,768]{2,1,0:T(8,128)(2,1)S(1)}, bf16[8,32,768]{2,1,0:T(8,128)(2,1)S(1)}, u32[]{:S(2)}, u32[]{:S(2)}) collective-permute-start(bf16[8,32,768]{2,1,0:T(8,128)(2,1)S(1)} %join.22.refs_0_.mine_ref), channel_id=1, source_target_pairs={{0,8},{1,9},{2,10},{3,11},{4,12},{5,13},{6,14},{7,15},{8,0},{9,1},... | collective-permute-start | bytes 1179656 | tf_op jit(solution)/shard_map/ppermute | solution.py:661
  (40 other events, 395.7 us)

commit v3 on v2

v3 whole, which is shorter than its diff:
```python
import functools

import jax
import jax.numpy as jnp
from jax import lax
from jax.experimental import pallas as pl
from jax.experimental.pallas import tpu as pltpu
from jax.sharding import PartitionSpec as P

HEAD_DIM = 64
EPSILON = 1e-05
SQRT_HALF = 0.7071067811865476
INV_ROOT_TWO_PI = 0.3989422804014327
LOG2E = 1.4426950408889634
NEG = -1e30
TILE = 256
ROW_BLOCK = 64
VMEM_BYTES = 32 * 2**20
SPLITS = 4
PAIR = 2 * HEAD_DIM
CHUNK = 512
ORDER = (
    "nb", "ab0", "ab1", "Mb", "ab2", "fb", "Ma", "Aa", "Mb", "um", "Ab", "Mb", "Ma", "Ab",
    "Aa", "Ma", "Mb", "sm", "Ab", "Aa", "blk", "sm", "Ab", "Ma", "Aa", "sm", "Mb", "Ab", "Ab",
    "Ma", "sm", "Aa", "Ma", "Ab", "Aa", "Mb", "Ma", "sm", "bo", "Mb", "fAb", "Aa", "fMa",
    "fAa", "fMb",
)
KINDS = (
    ((0, 1, 2, 3), (2, 0, 1, 3)),
    ((1, 0, 2, 3), (2, 1, 0, 3)),
    ((0, 1, 2, 3), (1, 0, 2, 3)),
    ((2, 0, 1, 3), (2, 1, 0, 3)),
)
KIND = {"Ma": 0, "Mb": 1, "Aa": 2, "Ab": 3}
EARLY = 3

PLAIN = (((1,), (0,)), ((), ()))
CONTRACT_COLS = (((1,), (1,)), ((), ()))
CONTRACT_ROWS = (((0,), (0,)), ((), ()))


def dot(lhs, rhs, dims=PLAIN):
    return lax.dot_general(lhs, rhs, dims, preferred_element_type=jnp.float32)


def cost(flops, moved, exps=0):
    return pl.CostEstimate(flops=flops, bytes_accessed=moved, transcendentals=exps)


def params():
    return pltpu.CompilerParams(vmem_limit_bytes=VMEM_BYTES)


def normalize(inputs):
    row_mean = jnp.mean(inputs, axis=-1, keepdims=True)
    centered = inputs - row_mean
    variance = jnp.mean(centered * centered, axis=-1, keepdims=True)
    inv_scale = lax.rsqrt(variance + EPSILON)
    return centered * inv_scale, inv_scale


def norm_back(grad_rows, gain_row, normed, inv_scale):
    scaled = grad_rows * gain_row
    first_mean = jnp.mean(scaled, axis=-1, keepdims=True)
    second_mean = jnp.mean(scaled * normed, axis=-1, keepdims=True)
    return inv_scale * (scaled - first_mean - normed * second_mean)


def gelu_value(inputs):
    return 0.5 * inputs * (1.0 + lax.erf(inputs * SQRT_HALF))


def gelu_slope(inputs):
    normal_cdf = 0.5 * (1.0 + lax.erf(inputs * SQRT_HALF))
    return normal_cdf + inputs * jnp.exp(-0.5 * inputs * inputs) * INV_ROOT_TWO_PI


def layer_copies(history_ref, held_ref, sems, out=False):
    copies = []
    for index in range(held_ref.shape[0]):
        rows = pl.ds(index * ROW_BLOCK, ROW_BLOCK)
        ends = (history_ref.at[:, rows, :], held_ref.at[index])
        copies.append(
            pltpu.make_async_copy(ends[out], ends[not out], sems.at[index])
        )
    return copies


def mix_kernel(weights_ref, gain_ref, history_ref, mixed_ref, first_ref, held_ref, sems):
    copies = layer_copies(history_ref, held_ref, sems)
    for copy in copies:
        copy.start()
    for index, copy in enumerate(copies):
        rows = pl.ds(index * ROW_BLOCK, ROW_BLOCK)
        copy.wait()
        mixed = weights_ref[0] * held_ref[index, 0].astype(jnp.float32)
        for layer in range(1, held_ref.shape[1]):
            mixed = mixed + weights_ref[layer] * held_ref[index, layer].astype(jnp.float32)
        mixed_ref[rows, :] = mixed
        normed, _ = normalize(mixed)
        first_ref[rows, :] = (normed * gain_ref[...]).astype(jnp.bfloat16)


def mix(weights, history, gain):
    layers, rows, width = history.shape
    in_vmem = pl.BlockSpec(memory_space=pltpu.VMEM)
    blocks = rows // ROW_BLOCK
    return pl.pallas_call(
        mix_kernel,
        in_specs=[
            pl.BlockSpec(memory_space=pltpu.SMEM),
            in_vmem,
            pl.BlockSpec(memory_space=pltpu.HBM),
        ],
        out_specs=[in_vmem, in_vmem],
        out_shape=[
            jax.ShapeDtypeStruct((rows, width), jnp.float32),
            jax.ShapeDtypeStruct((rows, width), jnp.bfloat16),
        ],
        scratch_shapes=[
            pltpu.VMEM((blocks, layers, ROW_BLOCK, width), jnp.bfloat16),
            pltpu.SemaphoreType.DMA((blocks,)),
        ],
        compiler_params=params(),
        cost_estimate=cost(1000, 1000),
        name="mix",
    )(weights, gain[None], history)


def unmix_kernel(
    weights_ref, gain_ref, mixed_ref, middle_ref, own_ref, other_ref, gain_mlp_ref, history_ref,
    *refs,
):
    grads_ref, small_ref, held_ref, given_ref, in_sems, out_sems = refs[-6:]
    copies = layer_copies(history_ref, held_ref, in_sems)
    gives = layer_copies(grads_ref, given_ref, out_sems, True)
    for copy in copies:
        copy.start()
    layers = held_ref.shape[1]
    small_ref[...] = jnp.zeros_like(small_ref)
    small_ref[1:2] = gain_mlp_ref[...]
    for index, (copy, give) in enumerate(zip(copies, gives)):
        rows = pl.ds(index * ROW_BLOCK, ROW_BLOCK)
        grad_first = own_ref[rows, :] + other_ref[rows, :].astype(jnp.float32)
        normed, inv_scale = normalize(mixed_ref[rows, :])
        grad_mixed = middle_ref[rows, :] + norm_back(
            grad_first, gain_ref[...], normed, inv_scale
        )
        small_ref[0:1] += jnp.sum(grad_first * normed, axis=0, keepdims=True)
        copy.wait()
        for layer in range(layers):
            given_ref[index, layer] = (weights_ref[layer] * grad_mixed).astype(jnp.bfloat16)
            product = held_ref[index, layer].astype(jnp.float32) * grad_mixed
            small_ref[8 + layer : 9 + layer] += jnp.sum(product, axis=0, keepdims=True)
        give.start()
    for give in gives:
        give.wait()


def unmix(weights, history, gain, mixed, grad_middle, own, other, gain_grad_mlp, after=()):
    layers, rows, width = history.shape
    in_vmem = pl.BlockSpec(memory_space=pltpu.VMEM)
    in_hbm = pl.BlockSpec(memory_space=pltpu.HBM)
    blocks = rows // ROW_BLOCK
    held = pltpu.VMEM((blocks, layers, ROW_BLOCK, width), jnp.bfloat16)
    return pl.pallas_call(
        unmix_kernel,
        in_specs=[pl.BlockSpec(memory_space=pltpu.SMEM)]
        + [in_vmem] * 6
        + [in_hbm]
        + [pl.BlockSpec(memory_space=pl.ANY)] * len(after),
        out_specs=[in_hbm, in_vmem],
        out_shape=[
            jax.ShapeDtypeStruct(history.shape, jnp.bfloat16),
            jax.ShapeDtypeStruct((8 + layers, width), jnp.float32),
        ],
        scratch_shapes=[
            held,
            held,
            pltpu.SemaphoreType.DMA((blocks,)),
            pltpu.SemaphoreType.DMA((blocks,)),
        ],
        compiler_params=params(),
        cost_estimate=cost(1000, 1000),
        name="unmix",
    )(weights, gain[None], mixed, grad_middle, own, other, gain_grad_mlp, history, *after)


def head_mask(head):
    lanes = lax.broadcasted_iota(jnp.int32, (1, PAIR), 1)
    return (lanes // HEAD_DIM) == head


def future_mask():
    keys = lax.broadcasted_iota(jnp.int32, (TILE, TILE), 0)
    asks = lax.broadcasted_iota(jnp.int32, (TILE, TILE), 1)
    return keys > asks


def local_call(kernel, name, at, arrays, outs, after=(), scratch=(), aliases=None):
    in_vmem = pl.BlockSpec(memory_space=pltpu.VMEM)
    return pl.pallas_call(
        kernel,
        in_specs=[pl.BlockSpec(memory_space=pltpu.SMEM)]
        + [in_vmem] * len(arrays)
        + [pl.BlockSpec(memory_space=pl.ANY)] * len(after),
        out_specs=[in_vmem] * len(outs),
        out_shape=[jax.ShapeDtypeStruct(shape, dtype) for shape, dtype in outs],
        scratch_shapes=list(scratch),
        input_output_aliases=aliases or {},
        compiler_params=params(),
        cost_estimate=cost(1000, 1000),
        name=name,
    )(at, *arrays, *after)


def attend_kernel(
    at_ref, own_ref, other_ref, weight_ref, out_weight_ref,
    qkv_ref, att_ref, lse_ref, out_own_ref, out_other_ref,
):
    rows = own_ref.shape[0]
    tiles = rows // TILE
    first = at_ref[0]
    scale = HEAD_DIM ** (-0.5) * LOG2E
    places = (first, 1 - first)
    later = future_mask()

    def one_pair(pair, carry):
        lanes = pl.ds(pl.multiple_of(pair * PAIR, PAIR), PAIR)
        weight = jnp.concatenate([weight_ref[c, :, lanes] for c in range(3)], axis=1)
        for side, ref in enumerate((own_ref, other_ref)):
            made = dot(ref[...], weight).astype(jnp.bfloat16)
            for c in range(3):
                qkv_ref[c, side, :, lanes] = made[:, c * PAIR : (c + 1) * PAIR]
        half_keys = [qkv_ref[1, places[half], :, lanes] for half in range(2)]
        half_values = [qkv_ref[2, places[half], :, lanes].T for half in range(2)]
        for half in range(2):
            for tile in range(tiles):
                at_rows = pl.ds(tile * TILE, TILE)
                queries = qkv_ref[0, places[half], at_rows, lanes]
                outs = []
                for head in range(2):
                    asked = jnp.where(head_mask(head), queries, jnp.zeros_like(queries))
                    spans = []
                    if half == 1:
                        spans.append((0, 0, rows))
                    if tile > 0:
                        spans.append((half, 0, tile * TILE))
                    spans.append((half, tile * TILE, TILE))
                    scores = [
                        dot(half_keys[where][start : start + size], asked, CONTRACT_COLS)
                        for where, start, size in spans
                    ]
                    scores[-1] = jnp.where(later, NEG, scores[-1])
                    top = functools.reduce(
                        jnp.maximum, [jnp.max(part, axis=0, keepdims=True) for part in scores]
                    )
                    top = top * scale
                    total = 0.0
                    summed = 0.0
                    mine = slice(head * HEAD_DIM, (head + 1) * HEAD_DIM)
                    for part, (where, start, size) in zip(scores, spans):
                        weights = jnp.exp2(part * scale - top)
                        total = total + jnp.sum(weights, axis=0, keepdims=True)
                        summed = summed + dot(
                            half_values[where][mine, start : start + size],
                            weights.astype(jnp.bfloat16),
                        )
                    outs.append(summed / total)
                    lse_ref[pair, head, half, :, at_rows] = top + jnp.log2(total)
                joined = jnp.concatenate(outs, axis=0).T
                att_ref[places[half], at_rows, lanes] = joined.astype(jnp.bfloat16)
        return carry

    lax.fori_loop(0, att_ref.shape[2] // PAIR, one_pair, 0)
    out_other_ref[...] = dot(att_ref[1], out_weight_ref[...]).astype(jnp.bfloat16)
    out_own_ref[...] = dot(att_ref[0], out_weight_ref[...])


def attend(at, own, other, weight, out_weight):
    rows, width = own.shape
    local = weight.shape[2]
    return local_call(
        attend_kernel,
        "attend",
        at,
        [own, other, weight, out_weight],
        [
            ((3, 2, rows, local), jnp.bfloat16),
            ((2, rows, local), jnp.bfloat16),
            ((local // PAIR, 2, 2, 1, rows), jnp.float32),
            ((rows, width), jnp.float32),
            ((rows, width), jnp.bfloat16),
        ],
    )


def renorm_kernel(at_ref, mixed_ref, own_ref, other_ref, gain_ref, middle_ref, second_ref):
    middle = mixed_ref[...] + own_ref[...] + other_ref[...].astype(jnp.float32)
    middle_ref[...] = middle
    second_ref[...] = (normalize(middle)[0] * gain_ref[...]).astype(jnp.bfloat16)


def renorm(at, mixed, own, other, gain):
    return local_call(
        renorm_kernel,
        "renorm",
        at,
        [mixed, own, other, gain[None]],
        [(mixed.shape, jnp.float32), (mixed.shape, jnp.bfloat16)],
    )


def split_halves(bit, rows, top, bottom, keep_ref, send_ref):
    shape = (keep_ref.shape[0], -1, keep_ref.shape[2])
    top = top.astype(jnp.bfloat16).reshape(shape)
    bottom = bottom.astype(jnp.bfloat16).reshape(shape)
    keep_ref[:, rows, :] = jnp.where(bit == 0, top, bottom)
    send_ref[:, rows, :] = jnp.where(bit == 0, bottom, top)


def mlp_kernel(
    slots, at_ref, second_own_ref, second_other_ref, cot_own_ref, cot_other_ref, up_ref, down_ref,
    *refs,
):
    (
        keep_a_ref, send_a_ref, keep_b_ref, send_b_ref, hidden_ref, own_ref, other_ref, grad_pre_ref
    ) = refs[-8:]
    bf16 = jnp.bfloat16
    chunks = hidden_ref.shape[2] // CHUNK
    sides = ((second_own_ref, cot_own_ref), (second_other_ref, cot_other_ref))
    unit = TILE // keep_a_ref.shape[0]
    early = keep_a_ref.shape[1] // unit

    def make(chunk):
        lanes = pl.ds(chunk * CHUNK, CHUNK)
        for side, (second_ref, cot_ref) in enumerate(sides):
            pre = dot(second_ref[...], up_ref[:, lanes])
            cdf = 0.5 * (1.0 + lax.erf(pre * SQRT_HALF))
            hidden_ref[side, :, lanes] = (pre * cdf).astype(bf16)
            slope = cdf + pre * jnp.exp(-0.5 * pre * pre) * INV_ROOT_TWO_PI
            grad_hidden = dot(cot_ref[...], down_ref[lanes, :], CONTRACT_COLS)
            grad_pre_ref[side, :, lanes] = (grad_hidden * slope).astype(bf16)

    def give(chunk):
        lanes = pl.ds(chunk * CHUNK, CHUNK)
        grad_up, grad_down = 0.0, 0.0
        for side, (second_ref, cot_ref) in enumerate(sides):
            grad_up = grad_up + dot(grad_pre_ref[side, :, lanes], second_ref[...], CONTRACT_ROWS)
            grad_down = grad_down + dot(hidden_ref[side, :, lanes], cot_ref[...], CONTRACT_ROWS)
        for part in range(CHUNK // TILE):
            tile = chunk * (CHUNK // TILE) + part
            late = tile >= early
            refs = (keep_b_ref, send_b_ref) if late else (keep_a_ref, send_a_ref)
            place = pl.ds((tile - early if late else tile) * unit, unit)
            rows = slice(part * TILE, (part + 1) * TILE)
            split_halves(at_ref[slots[late]], place, grad_up[rows], grad_down[rows], *refs)

    make(0)
    for chunk in range(1, chunks):
        make(chunk)
        give(chunk - 1)
    give(chunks - 1)
    other_ref[...] = dot(grad_pre_ref[1], up_ref[...], CONTRACT_COLS).astype(bf16)
    own_ref[...] = dot(grad_pre_ref[0], up_ref[...], CONTRACT_COLS)


def mlp(at, slots, second_own, second_other, cot_own, cot_other, up, down, after=()):
    rows, width = second_own.shape
    hidden = down.shape[0]
    blocks = 2 ** (SPLITS - 1)
    tiles = hidden // TILE
    unit = TILE // blocks
    pieces = [
        ((blocks, count * unit, width), jnp.bfloat16) for count in (EARLY, tiles - EARLY)
    ]
    return local_call(
        functools.partial(mlp_kernel, slots),
        "mlp",
        at,
        [second_own, second_other, cot_own, cot_other, up, down],
        [pieces[0], pieces[0], pieces[1], pieces[1]]
        + [
            ((2, rows, hidden), jnp.bfloat16),
            ((rows, width), jnp.float32),
            ((rows, width), jnp.bfloat16),
        ],
        after,
        [pltpu.VMEM((2, rows, hidden), jnp.bfloat16)],
    )


def rows_kernel(at_ref, rows_ref, weight_ref, *refs):
    own_ref, other_ref = refs[-2:]
    other_ref[...] = dot(rows_ref[1], weight_ref[...]).astype(jnp.bfloat16)
    own_ref[...] = dot(rows_ref[0], weight_ref[...])


def rows_times(at, rows, weight, after=()):
    shape = (rows.shape[1], weight.shape[1])
    return local_call(
        rows_kernel, "block", at, [rows, weight], [(shape, jnp.float32), (shape, jnp.bfloat16)],
        after,
    )


def block_kernel(at_ref, middle_ref, own_ref, other_ref, *refs):
    total = middle_ref[...] + own_ref[...] + other_ref[...].astype(jnp.float32)
    refs[-1][...] = total.astype(jnp.bfloat16)


def block_sum(at, middle, own, other, after=()):
    outs = [(middle.shape, jnp.bfloat16)]
    return local_call(block_kernel, "block_sum", at, [middle, own, other], outs, after)[0]


def small_kernel(at_ref, mine_ref, came_ref, *refs):
    refs[-1][...] = mine_ref[...] + came_ref[...]


def small_sum(at, mine, came, after=()):
    outs = [(mine.shape, jnp.float32)]
    return local_call(small_kernel, "small", at, [mine, came], outs, after)[0]


def norm_back_kernel(at_ref, own_ref, other_ref, middle_ref, cot_ref, gain_ref, *refs):
    grad_ref, narrow_ref, gain_grad_ref = refs[-3:]
    grad_second = own_ref[...] + other_ref[...].astype(jnp.float32)
    normed, inv_scale = normalize(middle_ref[...])
    grad = cot_ref[...].astype(jnp.float32) + norm_back(
        grad_second, gain_ref[...], normed, inv_scale
    )
    grad_ref[...] = grad
    narrow_ref[...] = grad.astype(jnp.bfloat16)
    gain_grad_ref[...] = jnp.sum(grad_second * normed, axis=0, keepdims=True)


def norm_back_rows(at, own, other, middle, cotangent, gain, after=()):
    shape = own.shape
    return local_call(
        norm_back_kernel,
        "norm_back_rows",
        at,
        [own, other, middle, cotangent, gain[None]],
        [(shape, jnp.float32), (shape, jnp.bfloat16), ((1, shape[1]), jnp.float32)],
        after,
    )


def attend_back_kernel(
    slot, pair, place, at_ref, qkv_ref, att_ref, lse_ref, grad_own_ref, grad_other_ref, out_weight_ref,
    first_own_ref, first_other_ref, *refs,
):
    keep_ref, send_ref, grad_rows_ref = refs[-3:]
    rows = grad_own_ref.shape[0]
    tiles = rows // TILE
    first = at_ref[0]
    plain = HEAD_DIM ** (-0.5)
    scale = plain * LOG2E
    places = (first, 1 - first)
    later = future_mask()
    bf16 = jnp.bfloat16
    sides = (grad_own_ref, grad_other_ref)
    firsts = (first_own_ref, first_other_ref)
    masked = [head_mask(head) for head in range(2)]
    unit = 4 * PAIR // (2 * keep_ref.shape[0])
    is_own = [places[half] == 0 for half in range(2)]
    chunks = [(half, tile) for half in range(2) for tile in range(tiles)]

    def only(head, part):
        return jnp.where(masked[head], part, jnp.zeros_like(part))

    def plus(old, term):
        return term if old is None else old + term

    lanes = pl.ds(pair * PAIR, PAIR)
    outer = [
        dot(ref[...], out_weight_ref[lanes, :], CONTRACT_COLS).astype(bf16) for ref in sides
    ]
    grads = [jnp.where(is_own[half], outer[0], outer[1]) for half in range(2)]
    queries, keys, values = [
        [qkv_ref[c, places[half], :, lanes] for half in range(2)] for c in range(3)
    ]
    keys_t = [part.T for part in keys]
    deltas = []
    for half in range(2):
        attended = att_ref[places[half], :, lanes].astype(jnp.float32)
        product = (grads[half].astype(jnp.float32) * attended).T
        deltas.append([
            jnp.sum(product[head * HEAD_DIM : (head + 1) * HEAD_DIM], axis=0, keepdims=True)
            for head in range(2)
        ])
    key_grads = [None for _ in chunks]
    value_grads = [None for _ in chunks]
    query_grads = []
    for ask, (ask_half, ask_tile) in enumerate(chunks):
        ask_rows = slice(ask_tile * TILE, (ask_tile + 1) * TILE)
        sums_here = []
        for head in range(2):
            asked = only(head, queries[ask_half][ask_rows])
            grad = only(head, grads[ask_half][ask_rows])
            lse = lse_ref[pair, head, ask_half, :, ask_rows]
            delta = deltas[ask_half][head][:, ask_rows]
            query_grad = None
            for key in range(ask + 1):
                key_half, key_tile = chunks[key]
                key_rows = slice(key_tile * TILE, (key_tile + 1) * TILE)
                scores = dot(keys[key_half][key_rows], asked, CONTRACT_COLS)
                probs = jnp.exp2(scores * scale - lse)
                if key == ask:
                    probs = jnp.where(later, 0.0, probs)
                grad_probs = dot(values[key_half][key_rows], grad, CONTRACT_COLS)
                grad_scores = (probs * (grad_probs - delta)).astype(bf16)
                value_grads[key] = plus(value_grads[key], dot(probs.astype(bf16), grad))
                key_grads[key] = plus(key_grads[key], dot(grad_scores, asked))
                mine = slice(head * HEAD_DIM, (head + 1) * HEAD_DIM)
                query_grad = plus(
                    query_grad, dot(keys_t[key_half][mine, key_rows], grad_scores)
                )
            sums_here.append(query_grad)
        query_grads.append((jnp.concatenate(sums_here, axis=0) * plain).astype(bf16))
    turned = []
    for half in range(2):
        at_half = [i for i, (where, _) in enumerate(chunks) if where == half]
        query_t = jnp.concatenate([query_grads[i] for i in at_half], axis=1)
        key = jnp.concatenate([(key_grads[i] * plain).astype(bf16) for i in at_half], axis=0)
        value = jnp.concatenate([value_grads[i].astype(bf16) for i in at_half], axis=0)
        turned.append([query_t, key.T, value.T, att_ref[places[half], :, lanes].T])
        for c, part in enumerate((query_t.T, key, value)):
            grad_rows_ref[c, places[half]] = part
    top, bottom = 0.0, 0.0
    for side in range(2):
        mine = [jnp.where(is_own[side], a, b) for a, b in zip(turned[0], turned[1])]
        rows_here = firsts[side][...]
        top = top + dot(jnp.concatenate(mine[:2], axis=0), rows_here)
        bottom = bottom + jnp.concatenate(
            [dot(mine[2], rows_here), dot(mine[3], sides[side][...])], axis=0
        )
    split_halves(
        at_ref[slot], pl.ds(place * unit, unit), top, bottom, keep_ref, send_ref
    )


def attend_back(at, slot, pair, place, count, qkv, att, lse, grad_own, grad_other, out_weight,
                first_own, first_other, old=(), after=()):
    rows, width = grad_own.shape
    blocks = 2 ** (SPLITS - 1)
    unit = 4 * PAIR // (2 * blocks)
    pieces = ((blocks, count * unit, width), jnp.bfloat16)
    arrays = [qkv, att, lse, grad_own, grad_other, out_weight, first_own, first_other, *old]
    return local_call(
        functools.partial(attend_back_kernel, slot, pair, place),
        "attend_back",
        at,
        arrays,
        [pieces, pieces, ((3, 2, rows, PAIR), jnp.bfloat16)],
        after,
        aliases={len(arrays) - 1: 0, len(arrays): 1} if old else {},
    )


def first_back_kernel(count, at_ref, weight_ref, *refs):
    own_ref, other_ref = refs[-2:]
    groups = []
    start = 0
    for ref in refs[:count]:
        groups.append((ref, start))
        start += ref.shape[3]
    for side, out_ref in ((1, other_ref), (0, own_ref)):
        total = 0.0
        for ref, begin in groups:
            for c in range(3):
                lanes = slice(begin, begin + ref.shape[3])
                total = total + dot(ref[c, side], weight_ref[c, :, lanes], CONTRACT_COLS)
        out_ref[...] = total.astype(out_ref.dtype)


def first_back(at, weight, groups, after=()):
    shape = (groups[0].shape[2], weight.shape[1])
    return local_call(
        functools.partial(first_back_kernel, len(groups)), "first_back", at, [weight, *groups],
        [(shape, jnp.float32), (shape, jnp.bfloat16)], after,
    )


def fold_kernel(slot, at_ref, kept_ref, came_ref, *refs):
    keep_ref, send_ref = refs[-2:]
    half = keep_ref.shape[0]
    bit = at_ref[slot]
    for target, start in ((send_ref, (1 - bit) * half), (keep_ref, bit * half)):
        for index in range(half):
            total = kept_ref[start + index].astype(jnp.float32) + came_ref[
                start + index
            ].astype(jnp.float32)
            target[index] = total.astype(jnp.bfloat16)


def add_kernel(at_ref, kept_ref, came_ref, *refs):
    total = kept_ref[...].astype(jnp.float32) + came_ref[...].astype(jnp.float32)
    refs[-1][...] = total.astype(jnp.bfloat16)


def join_kernel(slot, at_ref, mine_ref, came_ref, *refs):
    both_ref = refs[-1]
    half = mine_ref.shape[0]
    bit = at_ref[slot]
    for source, start in ((mine_ref, bit * half), (came_ref, (1 - bit) * half)):
        for index in range(half):
            both_ref[start + index] = source[index]


def fold(at, slot, kept, came, after=()):
    blocks, rows, width = kept.shape
    if blocks == 1:
        outs = [(kept.shape, jnp.bfloat16)]
        return local_call(add_kernel, "add", at, [kept, came], outs, after)[0]
    outs = [((blocks // 2, rows, width), jnp.bfloat16)] * 2
    return local_call(
        functools.partial(fold_kernel, slot), "fold", at, [kept, came], outs, after
    )


def join(at, slot, mine, came, after=()):
    blocks, rows, width = mine.shape
    outs = [((2 * blocks, rows, width), jnp.bfloat16)]
    return local_call(
        functools.partial(join_kernel, slot), "join", at, [mine, came], outs, after
    )[0]


def in_order(bit, mine, came):
    rows = mine.shape[0] * mine.shape[1]
    mine = mine.reshape(rows, -1).astype(jnp.float32)
    came = came.reshape(rows, -1).astype(jnp.float32)
    return jnp.where(bit == 0, mine, came), jnp.where(bit == 0, came, mine)


def finish_mlp_kernel(slot, at_ref, mine_ref, came_ref, *refs):
    up_ref, down_ref, token_ref = refs[-3:]
    token_ref[...] = jnp.zeros_like(token_ref)
    top, bottom = in_order(at_ref[slot], mine_ref[...], came_ref[...])
    up_ref[...] = top.T
    down_ref[...] = bottom


def finish_mlp(at, slot, start, mine, came, width, hidden, old=None, after=()):
    blocks, rows, _ = mine.shape
    unit = TILE // blocks
    part = pl.BlockSpec((blocks, unit, TILE), lambda i, j, at: (0, i, j))
    return pl.pallas_call(
        functools.partial(finish_mlp_kernel, slot),
        grid_spec=pltpu.PrefetchScalarGridSpec(
            num_scalar_prefetch=1,
            grid=(rows // unit, width // TILE),
            in_specs=[part, part]
            + [pl.BlockSpec(memory_space=pl.ANY)] * (len(old or []) + len(after)),
            out_specs=[
                pl.BlockSpec((TILE, TILE), lambda i, j, at: (j, start + i)),
                pl.BlockSpec((TILE, TILE), lambda i, j, at: (start + i, j)),
                pl.BlockSpec((8, 128), lambda i, j, at: (0, 0)),
            ],
        ),
        out_shape=[
            jax.ShapeDtypeStruct((width, hidden), jnp.float32),
            jax.ShapeDtypeStruct((hidden, width), jnp.float32),
            jax.ShapeDtypeStruct((8, 128), jnp.float32),
        ],
        input_output_aliases={3: 0, 4: 1} if old else {},
        compiler_params=params(),
        cost_estimate=cost(1000, 1000),
        name="finish_mlp",
    )(at, mine, came, *(old or []), *after)


def finish_attend_kernel(slot, at_ref, mine_ref, came_ref, *refs):
    qkv_ref, out_ref, token_ref = refs[-3:]
    token_ref[...] = jnp.zeros_like(token_ref)
    top, bottom = in_order(at_ref[slot], mine_ref[...], came_ref[...])
    qkv_ref[0] = top[:PAIR].T
    qkv_ref[1] = top[PAIR:].T
    qkv_ref[2] = bottom[:PAIR].T
    out_ref[...] = bottom[PAIR:]


def finish_attend(at, slot, start, mine, came, width, local, old=None, after=()):
    blocks, rows, _ = mine.shape
    unit = 2 * PAIR // blocks
    part = pl.BlockSpec((blocks, unit, TILE), lambda i, j, at: (0, i, j))
    return pl.pallas_call(
        functools.partial(finish_attend_kernel, slot),
        grid_spec=pltpu.PrefetchScalarGridSpec(
            num_scalar_prefetch=1,
            grid=(rows // unit, width // TILE),
            in_specs=[part, part]
            + [pl.BlockSpec(memory_space=pl.ANY)] * (len(old or []) + len(after)),
            out_specs=[
                pl.BlockSpec((3, TILE, PAIR), lambda i, j, at: (0, j, start + i)),
                pl.BlockSpec((PAIR, TILE), lambda i, j, at: (start + i, j)),
                pl.BlockSpec((8, 128), lambda i, j, at: (0, 0)),
            ],
        ),
        out_shape=[
            jax.ShapeDtypeStruct((3, width, local), jnp.float32),
            jax.ShapeDtypeStruct((local, width), jnp.float32),
            jax.ShapeDtypeStruct((8, 128), jnp.float32),
        ],
        input_output_aliases={3: 0, 4: 1} if old else {},
        compiler_params=params(),
        cost_estimate=cost(1000, 1000),
        name="finish_attend",
    )(at, mine, came, *(old or []), *after)


def mp_swap(rows):
    return lax.ppermute(rows, "mp", [(0, 1), (1, 0)])


def dp_bits():
    return lax.axis_size("dp").bit_length() - 1


def bit_swap(rows, bits):
    size, cores = lax.axis_size("dp"), lax.axis_size("mp")
    pairs = [
        (i * cores + core, (i ^ (1 << bits[core])) * cores + core)
        for i in range(size)
        for core in range(cores)
    ]
    return lax.ppermute(rows, ("dp", "mp"), pairs)


def step_bits(kind, step):
    return [order[step] for order in KINDS[kind]]


def slot_of(kind, step):
    return 1 + kind * SPLITS + step


def where_am_i():
    core, index = lax.axis_index("mp"), lax.axis_index("dp")
    values = [core]
    for kind in range(len(KINDS)):
        for step in range(SPLITS):
            bits = step_bits(kind, step)
            values.append((index >> jnp.where(core == 0, bits[0], bits[1])) & 1)
    return jnp.stack(values).astype(jnp.int32)


class Stream:
    def __init__(self, at, kind, kept, sent):
        self.at, self.kind, self.kept, self.step = at, kind, kept, 0
        self.came = bit_swap(sent, step_bits(kind, 0))

    def advance(self, after=()):
        step, kind = self.step, self.kind
        self.step += 1
        if step < SPLITS - 1:
            self.kept, sent = fold(
                self.at, slot_of(kind, step + 1), self.kept, self.came, after
            )
            self.came = bit_swap(sent, step_bits(kind, step + 1))
            return self.kept
        if step == SPLITS - 1:
            self.kept = fold(self.at, 0, self.kept, self.came, after)
            for bit in range(SPLITS, dp_bits()):
                other = bit_swap(self.kept, [bit, bit])
                self.kept = fold(self.at, 0, self.kept, other)
        else:
            bit_step = 2 * SPLITS - 1 - step
            self.kept = join(self.at, slot_of(kind, bit_step), self.kept, self.came, after)
        self.came = bit_swap(self.kept, step_bits(kind, 2 * SPLITS - 2 - step))
        return self.kept


def shards(
    history,
    depth_weights,
    gain_attn,
    gain_mlp,
    qkv_weight,
    out_weight,
    up_weight,
    down_weight,
    cotangent,
):
    width = cotangent.shape[1]
    local = out_weight.shape[0]
    hidden = down_weight.shape[0]
    pairs = local // PAIR
    at = where_am_i()

    cot_other = mp_swap(cotangent)
    mixed, first = mix(depth_weights, history, gain_attn)
    first_other = mp_swap(first)
    qkv, att, lse, out_own, out_other = attend(at, first, first_other, qkv_weight, out_weight)
    middle, second = renorm(at, mixed, out_own, mp_swap(out_other), gain_mlp)
    second_other = mp_swap(second)
    kept_a, sent_a, kept_b, sent_b, hidden_rows, grad_own, grad_other = mlp(
        at, (slot_of(KIND["Ma"], 0), slot_of(KIND["Mb"], 0)), second, second_other, cotangent, cot_other,
        up_weight, down_weight,
    )
    streams = {
        "Ma": Stream(at, KIND["Ma"], kept_a, sent_a),
        "Mb": Stream(at, KIND["Mb"], kept_b, sent_b),
    }
    grad_came = mp_swap(grad_other)
    made = {}

    def back_norm(after):
        made["middle"], made["narrow"], made["gain"] = norm_back_rows(
            at, grad_own, grad_came, middle, cotangent, gain_mlp, after
        )
        made["narrow_came"] = mp_swap(made["narrow"])
        return made["gain"]

    def back_pair(pair, after):
        late = pair == pairs - 1
        name, place = ("Ab", 0) if late else ("Aa", pair)
        old = () if late or pair == 0 else made["stack"]
        kept, sent, made[pair] = attend_back(
            at, slot_of(KIND[name], 0), pair, place, 1 if late else pairs - 1, qkv, att, lse,
            made["narrow"], made["narrow_came"], out_weight, first, first_other, old, after,
        )
        made["stack"] = (kept, sent)
        if pair >= pairs - 2:
            streams[name] = Stream(at, KIND[name], kept, sent)
        return made[pair]

    def back_first(after):
        groups = [made[pair] for pair in range(pairs)]
        made["own"], other = first_back(at, qkv_weight, groups, after)
        made["came"] = mp_swap(other)
        return made["own"]

    def back_start(after):
        made["history"], made["small"] = unmix(
            depth_weights, history, gain_attn, mixed, made["middle"], made["own"], made["came"],
            made["gain"], after,
        )
        made["small_came"] = mp_swap(made["small"])
        return made["small"]

    def small_step(bit, after):
        made["small"] = small_sum(at, made["small"], made["small_came"], after)
        if bit < dp_bits():
            made["small_came"] = bit_swap(made["small"], [bit, bit])
        return made["small"]

    def block_rows(after):
        made["block"], other = rows_times(at, hidden_rows, down_weight, after)
        made["block_came"] = mp_swap(other)
        return made["block"]

    def block_end(after):
        made["out"] = block_sum(at, middle, made["block"], made["block_came"], after)
        return made["out"]

    def end_mlp(name, start, after):
        stream = streams[name]
        *made["mlp"], token = finish_mlp(
            at, slot_of(KIND[name], 0), start, stream.kept, stream.came, width, hidden,
            made.get("mlp"), after,
        )
        return token

    def end_attend(name, start, after):
        stream = streams[name]
        *made["attend"], token = finish_attend(
            at, slot_of(KIND[name], 0), start, stream.kept, stream.came, width, local,
            made.get("attend"), after,
        )
        return token

    units = {
        "nb": back_norm,
        "fb": back_first,
        "um": back_start,
        "blk": block_rows,
        "bo": block_end,
        "fMa": functools.partial(end_mlp, "Ma", 0),
        "fMb": functools.partial(end_mlp, "Mb", EARLY),
        "fAa": functools.partial(end_attend, "Aa", 0),
        "fAb": functools.partial(end_attend, "Ab", pairs - 1),
    }
    for pair in range(pairs):
        units["ab" + str(pair)] = functools.partial(back_pair, pair)
    bits = 0
    last = hidden_rows
    for name in ORDER:
        if name in streams:
            last = streams[name].advance([last])
        elif name == "sm":
            last = small_step(bits, [last])
            bits += 1
        else:
            last = units[name]([last])
    for bit in range(bits, dp_bits() + 1):
        last = small_step(bit, [last])
    small = made["small"]
    grad_depth = jnp.sum(small[8:], axis=1)
    block_out, grad_history = made["out"], made["history"]
    gain_grad_attn, gain_grad_mlp = small[0], small[1]
    (grad_up, grad_down), (grad_qkv, grad_out) = made["mlp"], made["attend"]
    return (
        block_out,
        grad_history,
        grad_depth,
        gain_grad_attn,
        gain_grad_mlp,
        grad_qkv,
        grad_out,
        grad_up,
        grad_down,
    )


def solution(mesh):
    in_specs = (
        P(None, ("dp", "mp"), None),
        P(),
        P(),
        P(),
        P(None, None, "mp"),
        P("mp", None),
        P(None, "mp"),
        P("mp", None),
        P(("dp", "mp"), None),
    )
    out_specs = (
        P(("dp", "mp"), None),
        P(None, ("dp", "mp"), None),
        P(),
        P(),
        P(),
        P(None, None, "mp"),
        P("mp", None),
        P(None, "mp"),
        P("mp", None),
    )
    return jax.shard_map(shards, mesh=mesh, in_specs=in_specs, out_specs=out_specs, check_vma=False)
```

time: 254 us -> 229 us (0.902)
  waiting for transfers between devices: 87.2 us -> 43.2 us
  Pallas kernels: 96.7 us -> 109 us
  starting transfers between devices: 49.5 us -> 56.4 us
  other arithmetic: 4.4 us -> 0.63 us
  local copies, waits for them, and re-layouts: 11.1 us -> 13.8 us
    ppermute x36, waiting for transfers between devices: 81.2 us -> 37.7 us  [bit_swap(): return lax.ppermute(rows, ('dp', 'mp'), pairs)]
    ppermute x36, starting transfers between devices: 47.2 us -> 54.4 us  [bit_swap(): return lax.ppermute(rows, ('dp', 'mp'), pairs)]
    pallas_call x37 -> x43, Pallas kernels: 76.4 us -> 82.4 us  [local_call(): pl.pallas_call(kernel, in_specs=[pl.BlockSpec(memory_space=pltpu.SMEM)] +...]
    unnamed x54 -> x50, local copies, waits for them, and re-layouts: 9.21 us -> 12.4 us
  transfers between devices with their start and end apart: 45 -> 45, of which waited for: 20 -> 16; matrix products, arithmetic and copies ran while one was open for 2% -> 1% of each run, Pallas kernels for 24% -> 31%
where the time goes in v3:
time: 229 us; the launch traced here: 224 us
  Pallas kernels  109 us (48%)
  starting transfers between devices  56.4 us (25%)
  waiting for transfers between devices  43.2 us (19%)
  local copies, waits for them, and re-layouts  13.8 us (6%)
    pallas_call x43, Pallas kernels, local_call(): pl.pallas_call(kernel, in_specs=[pl.BlockSpec(memory_space=pltpu.SMEM)] +...  82.4 us
    ppermute x36, starting transfers between devices, bit_swap(): return lax.ppermute(rows, ('dp', 'mp'), pairs)  54.4 us
    ppermute x36, waiting for transfers between devices, bit_swap(): return lax.ppermute(rows, ('dp', 'mp'), pairs)  37.7 us
    unnamed x50, local copies, waits for them, and re-layouts  12.4 us
    pallas_call x2, Pallas kernels, finish_mlp(): pl.pallas_call(functools.partial(finish_mlp_kernel, slot), grid_spec=pltp...  9.68 us
    pallas_call x1, Pallas kernels, unmix(): pl.pallas_call(unmix_kernel, in_specs=[pl.BlockSpec(memory_space=pltpu.SM...  6.74 us
    pallas_call x2, Pallas kernels, finish_attend(): pl.pallas_call(functools.partial(finish_attend_kernel, slot), grid_spec=p...  6.13 us
    ppermute x9, waiting for transfers between devices, mp_swap(): return lax.ppermute(rows, 'mp', [(0, 1), (1, 0)])  5.54 us
  transfers between devices with their start and end apart: 45, of which 16 were waited for; matrix products, arithmetic and copies ran while one was open for 1% of the time, Pallas kernels for 31%

profile of v3, /device:TPU:0, one launch (start us, length us, event | category | flops | bytes accessed | tf_op | source)
XLA Modules:
  0.0 224.4 jit_solution(877091198076288041)
XLA Ops:
  1.3 2.8 %copy-done = bf16[8,512,768]{2,1,0:T(8,128)(2,1)S(1)} copy-done((bf16[8,512,768]{2,1,0:T(8,128)(2,1)S(1)}, bf16[8,512,768]{2,1,0:T(8,128)(2,1)}, u32[]{:S(2)}) %copy-start) | copy-done | bytes 6291480
  4.8 3.7 %mix.1 = (f32[512,768]{1,0:T(8,128)S(1)}, bf16[512,768]{1,0:T(8,128)(2,1)S(1)}) custom-call(f32[8]{0:T(128)S(1)} %copy-done.18, f32[1,768]{1,0:T(1,128)S(1)} %broadcast_in_dim.8.gain_ref, bf16[8,512,768]{2,1,0:T(8,128)(2,1)S(1)} %copy-done), custom_call_target="tpu_custom_call" | custom-call | flops 1000 | bytes 1000 | tf_op jit(solution)/shard_map/mix/pallas_call | solution.py:108
  13.4 14.9 %attend.1 = (bf16[3,2,512,384]{3,2,1,0:T(8,128)(2,1)S(1)}, bf16[2,512,384]{2,1,0:T(8,128)(2,1)S(1)}, f32[3,2,2,1,512]{4,3,2,1,0:T(1,128)S(1)}, f32[512,768]{1,0:T(8,128)S(1)}, bf16[512,768]{1,0:T(8,128)(2,1)S(1)}) custom-call(s32[17]{0:T(128)S(1)} %stack.47.at_ref, bf16[512,768]{1,0:T(8,128)(2,1)S(1)} %get-tuple-element.79.own_ref.first_own_ref, ...), custom_call_target="tpu_custom_call" | custom-call | flops 1000 | bytes 1000 | tf_op jit(solution)/shard_map/attend/pallas_call | solution.py:202
  34.2 14.5 %mlp.1 = (bf16[8,96,768]{2,1,0:T(8,128)(2,1)S(1)}, bf16[8,96,768]{2,1,0:T(8,128)(2,1)}, bf16[8,96,768]{2,1,0:T(8,128)(2,1)S(1)}, bf16[8,96,768]{2,1,0:T(8,128)(2...) custom-call(s32[17]{0:T(128)S(1)} %stack.47.at_ref, ...), custom_call_target="tpu_custom_call" | custom-call | flops 1000 | bytes 1000 | tf_op jit(solution)/shard_map/mlp/pallas_call | solution.py:202
  50.1 2.7 %collective-permute-start.8 = (bf16[8,96,768]{2,1,0:T(8,128)(2,1)S(1)}, bf16[8,96,768]{2,1,0:T(8,128)(2,1)S(1)}, u32[]{:S(2)}, u32[]{:S(2)}) collective-permute-start(bf16[8,96,768]{2,1,0:T(8,128)(2,1)S(1)} %get-tuple-element.101), channel_id=1, source_target_pairs={{0,4},{1,9},{2,6},{3,11},{4,0},{5,13},{6,2},{7,15},{8,12},{9,1},{1... | collective-permute-start | bytes 3538952 | tf_op jit(solution)/shard_map/ppermute | solution.py:729
  55.8 2.1 collective-permute-start.7
  57.9 6.7 %attend_back.3 = (bf16[8,64,768]{2,1,0:T(8,128)(2,1)S(1)}, bf16[8,64,768]{2,1,0:T(8,128)(2,1)S(1)}, bf16[3,2,512,128]{3,2,1,0:T(8,128)(2,1)S(1)}) custom-call(s32[17]{0:T(128)S(1)} %stack.47.at_ref, bf16[3,2,512,384]{3,2,1,0:T(8,128)(2,1)S(1)} %get-tuple-element.85.qkv_ref, bf16[2,512,384]{2,1,0:T(8,128)(2,1)S(1)} %get-tuple-element.86.att_ref, ...), custom_call_target="tpu_custom_call" | custom-call | flops 1000 | bytes 1000 | tf_op jit(solution)/shard_map/attend_back/pallas_call | solution.py:202
  64.6 6.9 %attend_back.4 = (bf16[8,64,768]{2,1,0:T(8,128)(2,1)S(1)}, bf16[8,64,768]{2,1,0:T(8,128)(2,1)S(1)}, bf16[3,2,512,128]{3,2,1,0:T(8,128)(2,1)S(1)}) custom-call(s32[17]{0:T(128)S(1)} %stack.47.at_ref, bf16[3,2,512,384]{3,2,1,0:T(8,128)(2,1)S(1)} %get-tuple-element.85.qkv_ref, ...), custom_call_target="tpu_custom_call", output_to_operand_aliasing={{0}: (9, {}), {1}: (10, {})} | custom-call | flops 1000 | bytes 1000 | tf_op jit(solution)/shard_map/attend_back/pallas_call | solution.py:202
  71.5 2.2 collective-permute-start.6
  75.3 6.7 %attend_back.5 = (bf16[8,32,768]{2,1,0:T(8,128)(2,1)S(1)}, bf16[8,32,768]{2,1,0:T(8,128)(2,1)S(1)}, bf16[3,2,512,128]{3,2,1,0:T(8,128)(2,1)S(1)}) custom-call(s32[17]{0:T(128)S(1)} %stack.47.at_ref, bf16[3,2,512,384]{3,2,1,0:T(8,128)(2,1)S(1)} %get-tuple-element.85.qkv_ref, bf16[2,512,384]{2,1,0:T(8,128)(2,1)S(1)} %get-tuple-element.86.att_ref, ...), custom_call_target="tpu_custom_call" | custom-call | flops 1000 | bytes 1000 | tf_op jit(solution)/shard_map/attend_back/pallas_call | solution.py:202
  82.8 4.4 %first_back.1 = (f32[512,768]{1,0:T(8,128)S(1)}, bf16[512,768]{1,0:T(8,128)(2,1)S(1)}) custom-call(s32[17]{0:T(128)S(1)} %stack.47.at_ref, bf16[3,768,384]{2,1,0:T(8,128)(2,1)S(1)} %copy-done.4, bf16[3,2,512,128]{3,2,1,0:T(8,128)(2,1)S(1)} %get-tuple-element.94.refs_2_.refs_0_, bf16[3,2,512,128]{3,2,1,0:T(8,128)(2,1)S(1)} %get-tuple-element.99.refs_0_.refs_1_, ...), custom_call_target="tpu_custom_call" | custom-call | flops 1000 | bytes 1000 | tf_op jit(solution)/shard_map/first_back/pallas_call | solution.py:202
  96.2 6.7 %unmix.1 = (bf16[8,512,768]{2,1,0:T(8,128)(2,1)}, f32[16,768]{1,0:T(8,128)S(1)}) custom-call(f32[8]{0:T(128)S(1)} %copy-done.19, f32[1,768]{1,0:T(1,128)S(1)} %broadcast_in_dim.8.gain_ref, f32[512,768]{1,0:T(8,128)S(1)} %copy-done.6, f32[512,768]{1,0:T(8,128)S(1)} %copy-done.11, f32[512,768]{1,0:T(8,128)S(1)} %get-tuple-element.104.refs_0_.own_ref, ...), custom_call_target="tpu_custom_call" | custom-call | flops 1000 | bytes 1000 | tf_op jit(solution)/shard_map/unmix/pallas_call | solution.py:166
  113.0 2.6 %collective-permute-start.19 = (bf16[1,96,768]{2,1,0:T(8,128)(2,1)S(1)}, bf16[1,96,768]{2,1,0:T(8,128)(2,1)S(1)}, u32[]{:S(2)}, u32[]{:S(2)}) collective-permute-start(bf16[1,96,768]{2,1,0:T(8,128)(2,1)S(1)} %get-tuple-element.125), channel_id=1, source_target_pairs={{0,16},{1,17},{2,18},{3,19},{4,20},{5,21},{6,22},{7,23},{8,24},{9,... | collective-permute-start | bytes 442376 | tf_op jit(solution)/shard_map/ppermute | solution.py:729
  116.9 4.2 %collective-permute-done.20.came_ref = bf16[2,96,768]{2,1,0:T(8,128)(2,1)S(1)} collective-permute-done((bf16[2,96,768]{2,1,0:T(8,128)(2,1)S(1)}, bf16[2,96,768]{2,1,0:T(8,128)(2,1)S(1)}, u32[]{:S(2)}, u32[]{:S(2)}) %collective-permute-start.20) | collective-permute-done | bytes 294944 | tf_op jit(solution)/shard_map/ppermute | solution.py:729
  123.8 3.3 %collective-permute-start.30 = (bf16[1,96,768]{2,1,0:T(8,128)(2,1)S(1)}, bf16[1,96,768]{2,1,0:T(8,128)(2,1)S(1)}, u32[]{:S(2)}, u32[]{:S(2)}) collective-permute-start(bf16[1,96,768]{2,1,0:T(8,128)(2,1)S(1)} %add.6.refs_0_.mine_ref), channel_id=1, source_target_pairs={{0,16},{1,17},{2,18},{3,19},{4,20},{5,21},{6,22},{7,23},{8,24},{9,... | collective-permute-start | bytes 442376 | tf_op jit(solution)/shard_map/ppermute | solution.py:729
  129.6 2.9 %collective-permute-start.26 = (bf16[1,32,768]{2,1,0:T(8,128)(2,1)S(1)}, bf16[1,32,768]{2,1,0:T(8,128)(2,1)S(1)}, u32[]{:S(2)}, u32[]{:S(2)}) collective-permute-start(bf16[1,32,768]{2,1,0:T(8,128)(2,1)S(1)} %get-tuple-element.134), channel_id=1, source_target_pairs={{0,16},{1,17},{2,18},{3,19},{4,20},{5,21},{6,22},{7,23},{8,24},{9,... | collective-permute-start | bytes 147464 | tf_op jit(solution)/shard_map/ppermute | solution.py:729
  132.5 3.1 %block.1 = (f32[512,768]{1,0:T(8,128)S(1)}, bf16[512,768]{1,0:T(8,128)(2,1)S(1)}) custom-call(s32[17]{0:T(128)S(1)} %stack.47.at_ref, bf16[2,512,1536]{2,1,0:T(8,128)(2,1)S(1)} %get-tuple-element.84.refs_0_.rows_ref, bf16[1536,768]{1,0:T(8,128)(2,1)S(1)} %copy-done.1, bf16[1,64,768]{2,1,0:T(8,128)(2,1)S(1)} %get-tuple-element.129.refs_0_.kept_ref), custom_call_target="tpu_custom_call" | custom-call | flops 1000 | bytes 1000 | tf_op jit(solution)/shard_map/block/pallas_call | solution.py:202
  137.8 4.2 %collective-permute-done.26.came_ref = bf16[1,32,768]{2,1,0:T(8,128)(2,1)S(1)} collective-permute-done((bf16[1,32,768]{2,1,0:T(8,128)(2,1)S(1)}, bf16[1,32,768]{2,1,0:T(8,128)(2,1)S(1)}, u32[]{:S(2)}, u32[]{:S(2)}) %collective-permute-start.26) | collective-permute-done | bytes 49184 | tf_op jit(solution)/shard_map/ppermute | solution.py:729
  143.3 3.0 %collective-permute-start.28 = (bf16[1,96,768]{2,1,0:T(8,128)(2,1)S(1)}, bf16[1,96,768]{2,1,0:T(8,128)(2,1)S(1)}, u32[]{:S(2)}, u32[]{:S(2)}) collective-permute-start(bf16[1,96,768]{2,1,0:T(8,128)(2,1)S(1)} %add.8.refs_0_.mine_ref), channel_id=1, source_target_pairs={{0,16},{1,17},{2,18},{3,19},{4,20},{5,21},{6,22},{7,23},{8,24},{9,... | collective-permute-start | bytes 442376 | tf_op jit(solution)/shard_map/ppermute | solution.py:729
  151.4 3.7 %collective-permute-done.31.came_ref = bf16[2,32,768]{2,1,0:T(8,128)(2,1)S(1)} collective-permute-done((bf16[2,32,768]{2,1,0:T(8,128)(2,1)S(1)}, bf16[2,32,768]{2,1,0:T(8,128)(2,1)S(1)}, u32[]{:S(2)}, u32[]{:S(2)}) %collective-permute-start.31) | collective-permute-done | bytes 98336 | tf_op jit(solution)/shard_map/ppermute | solution.py:729
  156.2 2.2 collective-permute-start.33
  158.4 3.4 %collective-permute-start.34 = (bf16[1,64,768]{2,1,0:T(8,128)(2,1)S(1)}, bf16[1,64,768]{2,1,0:T(8,128)(2,1)S(1)}, u32[]{:S(2)}, u32[]{:S(2)}) collective-permute-start(bf16[1,64,768]{2,1,0:T(8,128)(2,1)S(1)} %add.9.refs_0_.mine_ref), channel_id=1, source_target_pairs={{0,16},{1,17},{2,18},{3,19},{4,20},{5,21},{6,22},{7,23},{8,24},{9,... | collective-permute-start | bytes 294920 | tf_op jit(solution)/shard_map/ppermute | solution.py:729
  164.0 6.0 %collective-permute-done.27.came_ref = f32[16,768]{1,0:T(8,128)S(1)} collective-permute-done((f32[16,768]{1,0:T(8,128)S(1)}, f32[16,768]{1,0:T(8,128)S(1)}, u32[]{:S(2)}, u32[]{:S(2)}) %collective-permute-start.27) | collective-permute-done | bytes 49184 | tf_op jit(solution)/shard_map/ppermute | solution.py:729
  171.1 2.1 collective-permute-start.37
  178.5 3.2 %collective-permute-start.32 = (f32[16,768]{1,0:T(8,128)S(1)}, f32[16,768]{1,0:T(8,128)S(1)}, u32[]{:S(2)}, u32[]{:S(2)}) collective-permute-start(f32[16,768]{1,0:T(8,128)S(1)} %small.8.refs_0_.mine_ref), channel_id=1, source_target_pairs={{0,16},{1,17},{2,18},{3,19},{4,20},{5,21},{6,22},{7,23},{8,24},{9,... | collective-permute-start | bytes 147464 | tf_op jit(solution)/shard_map/ppermute | solution.py:729
  183.6 4.9 %collective-permute-done.35.came_ref = bf16[4,96,768]{2,1,0:T(8,128)(2,1)S(1)} collective-permute-done((bf16[4,96,768]{2,1,0:T(8,128)(2,1)S(1)}, bf16[4,96,768]{2,1,0:T(8,128)(2,1)S(1)}, u32[]{:S(2)}, u32[]{:S(2)}) %collective-permute-start.35) | collective-permute-done | bytes 589856 | tf_op jit(solution)/shard_map/ppermute | solution.py:729
  195.3 2.5 %finish_attend.2 = (f32[3,768,384]{2,1,0:T(8,128)}, f32[384,768]{1,0:T(8,128)}, f32[8,128]{1,0:T(8,128)S(1)}) custom-call(s32[17]{0:T(128)S(1)} %stack.47.at_ref, bf16[8,32,768]{2,1,0:T(8,128)(2,1)S(1)} %join.18.refs_0_.mine_ref, bf16[8,32,768]{2,1,0:T(8,128)(2,1)S(1)} %collective-permute-done.40.came_ref, bf16[8,96,768]{2,1,0:T(8,128)(2,1)S(1)} %join.22.refs_0_.mine_ref), custom_call_target="tpu_custom_call" | custom-call | flops 1000 | bytes 1000 | tf_op jit(solution)/shard_map/finish_attend/pallas_call | solution.py:689
  201.7 4.7 %collective-permute-done.43.came_ref = bf16[8,96,768]{2,1,0:T(8,128)(2,1)S(1)} collective-permute-done((bf16[8,96,768]{2,1,0:T(8,128)(2,1)S(1)}, bf16[8,96,768]{2,1,0:T(8,128)(2,1)S(1)}, u32[]{:S(2)}, u32[]{:S(2)}) %collective-permute-start.43) | collective-permute-done | bytes 1179680 | tf_op jit(solution)/shard_map/ppermute | solution.py:729
  206.4 4.8 %finish_mlp.2 = (f32[768,1536]{1,0:T(8,128)}, f32[1536,768]{1,0:T(8,128)}, f32[8,128]{1,0:T(8,128)S(1)}) custom-call(s32[17]{0:T(128)S(1)} %stack.47.at_ref, bf16[8,96,768]{2,1,0:T(8,128)(2,1)S(1)} %join.21.refs_0_.mine_ref, bf16[8,96,768]{2,1,0:T(8,128)(2,1)S(1)} %collective-permute-done.43.came_ref, bf16[8,64,768]{2,1,0:T(8,128)(2,1)S(1)} %join.23.refs_0_.mine_ref), custom_call_target="tpu_custom_call" | custom-call | flops 1000 | bytes 1000 | tf_op jit(solution)/shard_map/finish_mlp/pallas_call | solution.py:650
  211.3 3.6 %collective-permute-done.42.came_ref = bf16[8,64,768]{2,1,0:T(8,128)(2,1)S(1)} collective-permute-done((bf16[8,64,768]{2,1,0:T(8,128)(2,1)S(1)}, bf16[8,64,768]{2,1,0:T(8,128)(2,1)S(1)}, u32[]{:S(2)}, u32[]{:S(2)}) %collective-permute-start.42) | collective-permute-done | bytes 786464 | tf_op jit(solution)/shard_map/ppermute | solution.py:729
  214.9 3.6 %finish_attend.3 = (f32[3,768,384]{2,1,0:T(8,128)}, f32[384,768]{1,0:T(8,128)}, f32[8,128]{1,0:T(8,128)S(1)}) custom-call(s32[17]{0:T(128)S(1)} %stack.47.at_ref, bf16[8,64,768]{2,1,0:T(8,128)(2,1)S(1)} %join.23.refs_0_.mine_ref, bf16[8,64,768]{2,1,0:T(8,128)(2,1)S(1)} %collective-permute-done.42.came_ref, ...), custom_call_target="tpu_custom_call", output_to_operand_aliasing={{0}: (3, {}), {1}: (4, {})} | custom-call | flops 1000 | bytes 1000 | tf_op jit(solution)/shard_map/finish_attend/pallas_call | solution.py:689
  219.1 4.8 %finish_mlp.3 = (f32[768,1536]{1,0:T(8,128)}, f32[1536,768]{1,0:T(8,128)}, f32[8,128]{1,0:T(8,128)}) custom-call(s32[17]{0:T(128)S(1)} %stack.47.at_ref, bf16[8,96,768]{2,1,0:T(8,128)(2,1)S(1)} %join.22.refs_0_.mine_ref, bf16[8,96,768]{2,1,0:T(8,128)(2,1)S(1)} %collective-permute-done.44.came_ref, ...), custom_call_target="tpu_custom_call", output_to_operand_aliasing={{0}: (3, {}), {1}: (4, {})} | custom-call | flops 1000 | bytes 1000 | tf_op jit(solution)/shard_map/finish_mlp/pallas_call | solution.py:650
  (163 shorter events, 75.7 us)
Async XLA Ops:
  50.1 23.6 %collective-permute-start.8 = (bf16[8,96,768]{2,1,0:T(8,128)(2,1)S(1)}, bf16[8,96,768]{2,1,0:T(8,128)(2,1)S(1)}, u32[]{:S(2)}, u32[]{:S(2)}) collective-permute-start(bf16[8,96,768]{2,1,0:T(8,128)(2,1)S(1)} %get-tuple-element.101), channel_id=1, source_target_pairs={{0,4},{1,9},{2,6},{3,11},{4,0},{5,13},{6,2},{7,15},{8,12},{9,1},{1... | collective-permute-start | bytes 3538952 | tf_op jit(solution)/shard_map/ppermute | solution.py:729
  55.8 31.5 %collective-permute-start.7 = (bf16[8,96,768]{2,1,0:T(8,128)(2,1)}, bf16[8,96,768]{2,1,0:T(8,128)(2,1)S(1)}, u32[]{:S(2)}, u32[]{:S(2)}) collective-permute-start(bf16[8,96,768]{2,1,0:T(8,128)(2,1)} %get-tuple-element.98), channel_id=1, source_target_pairs={{0,2},{1,9},{2,0},{3,11},{4,6},{5,13},{6,4},{7,15},{8,10},{9,1},{1... | collective-permute-start | bytes 3538952 | tf_op jit(solution)/shard_map/ppermute | solution.py:729
  71.5 22.6 %collective-permute-start.6 = (bf16[8,64,768]{2,1,0:T(8,128)(2,1)S(1)}, bf16[8,64,768]{2,1,0:T(8,128)(2,1)S(1)}, u32[]{:S(2)}, u32[]{:S(2)}) collective-permute-start(bf16[8,64,768]{2,1,0:T(8,128)(2,1)S(1)} %get-tuple-element.96), channel_id=1, source_target_pairs={{0,2},{1,5},{2,0},{3,7},{4,6},{5,1},{6,4},{7,3},{8,10},{9,13},{10,... | collective-permute-start | bytes 2359304 | tf_op jit(solution)/shard_map/ppermute | solution.py:729
  75.3 19.6 %collective-permute-start.12 = (bf16[4,96,768]{2,1,0:T(8,128)(2,1)}, bf16[4,96,768]{2,1,0:T(8,128)(2,1)S(1)}, u32[]{:S(2)}, u32[]{:S(2)}) collective-permute-start(bf16[4,96,768]{2,1,0:T(8,128)(2,1)} %get-tuple-element.112), channel_id=1, source_target_pairs={{0,2},{1,5},{2,0},{3,7},{4,6},{5,1},{6,4},{7,3},{8,10},{9,13},{10,... | collective-permute-start | bytes 1769480 | tf_op jit(solution)/shard_map/ppermute | solution.py:729
  87.2 9.0 %collective-permute-start.11 = (bf16[512,768]{1,0:T(8,128)(2,1)S(1)}, bf16[512,768]{1,0:T(8,128)(2,1)S(1)}, u32[]{:S(2)}, u32[]{:S(2)}) collective-permute-start(bf16[512,768]{1,0:T(8,128)(2,1)S(1)} %get-tuple-element.111), channel_id=1, source_target_pairs={{0,1},{1,0},{2,3},{3,2},{4,5},{5,4},{6,7},{7,6},{8,9},{9,8},{10,11... | collective-permute-start | bytes 2359304 | tf_op jit(solution)/shard_map/ppermute | solution.py:715
  90.4 17.1 %collective-permute-start.14 = (bf16[4,96,768]{2,1,0:T(8,128)(2,1)S(1)}, bf16[4,96,768]{2,1,0:T(8,128)(2,1)S(1)}, u32[]{:S(2)}, u32[]{:S(2)}) collective-permute-start(bf16[4,96,768]{2,1,0:T(8,128)(2,1)S(1)} %get-tuple-element.117), channel_id=1, source_target_pairs={{0,4},{1,3},{2,6},{3,1},{4,0},{5,7},{6,2},{7,5},{8,12},{9,11},{10,... | collective-permute-start | bytes 1769480 | tf_op jit(solution)/shard_map/ppermute | solution.py:729
  92.5 11.2 %collective-permute-start.10 = (bf16[8,32,768]{2,1,0:T(8,128)(2,1)S(1)}, bf16[8,32,768]{2,1,0:T(8,128)(2,1)S(1)}, u32[]{:S(2)}, u32[]{:S(2)}) collective-permute-start(bf16[8,32,768]{2,1,0:T(8,128)(2,1)S(1)} %copy-done.21), channel_id=1, source_target_pairs={{0,8},{1,9},{2,10},{3,11},{4,12},{5,13},{6,14},{7,15},{8,0},{9,1},... | collective-permute-start | bytes 1179656 | tf_op jit(solution)/shard_map/ppermute | solution.py:729
  95.5 11.3 %collective-permute-start.15 = (bf16[2,96,768]{2,1,0:T(8,128)(2,1)S(1)}, bf16[2,96,768]{2,1,0:T(8,128)(2,1)S(1)}, u32[]{:S(2)}, u32[]{:S(2)}) collective-permute-start(bf16[2,96,768]{2,1,0:T(8,128)(2,1)S(1)} %get-tuple-element.118), channel_id=1, source_target_pairs={{0,8},{1,3},{2,10},{3,1},{4,12},{5,7},{6,14},{7,5},{8,0},{9,11},{1... | collective-permute-start | bytes 884744 | tf_op jit(solution)/shard_map/ppermute | solution.py:729
  96.0 14.6 %collective-permute-start.9 = (bf16[4,64,768]{2,1,0:T(8,128)(2,1)S(1)}, bf16[4,64,768]{2,1,0:T(8,128)(2,1)S(1)}, u32[]{:S(2)}, u32[]{:S(2)}) collective-permute-start(bf16[4,64,768]{2,1,0:T(8,128)(2,1)S(1)} %get-tuple-element.107), channel_id=1, source_target_pairs={{0,4},{1,3},{2,6},{3,1},{4,0},{5,7},{6,2},{7,5},{8,12},{9,11},{10,... | collective-permute-start | bytes 1179656 | tf_op jit(solution)/shard_map/ppermute | solution.py:729
  108.2 12.9 %collective-permute-start.20 = (bf16[2,96,768]{2,1,0:T(8,128)(2,1)S(1)}, bf16[2,96,768]{2,1,0:T(8,128)(2,1)S(1)}, u32[]{:S(2)}, u32[]{:S(2)}) collective-permute-start(bf16[2,96,768]{2,1,0:T(8,128)(2,1)S(1)} %get-tuple-element.126), channel_id=1, source_target_pairs={{0,8},{1,5},{2,10},{3,7},{4,12},{5,1},{6,14},{7,3},{8,0},{9,13},{1... | collective-permute-start | bytes 884744 | tf_op jit(solution)/shard_map/ppermute | solution.py:729
  111.3 17.6 %collective-permute-start.16 = (bf16[2,64,768]{2,1,0:T(8,128)(2,1)S(1)}, bf16[2,64,768]{2,1,0:T(8,128)(2,1)S(1)}, u32[]{:S(2)}, u32[]{:S(2)}) collective-permute-start(bf16[2,64,768]{2,1,0:T(8,128)(2,1)S(1)} %get-tuple-element.123), channel_id=1, source_target_pairs={{0,8},{1,9},{2,10},{3,11},{4,12},{5,13},{6,14},{7,15},{8,0},{9,1},... | collective-permute-start | bytes 589832 | tf_op jit(solution)/shard_map/ppermute | solution.py:729
  113.0 10.2 %collective-permute-start.19 = (bf16[1,96,768]{2,1,0:T(8,128)(2,1)S(1)}, bf16[1,96,768]{2,1,0:T(8,128)(2,1)S(1)}, u32[]{:S(2)}, u32[]{:S(2)}) collective-permute-start(bf16[1,96,768]{2,1,0:T(8,128)(2,1)S(1)} %get-tuple-element.125), channel_id=1, source_target_pairs={{0,16},{1,17},{2,18},{3,19},{4,20},{5,21},{6,22},{7,23},{8,24},{9,... | collective-permute-start | bytes 442376 | tf_op jit(solution)/shard_map/ppermute | solution.py:729
  115.6 12.7 %collective-permute-start.17 = (bf16[2,32,768]{2,1,0:T(8,128)(2,1)S(1)}, bf16[2,32,768]{2,1,0:T(8,128)(2,1)S(1)}, u32[]{:S(2)}, u32[]{:S(2)}) collective-permute-start(bf16[2,32,768]{2,1,0:T(8,128)(2,1)S(1)} %get-tuple-element.124), channel_id=1, source_target_pairs={{0,4},{1,3},{2,6},{3,1},{4,0},{5,7},{6,2},{7,5},{8,12},{9,11},{10,... | collective-permute-start | bytes 294920 | tf_op jit(solution)/shard_map/ppermute | solution.py:729
  121.7 21.0 %collective-permute-start.25 = (bf16[1,96,768]{2,1,0:T(8,128)(2,1)S(1)}, bf16[1,96,768]{2,1,0:T(8,128)(2,1)S(1)}, u32[]{:S(2)}, u32[]{:S(2)}) collective-permute-start(bf16[1,96,768]{2,1,0:T(8,128)(2,1)S(1)} %get-tuple-element.133), channel_id=1, source_target_pairs={{0,16},{1,17},{2,18},{3,19},{4,20},{5,21},{6,22},{7,23},{8,24},{9,... | collective-permute-start | bytes 442376 | tf_op jit(solution)/shard_map/ppermute | solution.py:729
  123.8 23.6 %collective-permute-start.30 = (bf16[1,96,768]{2,1,0:T(8,128)(2,1)S(1)}, bf16[1,96,768]{2,1,0:T(8,128)(2,1)S(1)}, u32[]{:S(2)}, u32[]{:S(2)}) collective-permute-start(bf16[1,96,768]{2,1,0:T(8,128)(2,1)S(1)} %add.6.refs_0_.mine_ref), channel_id=1, source_target_pairs={{0,16},{1,17},{2,18},{3,19},{4,20},{5,21},{6,22},{7,23},{8,24},{9,... | collective-permute-start | bytes 442376 | tf_op jit(solution)/shard_map/ppermute | solution.py:729
  129.5 16.7 %collective-permute-start.24 = (bf16[1,64,768]{2,1,0:T(8,128)(2,1)S(1)}, bf16[1,64,768]{2,1,0:T(8,128)(2,1)S(1)}, u32[]{:S(2)}, u32[]{:S(2)}) collective-permute-start(bf16[1,64,768]{2,1,0:T(8,128)(2,1)S(1)} %get-tuple-element.132), channel_id=1, source_target_pairs={{0,16},{1,17},{2,18},{3,19},{4,20},{5,21},{6,22},{7,23},{8,24},{9,... | collective-permute-start | bytes 294920 | tf_op jit(solution)/shard_map/ppermute | solution.py:729
  129.6 12.4 %collective-permute-start.26 = (bf16[1,32,768]{2,1,0:T(8,128)(2,1)S(1)}, bf16[1,32,768]{2,1,0:T(8,128)(2,1)S(1)}, u32[]{:S(2)}, u32[]{:S(2)}) collective-permute-start(bf16[1,32,768]{2,1,0:T(8,128)(2,1)S(1)} %get-tuple-element.134), channel_id=1, source_target_pairs={{0,16},{1,17},{2,18},{3,19},{4,20},{5,21},{6,22},{7,23},{8,24},{9,... | collective-permute-start | bytes 147464 | tf_op jit(solution)/shard_map/ppermute | solution.py:729
  136.2 10.6 %collective-permute-start.23 = (f32[16,768]{1,0:T(8,128)S(1)}, f32[16,768]{1,0:T(8,128)S(1)}, u32[]{:S(2)}, u32[]{:S(2)}) collective-permute-start(f32[16,768]{1,0:T(8,128)S(1)} %small.6.refs_0_.mine_ref), channel_id=1, source_target_pairs={{0,4},{1,5},{2,6},{3,7},{4,0},{5,1},{6,2},{7,3},{8,12},{9,13},{10,... | collective-permute-start | bytes 147464 | tf_op jit(solution)/shard_map/ppermute | solution.py:729
  143.3 12.4 %collective-permute-start.28 = (bf16[1,96,768]{2,1,0:T(8,128)(2,1)S(1)}, bf16[1,96,768]{2,1,0:T(8,128)(2,1)S(1)}, u32[]{:S(2)}, u32[]{:S(2)}) collective-permute-start(bf16[1,96,768]{2,1,0:T(8,128)(2,1)S(1)} %add.8.refs_0_.mine_ref), channel_id=1, source_target_pairs={{0,16},{1,17},{2,18},{3,19},{4,20},{5,21},{6,22},{7,23},{8,24},{9,... | collective-permute-start | bytes 442376 | tf_op jit(solution)/shard_map/ppermute | solution.py:729
  156.2 17.0 %collective-permute-start.33 = (bf16[2,96,768]{2,1,0:T(8,128)(2,1)S(1)}, bf16[2,96,768]{2,1,0:T(8,128)(2,1)S(1)}, u32[]{:S(2)}, u32[]{:S(2)}) collective-permute-start(bf16[2,96,768]{2,1,0:T(8,128)(2,1)S(1)} %join.15.refs_0_.mine_ref), channel_id=1, source_target_pairs={{0,8},{1,5},{2,10},{3,7},{4,12},{5,1},{6,14},{7,3},{8,0},{9,13},{1... | collective-permute-start | bytes 884744 | tf_op jit(solution)/shard_map/ppermute | solution.py:729
  158.4 12.1 %collective-permute-start.34 = (bf16[1,64,768]{2,1,0:T(8,128)(2,1)S(1)}, bf16[1,64,768]{2,1,0:T(8,128)(2,1)S(1)}, u32[]{:S(2)}, u32[]{:S(2)}) collective-permute-start(bf16[1,64,768]{2,1,0:T(8,128)(2,1)S(1)} %add.9.refs_0_.mine_ref), channel_id=1, source_target_pairs={{0,16},{1,17},{2,18},{3,19},{4,20},{5,21},{6,22},{7,23},{8,24},{9,... | collective-permute-start | bytes 294920 | tf_op jit(solution)/shard_map/ppermute | solution.py:729
  161.8 15.6 %collective-permute-start.36 = (bf16[2,96,768]{2,1,0:T(8,128)(2,1)S(1)}, bf16[2,96,768]{2,1,0:T(8,128)(2,1)S(1)}, u32[]{:S(2)}, u32[]{:S(2)}) collective-permute-start(bf16[2,96,768]{2,1,0:T(8,128)(2,1)S(1)} %join.12.refs_0_.mine_ref), channel_id=1, source_target_pairs={{0,8},{1,3},{2,10},{3,1},{4,12},{5,7},{6,14},{7,5},{8,0},{9,11},{1... | collective-permute-start | bytes 884744 | tf_op jit(solution)/shard_map/ppermute | solution.py:729
  163.8 10.9 %collective-permute-start.38 = (bf16[4,32,768]{2,1,0:T(8,128)(2,1)S(1)}, bf16[4,32,768]{2,1,0:T(8,128)(2,1)S(1)}, u32[]{:S(2)}, u32[]{:S(2)}) collective-permute-start(bf16[4,32,768]{2,1,0:T(8,128)(2,1)S(1)} %join.14.refs_0_.mine_ref), channel_id=1, source_target_pairs={{0,2},{1,5},{2,0},{3,7},{4,6},{5,1},{6,4},{7,3},{8,10},{9,13},{10,... | collective-permute-start | bytes 589832 | tf_op jit(solution)/shard_map/ppermute | solution.py:729
  173.2 18.1 %collective-permute-start.21 = (bf16[512,768]{1,0:T(8,128)(2,1)S(1)}, bf16[512,768]{1,0:T(8,128)(2,1)S(1)}, u32[]{:S(2)}, u32[]{:S(2)}) collective-permute-start(bf16[512,768]{1,0:T(8,128)(2,1)S(1)} %get-tuple-element.131), channel_id=1, source_target_pairs={{0,1},{1,0},{2,3},{3,2},{4,5},{5,4},{6,7},{7,6},{8,9},{9,8},{10,11... | collective-permute-start | bytes 2359304 | tf_op jit(solution)/shard_map/ppermute | solution.py:715
  173.8 14.8 %collective-permute-start.35 = (bf16[4,96,768]{2,1,0:T(8,128)(2,1)S(1)}, bf16[4,96,768]{2,1,0:T(8,128)(2,1)S(1)}, u32[]{:S(2)}, u32[]{:S(2)}) collective-permute-start(bf16[4,96,768]{2,1,0:T(8,128)(2,1)S(1)} %join.17.refs_0_.mine_ref), channel_id=1, source_target_pairs={{0,4},{1,3},{2,6},{3,1},{4,0},{5,7},{6,2},{7,5},{8,12},{9,11},{10,... | collective-permute-start | bytes 1769480 | tf_op jit(solution)/shard_map/ppermute | solution.py:729
  178.0 14.9 %collective-permute-start.41 = (bf16[4,96,768]{2,1,0:T(8,128)(2,1)S(1)}, bf16[4,96,768]{2,1,0:T(8,128)(2,1)S(1)}, u32[]{:S(2)}, u32[]{:S(2)}) collective-permute-start(bf16[4,96,768]{2,1,0:T(8,128)(2,1)S(1)} %join.20.refs_0_.mine_ref), channel_id=1, source_target_pairs={{0,2},{1,5},{2,0},{3,7},{4,6},{5,1},{6,4},{7,3},{8,10},{9,13},{10,... | collective-permute-start | bytes 1769480 | tf_op jit(solution)/shard_map/ppermute | solution.py:729
  178.5 10.8 %collective-permute-start.32 = (f32[16,768]{1,0:T(8,128)S(1)}, f32[16,768]{1,0:T(8,128)S(1)}, u32[]{:S(2)}, u32[]{:S(2)}) collective-permute-start(f32[16,768]{1,0:T(8,128)S(1)} %small.8.refs_0_.mine_ref), channel_id=1, source_target_pairs={{0,16},{1,17},{2,18},{3,19},{4,20},{5,21},{6,22},{7,23},{8,24},{9,... | collective-permute-start | bytes 147464 | tf_op jit(solution)/shard_map/ppermute | solution.py:729
  181.6 13.7 %collective-permute-start.40 = (bf16[8,32,768]{2,1,0:T(8,128)(2,1)S(1)}, bf16[8,32,768]{2,1,0:T(8,128)(2,1)S(1)}, u32[]{:S(2)}, u32[]{:S(2)}) collective-permute-start(bf16[8,32,768]{2,1,0:T(8,128)(2,1)S(1)} %join.18.refs_0_.mine_ref), channel_id=1, source_target_pairs={{0,8},{1,9},{2,10},{3,11},{4,12},{5,13},{6,14},{7,15},{8,0},{9,1},... | collective-permute-start | bytes 1179656 | tf_op jit(solution)/shard_map/ppermute | solution.py:729
  188.6 9.2 %collective-permute-start.39 = (bf16[4,64,768]{2,1,0:T(8,128)(2,1)S(1)}, bf16[4,64,768]{2,1,0:T(8,128)(2,1)S(1)}, u32[]{:S(2)}, u32[]{:S(2)}) collective-permute-start(bf16[4,64,768]{2,1,0:T(8,128)(2,1)S(1)} %join.19.refs_0_.mine_ref), channel_id=1, source_target_pairs={{0,4},{1,3},{2,6},{3,1},{4,0},{5,7},{6,2},{7,5},{8,12},{9,11},{10,... | collective-permute-start | bytes 1179656 | tf_op jit(solution)/shard_map/ppermute | solution.py:729
  189.2 17.2 %collective-permute-start.43 = (bf16[8,96,768]{2,1,0:T(8,128)(2,1)S(1)}, bf16[8,96,768]{2,1,0:T(8,128)(2,1)S(1)}, u32[]{:S(2)}, u32[]{:S(2)}) collective-permute-start(bf16[8,96,768]{2,1,0:T(8,128)(2,1)S(1)} %join.21.refs_0_.mine_ref), channel_id=1, source_target_pairs={{0,2},{1,9},{2,0},{3,11},{4,6},{5,13},{6,4},{7,15},{8,10},{9,1},{1... | collective-permute-start | bytes 3538952 | tf_op jit(solution)/shard_map/ppermute | solution.py:729
  194.6 24.5 %collective-permute-start.44 = (bf16[8,96,768]{2,1,0:T(8,128)(2,1)S(1)}, bf16[8,96,768]{2,1,0:T(8,128)(2,1)S(1)}, u32[]{:S(2)}, u32[]{:S(2)}) collective-permute-start(bf16[8,96,768]{2,1,0:T(8,128)(2,1)S(1)} %join.22.refs_0_.mine_ref), channel_id=1, source_target_pairs={{0,4},{1,9},{2,6},{3,11},{4,0},{5,13},{6,2},{7,15},{8,12},{9,1},{1... | collective-permute-start | bytes 3538952 | tf_op jit(solution)/shard_map/ppermute | solution.py:729
  198.4 16.4 %collective-permute-start.42 = (bf16[8,64,768]{2,1,0:T(8,128)(2,1)S(1)}, bf16[8,64,768]{2,1,0:T(8,128)(2,1)S(1)}, u32[]{:S(2)}, u32[]{:S(2)}) collective-permute-start(bf16[8,64,768]{2,1,0:T(8,128)(2,1)S(1)} %join.23.refs_0_.mine_ref), channel_id=1, source_target_pairs={{0,2},{1,5},{2,0},{3,7},{4,6},{5,1},{6,4},{7,3},{8,10},{9,13},{10,... | collective-permute-start | bytes 2359304 | tf_op jit(solution)/shard_map/ppermute | solution.py:729
  (38 other events, 216.1 us)

commit v4 on v3

--- a/solution.py
+++ b/solution.py
@@ -15,21 +15,21 @@
 NEG = -1e30
 TILE = 256
 ROW_BLOCK = 64
-VMEM_BYTES = 32 * 2**20
-SPLITS = 4
+MIX_BLOCK = 128
+SMALL_ROWS = 32
+SPLITS = 3
 PAIR = 2 * HEAD_DIM
 CHUNK = 512
 ORDER = (
-    "nb", "ab0", "ab1", "Mb", "ab2", "fb", "Ma", "Aa", "Mb", "um", "Ab", "Mb", "Ma", "Ab",
-    "Aa", "Ma", "Mb", "sm", "Ab", "Aa", "blk", "sm", "Ab", "Ma", "Aa", "sm", "Mb", "Ab", "Ab",
-    "Ma", "sm", "Aa", "Ma", "Ab", "Aa", "Mb", "Ma", "sm", "bo", "Mb", "fAb", "Aa", "fMa",
-    "fAa", "fMb",
+    "nb", "ab0", "ab1", "Mb", "ab2", "fb", "Ma", "Aa", "blk", "Mb", "Ma", "Mb", "Ma", "Aa",
+    "Ab", "um", "Mb", "Aa", "Ab", "Ab", "Ma", "Aa", "Mb", "Ma", "Aa", "Ab", "Ab", "Mb", "Ab",
+    "Aa", "Ma", "fMb", "fAb", "fAa", "fMa",
 )
 KINDS = (
-    ((0, 1, 2, 3), (2, 0, 1, 3)),
-    ((1, 0, 2, 3), (2, 1, 0, 3)),
-    ((0, 1, 2, 3), (1, 0, 2, 3)),
-    ((2, 0, 1, 3), (2, 1, 0, 3)),
+    ((2, 0, 1), (1, 2, 0)),
+    ((2, 0, 1), (0, 1, 2)),
+    ((0, 1, 2), (1, 2, 0)),
+    ((0, 1, 2), (2, 0, 1)),
 )
 KIND = {"Ma": 0, "Mb": 1, "Aa": 2, "Ab": 3}
 EARLY = 3
@@ -47,8 +47,8 @@
     return pl.CostEstimate(flops=flops, bytes_accessed=moved, transcendentals=exps)
 
 
-def params():
-    return pltpu.CompilerParams(vmem_limit_bytes=VMEM_BYTES)
+def params(mebibytes=8):
+    return pltpu.CompilerParams(vmem_limit_bytes=mebibytes * 2**20)
 
 
 def normalize(inputs):
@@ -86,56 +86,52 @@
     return copies
 
 
-def mix_kernel(weights_ref, gain_ref, history_ref, mixed_ref, first_ref, held_ref, sems):
-    copies = layer_copies(history_ref, held_ref, sems)
-    for copy in copies:
-        copy.start()
-    for index, copy in enumerate(copies):
-        rows = pl.ds(index * ROW_BLOCK, ROW_BLOCK)
-        copy.wait()
-        mixed = weights_ref[0] * held_ref[index, 0].astype(jnp.float32)
-        for layer in range(1, held_ref.shape[1]):
-            mixed = mixed + weights_ref[layer] * held_ref[index, layer].astype(jnp.float32)
-        mixed_ref[rows, :] = mixed
-        normed, _ = normalize(mixed)
-        first_ref[rows, :] = (normed * gain_ref[...]).astype(jnp.bfloat16)
+def mix_kernel(weights_ref, gain_ref, history_ref, mixed_ref, first_ref):
+    mixed = weights_ref[0] * history_ref[0].astype(jnp.float32)
+    for layer in range(1, history_ref.shape[0]):
+        mixed = mixed + weights_ref[layer] * history_ref[layer].astype(jnp.float32)
+    mixed_ref[...] = mixed
+    normed, _ = normalize(mixed)
+    first_ref[...] = (normed * gain_ref[...]).astype(jnp.bfloat16)
 
 
 def mix(weights, history, gain):
     layers, rows, width = history.shape
-    in_vmem = pl.BlockSpec(memory_space=pltpu.VMEM)
-    blocks = rows // ROW_BLOCK
+    row_spec = pl.BlockSpec((MIX_BLOCK, width), lambda i: (i, 0))
     return pl.pallas_call(
         mix_kernel,
+        grid=(rows // MIX_BLOCK,),
         in_specs=[
             pl.BlockSpec(memory_space=pltpu.SMEM),
-            in_vmem,
-            pl.BlockSpec(memory_space=pltpu.HBM),
+            pl.BlockSpec((1, width), lambda i: (0, 0)),
+            pl.BlockSpec((layers, MIX_BLOCK, width), lambda i: (0, i, 0)),
         ],
-        out_specs=[in_vmem, in_vmem],
+        out_specs=[row_spec, row_spec],
         out_shape=[
             jax.ShapeDtypeStruct((rows, width), jnp.float32),
             jax.ShapeDtypeStruct((rows, width), jnp.bfloat16),
         ],
-        scratch_shapes=[
-            pltpu.VMEM((blocks, layers, ROW_BLOCK, width), jnp.bfloat16),
-            pltpu.SemaphoreType.DMA((blocks,)),
-        ],
-        compiler_params=params(),
+        compiler_params=params(57),
         cost_estimate=cost(1000, 1000),
         name="mix",
     )(weights, gain[None], history)
 
 
 def unmix_kernel(
-    weights_ref, gain_ref, mixed_ref, middle_ref, own_ref, other_ref, gain_mlp_ref, history_ref,
-    *refs,
+    weights_ref, gain_ref, mixed_ref, middle_ref, own_ref, other_ref, gain_mlp_ref,
+    rows_ref, block_own_ref, block_other_ref, history_ref, *refs,
 ):
-    grads_ref, small_ref, held_ref, given_ref, in_sems, out_sems = refs[-6:]
+    (
+        grads_ref, out_ref, small_ref, held_ref, given_ref, made_ref, in_sems, out_sems, made_sem
+    ) = refs[-9:]
     copies = layer_copies(history_ref, held_ref, in_sems)
     gives = layer_copies(grads_ref, given_ref, out_sems, True)
     for copy in copies:
         copy.start()
+    block = rows_ref[...] + block_own_ref[...] + block_other_ref[...].astype(jnp.float32)
+    made_ref[...] = block.astype(jnp.bfloat16)
+    make = pltpu.make_async_copy(made_ref, out_ref, made_sem)
+    make.start()
     layers = held_ref.shape[1]
     small_ref[...] = jnp.zeros_like(small_ref)
     small_ref[1:2] = gain_mlp_ref[...]
@@ -153,11 +149,12 @@
             product = held_ref[index, layer].astype(jnp.float32) * grad_mixed
             small_ref[8 + layer : 9 + layer] += jnp.sum(product, axis=0, keepdims=True)
         give.start()
+    make.wait()
     for give in gives:
         give.wait()
 
 
-def unmix(weights, history, gain, mixed, grad_middle, own, other, gain_grad_mlp, after=()):
+def unmix(weights, history, gain, mixed, grad_middle, own, other, gain_grad_mlp, block, after=()):
     layers, rows, width = history.shape
     in_vmem = pl.BlockSpec(memory_space=pltpu.VMEM)
     in_hbm = pl.BlockSpec(memory_space=pltpu.HBM)
@@ -166,24 +163,27 @@
     return pl.pallas_call(
         unmix_kernel,
         in_specs=[pl.BlockSpec(memory_space=pltpu.SMEM)]
-        + [in_vmem] * 6
+        + [in_vmem] * 9
         + [in_hbm]
         + [pl.BlockSpec(memory_space=pl.ANY)] * len(after),
-        out_specs=[in_hbm, in_vmem],
+        out_specs=[in_hbm, in_hbm, in_vmem],
         out_shape=[
             jax.ShapeDtypeStruct(history.shape, jnp.bfloat16),
-            jax.ShapeDtypeStruct((8 + layers, width), jnp.float32),
+            jax.ShapeDtypeStruct((rows, width), jnp.bfloat16),
+            jax.ShapeDtypeStruct((SMALL_ROWS, width), jnp.float32),
         ],
         scratch_shapes=[
             held,
             held,
+            pltpu.VMEM((rows, width), jnp.bfloat16),
             pltpu.SemaphoreType.DMA((blocks,)),
             pltpu.SemaphoreType.DMA((blocks,)),
+            pltpu.SemaphoreType.DMA,
         ],
-        compiler_params=params(),
+        compiler_params=params(15),
         cost_estimate=cost(1000, 1000),
         name="unmix",
-    )(weights, gain[None], mixed, grad_middle, own, other, gain_grad_mlp, history, *after)
+    )(weights, gain[None], mixed, grad_middle, own, other, gain_grad_mlp, *block, history, *after)
 
 
 def head_mask(head):
@@ -197,7 +197,18 @@
     return keys > asks
 
 
-def local_call(kernel, name, at, arrays, outs, after=(), scratch=(), aliases=None):
+def stacked_heads(rows):
+    zero = jnp.zeros_like(rows)
+    return jnp.concatenate([jnp.where(head_mask(head), rows, zero) for head in range(2)], axis=0)
+
+
+def own_heads(columns):
+    half = columns.shape[1] // 2
+    return jnp.concatenate([columns[:HEAD_DIM, :half], columns[HEAD_DIM:, half:]], axis=0)
+
+
+def local_call(kernel, name, at, arrays, outs, after=(), scratch=(), aliases=None,
+               mebibytes=8):
     in_vmem = pl.BlockSpec(memory_space=pltpu.VMEM)
     return pl.pallas_call(
         kernel,
@@ -208,7 +219,7 @@
         out_shape=[jax.ShapeDtypeStruct(shape, dtype) for shape, dtype in outs],
         scratch_shapes=list(scratch),
         input_output_aliases=aliases or {},
-        compiler_params=params(),
+        compiler_params=params(mebibytes),
         cost_estimate=cost(1000, 1000),
         name=name,
     )(at, *arrays, *after)
@@ -223,7 +234,7 @@
     first = at_ref[0]
     scale = HEAD_DIM ** (-0.5) * LOG2E
     places = (first, 1 - first)
-    later = future_mask()
+    later = jnp.concatenate([future_mask()] * 2, axis=1)
 
     def one_pair(pair, carry):
         lanes = pl.ds(pl.multiple_of(pair * PAIR, PAIR), PAIR)
@@ -238,37 +249,34 @@
             for tile in range(tiles):
                 at_rows = pl.ds(tile * TILE, TILE)
                 queries = qkv_ref[0, places[half], at_rows, lanes]
-                outs = []
+                asked = stacked_heads(queries)
+                spans = []
+                if half == 1:
+                    spans.append((0, 0, rows))
+                if tile > 0:
+                    spans.append((half, 0, tile * TILE))
+                spans.append((half, tile * TILE, TILE))
+                scores = [
+                    dot(half_keys[where][start : start + size], asked, CONTRACT_COLS)
+                    for where, start, size in spans
+                ]
+                scores[-1] = jnp.where(later, NEG, scores[-1])
+                top = functools.reduce(
+                    jnp.maximum, [jnp.max(part, axis=0, keepdims=True) for part in scores]
+                )
+                top = top * scale
+                total = 0.0
+                summed = 0.0
+                for part, (where, start, size) in zip(scores, spans):
+                    weights = jnp.exp2(part * scale - top)
+                    total = total + jnp.sum(weights, axis=0, keepdims=True)
+                    summed = summed + dot(
+                        half_values[where][:, start : start + size], weights.astype(jnp.bfloat16)
+                    )
+                lse = top + jnp.log2(total)
                 for head in range(2):
-                    asked = jnp.where(head_mask(head), queries, jnp.zeros_like(queries))
-                    spans = []
-                    if half == 1:
-                        spans.append((0, 0, rows))
-                    if tile > 0:
-                        spans.append((half, 0, tile * TILE))
-                    spans.append((half, tile * TILE, TILE))
-                    scores = [
-                        dot(half_keys[where][start : start + size], asked, CONTRACT_COLS)
-                        for where, start, size in spans
-                    ]
-                    scores[-1] = jnp.where(later, NEG, scores[-1])
-                    top = functools.reduce(
-                        jnp.maximum, [jnp.max(part, axis=0, keepdims=True) for part in scores]
-                    )
-                    top = top * scale
-                    total = 0.0
-                    summed = 0.0
-                    mine = slice(head * HEAD_DIM, (head + 1) * HEAD_DIM)
-                    for part, (where, start, size) in zip(scores, spans):
-                        weights = jnp.exp2(part * scale - top)
-                        total = total + jnp.sum(weights, axis=0, keepdims=True)
-                        summed = summed + dot(
-                            half_values[where][mine, start : start + size],
-                            weights.astype(jnp.bfloat16),
-                        )
-                    outs.append(summed / total)
-                    lse_ref[pair, head, half, :, at_rows] = top + jnp.log2(total)
-                joined = jnp.concatenate(outs, axis=0).T
+                    lse_ref[pair, head, half, :, at_rows] = lse[:, head * TILE : (head + 1) * TILE]
+                joined = own_heads(summed / total).T
                 att_ref[places[half], at_rows, lanes] = joined.astype(jnp.bfloat16)
         return carry
 
@@ -292,6 +300,7 @@
             ((rows, width), jnp.float32),
             ((rows, width), jnp.bfloat16),
         ],
+        mebibytes=12,
     )
 
 
@@ -404,25 +413,6 @@
     )
 
 
-def block_kernel(at_ref, middle_ref, own_ref, other_ref, *refs):
-    total = middle_ref[...] + own_ref[...] + other_ref[...].astype(jnp.float32)
-    refs[-1][...] = total.astype(jnp.bfloat16)
-
-
-def block_sum(at, middle, own, other, after=()):
-    outs = [(middle.shape, jnp.bfloat16)]
-    return local_call(block_kernel, "block_sum", at, [middle, own, other], outs, after)[0]
-
-
-def small_kernel(at_ref, mine_ref, came_ref, *refs):
-    refs[-1][...] = mine_ref[...] + came_ref[...]
-
-
-def small_sum(at, mine, came, after=()):
-    outs = [(mine.shape, jnp.float32)]
-    return local_call(small_kernel, "small", at, [mine, came], outs, after)[0]
-
-
 def norm_back_kernel(at_ref, own_ref, other_ref, middle_ref, cot_ref, gain_ref, *refs):
     grad_ref, narrow_ref, gain_grad_ref = refs[-3:]
     grad_second = own_ref[...] + other_ref[...].astype(jnp.float32)
@@ -448,8 +438,8 @@
 
 
 def attend_back_kernel(
-    slot, pair, place, at_ref, qkv_ref, att_ref, lse_ref, grad_own_ref, grad_other_ref, out_weight_ref,
-    first_own_ref, first_other_ref, *refs,
+    slot, pair, place, at_ref, qkv_ref, att_ref, lse_ref, grad_own_ref, grad_other_ref,
+    out_weight_ref, first_own_ref, first_other_ref, *refs,
 ):
     keep_ref, send_ref, grad_rows_ref = refs[-3:]
     rows = grad_own_ref.shape[0]
@@ -458,17 +448,13 @@
     plain = HEAD_DIM ** (-0.5)
     scale = plain * LOG2E
     places = (first, 1 - first)
-    later = future_mask()
+    later = jnp.concatenate([future_mask()] * 2, axis=1)
     bf16 = jnp.bfloat16
     sides = (grad_own_ref, grad_other_ref)
     firsts = (first_own_ref, first_other_ref)
-    masked = [head_mask(head) for head in range(2)]
     unit = 4 * PAIR // (2 * keep_ref.shape[0])
     is_own = [places[half] == 0 for half in range(2)]
     chunks = [(half, tile) for half in range(2) for tile in range(tiles)]
-
-    def only(head, part):
-        return jnp.where(masked[head], part, jnp.zeros_like(part))
 
     def plus(old, term):
         return term if old is None else old + term
@@ -490,41 +476,49 @@
             jnp.sum(product[head * HEAD_DIM : (head + 1) * HEAD_DIM], axis=0, keepdims=True)
             for head in range(2)
         ])
-    key_grads = [None for _ in chunks]
-    value_grads = [None for _ in chunks]
+    key_grads = {}
+    value_grads = {}
     query_grads = []
-    for ask, (ask_half, ask_tile) in enumerate(chunks):
-        ask_rows = slice(ask_tile * TILE, (ask_tile + 1) * TILE)
-        sums_here = []
-        for head in range(2):
-            asked = only(head, queries[ask_half][ask_rows])
-            grad = only(head, grads[ask_half][ask_rows])
-            lse = lse_ref[pair, head, ask_half, :, ask_rows]
-            delta = deltas[ask_half][head][:, ask_rows]
-            query_grad = None
-            for key in range(ask + 1):
-                key_half, key_tile = chunks[key]
-                key_rows = slice(key_tile * TILE, (key_tile + 1) * TILE)
-                scores = dot(keys[key_half][key_rows], asked, CONTRACT_COLS)
-                probs = jnp.exp2(scores * scale - lse)
-                if key == ask:
-                    probs = jnp.where(later, 0.0, probs)
-                grad_probs = dot(values[key_half][key_rows], grad, CONTRACT_COLS)
-                grad_scores = (probs * (grad_probs - delta)).astype(bf16)
-                value_grads[key] = plus(value_grads[key], dot(probs.astype(bf16), grad))
-                key_grads[key] = plus(key_grads[key], dot(grad_scores, asked))
-                mine = slice(head * HEAD_DIM, (head + 1) * HEAD_DIM)
-                query_grad = plus(
-                    query_grad, dot(keys_t[key_half][mine, key_rows], grad_scores)
-                )
-            sums_here.append(query_grad)
-        query_grads.append((jnp.concatenate(sums_here, axis=0) * plain).astype(bf16))
+    for half, tile in chunks:
+        here = slice(tile * TILE, (tile + 1) * TILE)
+        asked = stacked_heads(queries[half][here])
+        grad = stacked_heads(grads[half][here])
+        lse = jnp.concatenate([lse_ref[pair, head, half, :, here] for head in range(2)], axis=1)
+        delta = jnp.concatenate([deltas[half][head][:, here] for head in range(2)], axis=1)
+        spans = []
+        if half == 1:
+            spans.append((0, 0, rows))
+        if tile > 0:
+            spans.append((half, 0, tile * TILE))
+        spans.append((half, tile * TILE, TILE))
+        query_grad = None
+        for where, start, size in spans:
+            span = slice(start, start + size)
+            scores = dot(keys[where][span], asked, CONTRACT_COLS)
+            probs = jnp.exp2(scores * scale - lse)
+            if (where, start) == (half, tile * TILE):
+                probs = jnp.where(later, 0.0, probs)
+            grad_probs = dot(values[where][span], grad, CONTRACT_COLS)
+            grad_scores = (probs * (grad_probs - delta)).astype(bf16)
+            value_term = dot(probs.astype(bf16), grad)
+            key_term = dot(grad_scores, asked)
+            query_grad = plus(query_grad, dot(keys_t[where][:, span], grad_scores))
+            for part in range(size // TILE):
+                at_part = (where, start // TILE + part)
+                cut = slice(part * TILE, (part + 1) * TILE)
+                value_grads[at_part] = plus(value_grads.get(at_part), value_term[cut])
+                key_grads[at_part] = plus(key_grads.get(at_part), key_term[cut])
+        query_grads.append((own_heads(query_grad) * plain).astype(bf16))
     turned = []
     for half in range(2):
         at_half = [i for i, (where, _) in enumerate(chunks) if where == half]
         query_t = jnp.concatenate([query_grads[i] for i in at_half], axis=1)
-        key = jnp.concatenate([(key_grads[i] * plain).astype(bf16) for i in at_half], axis=0)
-        value = jnp.concatenate([value_grads[i].astype(bf16) for i in at_half], axis=0)
+        key = jnp.concatenate(
+            [(key_grads[half, tile] * plain).astype(bf16) for tile in range(tiles)], axis=0
+        )
+        value = jnp.concatenate(
+            [value_grads[half, tile].astype(bf16) for tile in range(tiles)], axis=0
+        )
         turned.append([query_t, key.T, value.T, att_ref[places[half], :, lanes].T])
         for c, part in enumerate((query_t.T, key, value)):
             grad_rows_ref[c, places[half]] = part
@@ -536,9 +530,7 @@
         bottom = bottom + jnp.concatenate(
             [dot(mine[2], rows_here), dot(mine[3], sides[side][...])], axis=0
         )
-    split_halves(
-        at_ref[slot], pl.ds(place * unit, unit), top, bottom, keep_ref, send_ref
-    )
+    split_halves(at_ref[slot], pl.ds(place * unit, unit), top, bottom, keep_ref, send_ref)
 
 
 def attend_back(at, slot, pair, place, count, qkv, att, lse, grad_own, grad_other, out_weight,
@@ -556,23 +548,20 @@
         [pieces, pieces, ((3, 2, rows, PAIR), jnp.bfloat16)],
         after,
         aliases={len(arrays) - 1: 0, len(arrays): 1} if old else {},
+        mebibytes=12,
     )
 
 
 def first_back_kernel(count, at_ref, weight_ref, *refs):
     own_ref, other_ref = refs[-2:]
-    groups = []
-    start = 0
-    for ref in refs[:count]:
-        groups.append((ref, start))
-        start += ref.shape[3]
+    pieces = []
+    for index, ref in enumerate(refs[:count]):
+        lanes = slice(index * PAIR, (index + 1) * PAIR)
+        pieces += [(ref, c, lanes) for c in range(3)]
+    weight = jnp.concatenate([weight_ref[c, :, lanes] for _, c, lanes in pieces], axis=1)
     for side, out_ref in ((1, other_ref), (0, own_ref)):
-        total = 0.0
-        for ref, begin in groups:
-            for c in range(3):
-                lanes = slice(begin, begin + ref.shape[3])
-                total = total + dot(ref[c, side], weight_ref[c, :, lanes], CONTRACT_COLS)
-        out_ref[...] = total.astype(out_ref.dtype)
+        rows = jnp.concatenate([ref[c, side] for ref, c, _ in pieces], axis=1)
+        out_ref[...] = dot(rows, weight, CONTRACT_COLS).astype(out_ref.dtype)
 
 
 def first_back(at, weight, groups, after=()):
@@ -600,115 +589,166 @@
     refs[-1][...] = total.astype(jnp.bfloat16)
 
 
+def widen(pair):
+    half = pair.shape[0] // 2
+    pair = pair.astype(jnp.float32)
+    return pair[:half] + pair[half:]
+
+
+def narrow(value):
+    high = value.astype(jnp.bfloat16)
+    low = (value - high.astype(jnp.float32)).astype(jnp.bfloat16)
+    return jnp.concatenate([high, low], axis=0)
+
+
+def add_small_kernel(at_ref, kept_ref, came_ref, mine_ref, other_ref, *refs):
+    total = kept_ref[0].astype(jnp.float32) + came_ref[0].astype(jnp.float32)
+    refs[-1][0] = total.astype(jnp.bfloat16)
+    refs[-1][1] = narrow(mine_ref[...] + other_ref[...])
+
+
+def again_kernel(at_ref, mine_ref, came_ref, *refs):
+    total = mine_ref[0].astype(jnp.float32) + came_ref[0].astype(jnp.float32)
+    refs[-1][0] = total.astype(jnp.bfloat16)
+    if mine_ref.shape[0] > 1:
+        refs[-1][1] = narrow(widen(mine_ref[1]) + widen(came_ref[1]))
+
+
 def join_kernel(slot, at_ref, mine_ref, came_ref, *refs):
     both_ref = refs[-1]
-    half = mine_ref.shape[0]
+    half = both_ref.shape[0] // 2
     bit = at_ref[slot]
     for source, start in ((mine_ref, bit * half), (came_ref, (1 - bit) * half)):
         for index in range(half):
             both_ref[start + index] = source[index]
+    if both_ref.shape[0] > 2 * half:
+        both_ref[2 * half] = narrow(widen(mine_ref[half]) + widen(came_ref[half]))
 
 
 def fold(at, slot, kept, came, after=()):
     blocks, rows, width = kept.shape
-    if blocks == 1:
-        outs = [(kept.shape, jnp.bfloat16)]
-        return local_call(add_kernel, "add", at, [kept, came], outs, after)[0]
     outs = [((blocks // 2, rows, width), jnp.bfloat16)] * 2
     return local_call(
         functools.partial(fold_kernel, slot), "fold", at, [kept, came], outs, after
     )
 
 
-def join(at, slot, mine, came, after=()):
-    blocks, rows, width = mine.shape
-    outs = [((2 * blocks, rows, width), jnp.bfloat16)]
+def last_fold(at, kept, came, small, after=()):
+    blocks, rows, width = kept.shape
+    kernel = add_small_kernel if small else add_kernel
+    outs = [((blocks + (1 if small else 0), rows, width), jnp.bfloat16)]
+    return local_call(kernel, "add", at, [kept, came, *small], outs, after)[0]
+
+
+def again(at, mine, came, after=()):
+    outs = [(mine.shape, jnp.bfloat16)]
+    return local_call(again_kernel, "again", at, [mine, came], outs, after)[0]
+
+
+def join(at, slot, mine, came, blocks, after=()):
+    _, rows, width = mine.shape
+    extra = mine.shape[0] - blocks
+    outs = [((2 * blocks + extra, rows, width), jnp.bfloat16)]
     return local_call(
         functools.partial(join_kernel, slot), "join", at, [mine, came], outs, after
     )[0]
 
 
-def in_order(bit, mine, came):
-    rows = mine.shape[0] * mine.shape[1]
-    mine = mine.reshape(rows, -1).astype(jnp.float32)
-    came = came.reshape(rows, -1).astype(jnp.float32)
-    return jnp.where(bit == 0, mine, came), jnp.where(bit == 0, came, mine)
-
-
-def finish_mlp_kernel(slot, at_ref, mine_ref, came_ref, *refs):
-    up_ref, down_ref, token_ref = refs[-3:]
+def ordered_units(bit, mine_ref, came_ref, blocks, unit):
+    width = mine_ref.shape[2]
+    for index in range(mine_ref.shape[1] // unit):
+        rows = slice(index * unit, (index + 1) * unit)
+        mine = mine_ref[:blocks, rows, :].reshape(blocks * unit, width)
+        came = came_ref[:blocks, rows, :].reshape(blocks * unit, width)
+        yield index, jnp.where(bit == 0, mine, came), jnp.where(bit == 0, came, mine)
+
+
+def finish_mlp_kernel(slot, start, blocks, at_ref, mine_ref, came_ref, *refs):
+    up_ref, down_ref, token_ref, turned_ref, held_ref, up_sems, down_sems = refs[-7:]
     token_ref[...] = jnp.zeros_like(token_ref)
-    top, bottom = in_order(at_ref[slot], mine_ref[...], came_ref[...])
-    up_ref[...] = top.T
-    down_ref[...] = bottom
+    copies = []
+    for index, top, bottom in ordered_units(
+        at_ref[slot], mine_ref, came_ref, blocks, TILE // blocks
+    ):
+        place = pl.ds((start + index) * TILE, TILE)
+        held_ref[index] = bottom.astype(jnp.float32)
+        copies.append(
+            pltpu.make_async_copy(held_ref.at[index], down_ref.at[place, :], down_sems.at[index])
+        )
+        copies[-1].start()
+        turned_ref[index] = top.T.astype(jnp.float32)
+        copies.append(
+            pltpu.make_async_copy(turned_ref.at[index], up_ref.at[:, place], up_sems.at[index])
+        )
+        copies[-1].start()
+    for copy in copies:
+        copy.wait()
+
+
+def finish_attend_kernel(slot, start, blocks, at_ref, mine_ref, came_ref, *refs):
+    qkv_ref, out_ref, token_ref, turned_ref, held_ref, qkv_sems, out_sems = refs[-7:]
+    token_ref[...] = jnp.zeros_like(token_ref)
+    if mine_ref.shape[0] > blocks:
+        token_ref[...] = widen(mine_ref[blocks]) + widen(came_ref[blocks])
+    copies = []
+    for index, top, bottom in ordered_units(
+        at_ref[slot], mine_ref, came_ref, blocks, 2 * PAIR // blocks
+    ):
+        place = pl.ds((start + index) * PAIR, PAIR)
+        held_ref[index] = bottom[PAIR:].astype(jnp.float32)
+        copies.append(
+            pltpu.make_async_copy(held_ref.at[index], out_ref.at[place, :], out_sems.at[index])
+        )
+        copies[-1].start()
+        for c, part in enumerate((top[:PAIR], top[PAIR:], bottom[:PAIR])):
+            turned_ref[index, c] = part.T.astype(jnp.float32)
+        copies.append(
+            pltpu.make_async_copy(
+                turned_ref.at[index], qkv_ref.at[:, :, place], qkv_sems.at[index]
+            )
+        )
+        copies[-1].start()
+    for copy in copies:
+        copy.wait()
+
+
+def finish(kernel, name, at, slot, start, mine, came, shapes, scratch, old=None, after=()):
+    in_vmem = pl.BlockSpec(memory_space=pltpu.VMEM)
+    in_hbm = pl.BlockSpec(memory_space=pltpu.HBM)
+    blocks = 2 ** (SPLITS - 1)
+    units = mine.shape[1] * blocks // TILE
+    return pl.pallas_call(
+        functools.partial(kernel, slot, start, blocks),
+        in_specs=[pl.BlockSpec(memory_space=pltpu.SMEM), in_vmem, in_vmem]
+        + [in_hbm] * len(old or [])
+        + [pl.BlockSpec(memory_space=pl.ANY)] * len(after),
+        out_specs=[in_hbm, in_hbm, in_vmem],
+        out_shape=[jax.ShapeDtypeStruct(shape, jnp.float32) for shape in shapes]
+        + [jax.ShapeDtypeStruct((SMALL_ROWS, mine.shape[2]), jnp.float32)],
+        scratch_shapes=[pltpu.VMEM((units, *shape), jnp.float32) for shape in scratch]
+        + [pltpu.SemaphoreType.DMA((units,))] * 2,
+        input_output_aliases={3: 0, 4: 1} if old else {},
+        compiler_params=params(12),
+        cost_estimate=cost(1000, 1000),
+        name=name,
+    )(at, mine, came, *(old or []), *after)
 
 
 def finish_mlp(at, slot, start, mine, came, width, hidden, old=None, after=()):
-    blocks, rows, _ = mine.shape
-    unit = TILE // blocks
-    part = pl.BlockSpec((blocks, unit, TILE), lambda i, j, at: (0, i, j))
-    return pl.pallas_call(
-        functools.partial(finish_mlp_kernel, slot),
-        grid_spec=pltpu.PrefetchScalarGridSpec(
-            num_scalar_prefetch=1,
-            grid=(rows // unit, width // TILE),
-            in_specs=[part, part]
-            + [pl.BlockSpec(memory_space=pl.ANY)] * (len(old or []) + len(after)),
-            out_specs=[
-                pl.BlockSpec((TILE, TILE), lambda i, j, at: (j, start + i)),
-                pl.BlockSpec((TILE, TILE), lambda i, j, at: (start + i, j)),
-                pl.BlockSpec((8, 128), lambda i, j, at: (0, 0)),
-            ],
-        ),
-        out_shape=[
-            jax.ShapeDtypeStruct((width, hidden), jnp.float32),
-            jax.ShapeDtypeStruct((hidden, width), jnp.float32),
-            jax.ShapeDtypeStruct((8, 128), jnp.float32),
-        ],
-        input_output_aliases={3: 0, 4: 1} if old else {},
-        compiler_params=params(),
-        cost_estimate=cost(1000, 1000),
-        name="finish_mlp",
-    )(at, mine, came, *(old or []), *after)
-
-
-def finish_attend_kernel(slot, at_ref, mine_ref, came_ref, *refs):
-    qkv_ref, out_ref, token_ref = refs[-3:]
-    token_ref[...] = jnp.zeros_like(token_ref)
-    top, bottom = in_order(at_ref[slot], mine_ref[...], came_ref[...])
-    qkv_ref[0] = top[:PAIR].T
-    qkv_ref[1] = top[PAIR:].T
-    qkv_ref[2] = bottom[:PAIR].T
-    out_ref[...] = bottom[PAIR:]
+    shapes = [(width, hidden), (hidden, width)]
+    scratch = [(width, TILE), (TILE, width)]
+    return finish(
+        finish_mlp_kernel, "finish_mlp", at, slot, start, mine, came, shapes, scratch, old, after
+    )
 
 
 def finish_attend(at, slot, start, mine, came, width, local, old=None, after=()):
-    blocks, rows, _ = mine.shape
-    unit = 2 * PAIR // blocks
-    part = pl.BlockSpec((blocks, unit, TILE), lambda i, j, at: (0, i, j))
-    return pl.pallas_call(
-        functools.partial(finish_attend_kernel, slot),
-        grid_spec=pltpu.PrefetchScalarGridSpec(
-            num_scalar_prefetch=1,
-            grid=(rows // unit, width // TILE),
-            in_specs=[part, part]
-            + [pl.BlockSpec(memory_space=pl.ANY)] * (len(old or []) + len(after)),
-            out_specs=[
-                pl.BlockSpec((3, TILE, PAIR), lambda i, j, at: (0, j, start + i)),
-                pl.BlockSpec((PAIR, TILE), lambda i, j, at: (start + i, j)),
-                pl.BlockSpec((8, 128), lambda i, j, at: (0, 0)),
-            ],
-        ),
-        out_shape=[
-            jax.ShapeDtypeStruct((3, width, local), jnp.float32),
-            jax.ShapeDtypeStruct((local, width), jnp.float32),
-            jax.ShapeDtypeStruct((8, 128), jnp.float32),
-        ],
-        input_output_aliases={3: 0, 4: 1} if old else {},
-        compiler_params=params(),
-        cost_estimate=cost(1000, 1000),
-        name="finish_attend",
-    )(at, mine, came, *(old or []), *after)
+    shapes = [(3, width, local), (local, width)]
+    scratch = [(3, width, PAIR), (PAIR, width)]
+    return finish(
+        finish_attend_kernel, "finish_attend", at, slot, start, mine, came, shapes, scratch, old,
+        after,
+    )
 
 
 def mp_swap(rows):
@@ -748,28 +788,32 @@
 
 
 class Stream:
-    def __init__(self, at, kind, kept, sent):
-        self.at, self.kind, self.kept, self.step = at, kind, kept, 0
+    def __init__(self, at, kind, kept, sent, small=None):
+        self.at, self.kind, self.kept, self.step, self.small = at, kind, kept, 0, small
+        self.extra = dp_bits() - SPLITS
         self.came = bit_swap(sent, step_bits(kind, 0))
 
     def advance(self, after=()):
-        step, kind = self.step, self.kind
+        step, kind, at = self.step, self.kind, self.at
         self.step += 1
+        joined = step - SPLITS - self.extra
         if step < SPLITS - 1:
-            self.kept, sent = fold(
-                self.at, slot_of(kind, step + 1), self.kept, self.came, after
-            )
+            self.kept, sent = fold(at, slot_of(kind, step + 1), self.kept, self.came, after)
             self.came = bit_swap(sent, step_bits(kind, step + 1))
             return self.kept
         if step == SPLITS - 1:
-            self.kept = fold(self.at, 0, self.kept, self.came, after)
-            for bit in range(SPLITS, dp_bits()):
-                other = bit_swap(self.kept, [bit, bit])
-                self.kept = fold(self.at, 0, self.kept, other)
+            small = self.small() if self.small else ()
+            self.kept = last_fold(at, self.kept, self.came, small, after)
+        elif joined < 0:
+            self.kept = again(at, self.kept, self.came, after)
         else:
-            bit_step = 2 * SPLITS - 1 - step
-            self.kept = join(self.at, slot_of(kind, bit_step), self.kept, self.came, after)
-        self.came = bit_swap(self.kept, step_bits(kind, 2 * SPLITS - 2 - step))
+            slot = slot_of(kind, SPLITS - 1 - joined)
+            self.kept = join(at, slot, self.kept, self.came, 2**joined, after)
+        if joined < -1:
+            bit = SPLITS + joined + 1 + self.extra
+            self.came = bit_swap(self.kept, [bit, bit])
+        else:
+            self.came = bit_swap(self.kept, step_bits(kind, SPLITS - 2 - joined))
         return self.kept
 
 
@@ -824,7 +868,8 @@
         )
         made["stack"] = (kept, sent)
         if pair >= pairs - 2:
-            streams[name] = Stream(at, KIND[name], kept, sent)
+            small = (lambda: (made["small"], made["small_came"])) if late else None
+            streams[name] = Stream(at, KIND[name], kept, sent, small)
         return made[pair]
 
     def back_first(after):
@@ -834,27 +879,18 @@
         return made["own"]
 
     def back_start(after):
-        made["history"], made["small"] = unmix(
+        block = (middle, made["block"], made["block_came"])
+        made["history"], made["out"], made["small"] = unmix(
             depth_weights, history, gain_attn, mixed, made["middle"], made["own"], made["came"],
-            made["gain"], after,
+            made["gain"], block, after,
         )
         made["small_came"] = mp_swap(made["small"])
-        return made["small"]
-
-    def small_step(bit, after):
-        made["small"] = small_sum(at, made["small"], made["small_came"], after)
-        if bit < dp_bits():
-            made["small_came"] = bit_swap(made["small"], [bit, bit])
         return made["small"]
 
     def block_rows(after):
         made["block"], other = rows_times(at, hidden_rows, down_weight, after)
         made["block_came"] = mp_swap(other)
         return made["block"]
-
-    def block_end(after):
-        made["out"] = block_sum(at, middle, made["block"], made["block_came"], after)
-        return made["out"]
 
     def end_mlp(name, start, after):
         stream = streams[name]
@@ -866,18 +902,17 @@
 
     def end_attend(name, start, after):
         stream = streams[name]
-        *made["attend"], token = finish_attend(
+        *made["attend"], made[name] = finish_attend(
             at, slot_of(KIND[name], 0), start, stream.kept, stream.came, width, local,
             made.get("attend"), after,
         )
-        return token
+        return made[name]
 
     units = {
         "nb": back_norm,
         "fb": back_first,
         "um": back_start,
         "blk": block_rows,
-        "bo": block_end,
         "fMa": functools.partial(end_mlp, "Ma", 0),
         "fMb": functools.partial(end_mlp, "Mb", EARLY),
         "fAa": functools.partial(end_attend, "Aa", 0),
@@ -885,20 +920,17 @@
     }
     for pair in range(pairs):
         units["ab" + str(pair)] = functools.partial(back_pair, pair)
-    bits = 0
     last = hidden_rows
     for name in ORDER:
         if name in streams:
+            if streams[name].step == SPLITS:
+                for _ in range(streams[name].extra - 1):
+                    last = streams[name].advance([last])
             last = streams[name].advance([last])
-        elif name == "sm":
-            last = small_step(bits, [last])
-            bits += 1
         else:
             last = units[name]([last])
-    for bit in range(bits, dp_bits() + 1):
-        last = small_step(bit, [last])
-    small = made["small"]
-    grad_depth = jnp.sum(small[8:], axis=1)
+    small = made["Ab"]
+    grad_depth = jnp.sum(small[8 : 8 + history.shape[0]], axis=1)
     block_out, grad_history = made["out"], made["history"]
     gain_grad_attn, gain_grad_mlp = small[0], small[1]
     (grad_up, grad_down), (grad_qkv, grad_out) = made["mlp"], made["attend"]

time: 229 us -> 197 us (0.86)
  starting transfers between devices: 56.4 us -> 38.9 us
  Pallas kernels: 109 us -> 91.7 us
  waiting for transfers between devices: 43.2 us -> 58 us
  local copies, waits for them, and re-layouts: 13.8 us -> 3.16 us
    ppermute x36 -> x28, starting transfers between devices: 54.4 us -> 36.3 us  [bit_swap(): return lax.ppermute(rows, ('dp', 'mp'), pairs)]
    ppermute x36 -> x28, waiting for transfers between devices: 37.7 us -> 52.3 us  [bit_swap(): return lax.ppermute(rows, ('dp', 'mp'), pairs)]
    pallas_call x43 -> x33, Pallas kernels: 82.4 us -> 68.6 us  [local_call(): pl.pallas_call(kernel, in_specs=[pl.BlockSpec(memory_space=pltpu.SMEM)] +...]
    unnamed x50 -> x26, local copies, waits for them, and re-layouts: 12.4 us -> 1.19 us
    pallas_call x5, Pallas kernels: 19.5 us -> 16 us  [the longest x4 10.5 us: finish(): pl.pallas_call(functools.partial(kernel, slot, start, blocks), in_specs=[...]
  transfers between devices with their start and end apart: 45 -> 37, of which waited for: 16 -> 15; matrix products, arithmetic and copies ran while one was open for 1% -> 1% of each run, Pallas kernels for 31% -> 29%
where the time goes in v4:
time: 197 us; the launch traced here: 194 us
  Pallas kernels  91.7 us (47%)
  waiting for transfers between devices  58 us (29%)
  starting transfers between devices  38.9 us (20%)
  local copies, waits for them, and re-layouts  3.16 us (2%)
    pallas_call x33, Pallas kernels, local_call(): pl.pallas_call(kernel, in_specs=[pl.BlockSpec(memory_space=pltpu.SMEM)] +...  68.6 us
    ppermute x28, waiting for transfers between devices, bit_swap(): return lax.ppermute(rows, ('dp', 'mp'), pairs)  52.3 us
    ppermute x28, starting transfers between devices, bit_swap(): return lax.ppermute(rows, ('dp', 'mp'), pairs)  36.3 us
    pallas_call x4, Pallas kernels, finish(): pl.pallas_call(functools.partial(kernel, slot, start, blocks), in_specs=[...  10.5 us
    pallas_call x1, Pallas kernels, unmix(): pl.pallas_call(unmix_kernel, in_specs=[pl.BlockSpec(memory_space=pltpu.SM...  7.06 us
    ppermute x9, waiting for transfers between devices, mp_swap(): return lax.ppermute(rows, 'mp', [(0, 1), (1, 0)])  5.73 us
    pallas_call x1, Pallas kernels, mix(): pl.pallas_call(mix_kernel, grid=(rows // MIX_BLOCK,), in_specs=[pl.BlockS...  5.49 us
  transfers between devices with their start and end apart: 37, of which 15 were waited for; matrix products, arithmetic and copies ran while one was open for 1% of the time, Pallas kernels for 29%

profile of v4, /device:TPU:0, one launch (start us, length us, event | category | flops | bytes accessed | tf_op | source)
XLA Modules:
  0.0 193.7 jit_solution(5795002843140486478)
XLA Ops:
  1.9 5.5 %mix.1 = (f32[512,768]{1,0:T(8,128)}, bf16[512,768]{1,0:T(8,128)(2,1)}) custom-call(f32[8]{0:T(128)} %weights_ref.3, f32[1,768]{1,0:T(1,128)} %broadcast_in_dim.8.gain_ref, bf16[8,512,768]{2,1,0:T(8,128)(2,1)} %history_ref.3), custom_call_target="tpu_custom_call" | custom-call | flops 1000 | bytes 1000 | tf_op jit(solution)/shard_map/mix/pallas_call | solution.py:101
  11.1 12.2 %attend.1 = (bf16[3,2,512,384]{3,2,1,0:T(8,128)(2,1)S(1)}, bf16[2,512,384]{2,1,0:T(8,128)(2,1)S(1)}, f32[3,2,2,1,512]{4,3,2,1,0:T(1,128)S(1)}, f32[512,768]{1,0:T(8,128)S(1)}, bf16[512,768]{1,0:T(8,128)(2,1)S(1)}) custom-call(s32[13]{0:T(128)S(1)} %stack.37.at_ref, bf16[512,768]{1,0:T(8,128)(2,1)S(1)} %copy-done, ...), custom_call_target="tpu_custom_call" | custom-call | flops 1000 | bytes 1000 | tf_op jit(solution)/shard_map/attend/pallas_call | solution.py:213
  29.2 14.5 %mlp.1 = (bf16[4,192,768]{2,1,0:T(8,128)(2,1)S(1)}, bf16[4,192,768]{2,1,0:T(8,128)(2,1)S(1)}, bf16[4,192,768]{2,1,0:T(8,128)(2,1)S(1)}, bf16[4,192,768]{2,1,0:T(...) custom-call(s32[13]{0:T(128)S(1)} %stack.37.at_ref, ...), custom_call_target="tpu_custom_call" | custom-call | flops 1000 | bytes 1000 | tf_op jit(solution)/shard_map/mlp/pallas_call | solution.py:213
  44.1 2.7 %collective-permute-start.6 = (bf16[4,192,768]{2,1,0:T(8,128)(2,1)S(1)}, bf16[4,192,768]{2,1,0:T(8,128)(2,1)S(1)}, u32[]{:S(2)}, u32[]{:S(2)}) collective-permute-start(bf16[4,192,768]{2,1,0:T(8,128)(2,1)S(1)} %get-tuple-element.91), channel_id=1, source_target_pairs={{0,8},{1,3},{2,10},{3,1},{4,12},{5,7},{6,14},{7,5},{8,0},{9,11},{1... | collective-permute-start | bytes 3538952 | tf_op jit(solution)/shard_map/ppermute | solution.py:769
  48.7 2.3 %collective-permute-start.9 = (bf16[4,192,768]{2,1,0:T(8,128)(2,1)S(1)}, bf16[4,192,768]{2,1,0:T(8,128)(2,1)S(1)}, u32[]{:S(2)}, u32[]{:S(2)}) collective-permute-start(bf16[4,192,768]{2,1,0:T(8,128)(2,1)S(1)} %get-tuple-element.99), channel_id=1, source_target_pairs={{0,8},{1,5},{2,10},{3,7},{4,12},{5,1},{6,14},{7,3},{8,0},{9,13},{1... | collective-permute-start | bytes 3538952 | tf_op jit(solution)/shard_map/ppermute | solution.py:769
  50.9 5.8 %attend_back.3 = (bf16[4,128,768]{2,1,0:T(8,128)(2,1)S(1)}, bf16[4,128,768]{2,1,0:T(8,128)(2,1)S(1)}, bf16[3,2,512,128]{3,2,1,0:T(8,128)(2,1)S(1)}) custom-call(s32[13]{0:T(128)S(1)} %stack.37.at_ref, bf16[3,2,512,384]{3,2,1,0:T(8,128)(2,1)S(1)} %get-tuple-element.81.qkv_ref, bf16[2,512,384]{2,1,0:T(8,128)(2,1)S(1)} %get-tuple-element.82.att_ref, ...), custom_call_target="tpu_custom_call" | custom-call | flops 1000 | bytes 1000 | tf_op jit(solution)/shard_map/attend_back/pallas_call | solution.py:213
  56.8 5.8 %attend_back.4 = (bf16[4,128,768]{2,1,0:T(8,128)(2,1)S(1)}, bf16[4,128,768]{2,1,0:T(8,128)(2,1)S(1)}, bf16[3,2,512,128]{3,2,1,0:T(8,128)(2,1)S(1)}) custom-call(s32[13]{0:T(128)S(1)} %stack.37.at_ref, bf16[3,2,512,384]{3,2,1,0:T(8,128)(2,1)S(1)} %get-tuple-element.81.qkv_ref, ...), custom_call_target="tpu_custom_call", output_to_operand_aliasing={{0}: (9, {}), {1}: (10, {})} | custom-call | flops 1000 | bytes 1000 | tf_op jit(solution)/shard_map/attend_back/pallas_call | solution.py:213
  62.6 2.1 %collective-permute-start.8 = (bf16[4,128,768]{2,1,0:T(8,128)(2,1)S(1)}, bf16[4,128,768]{2,1,0:T(8,128)(2,1)S(1)}, u32[]{:S(2)}, u32[]{:S(2)}) collective-permute-start(bf16[4,128,768]{2,1,0:T(8,128)(2,1)S(1)} %get-tuple-element.97), channel_id=1, source_target_pairs={{0,2},{1,5},{2,0},{3,7},{4,6},{5,1},{6,4},{7,3},{8,10},{9,13},{10,... | collective-permute-start | bytes 2359304 | tf_op jit(solution)/shard_map/ppermute | solution.py:769
  65.7 6.2 %attend_back.5 = (bf16[4,64,768]{2,1,0:T(8,128)(2,1)S(1)}, bf16[4,64,768]{2,1,0:T(8,128)(2,1)S(1)}, bf16[3,2,512,128]{3,2,1,0:T(8,128)(2,1)S(1)}) custom-call(s32[13]{0:T(128)S(1)} %stack.37.at_ref, bf16[3,2,512,384]{3,2,1,0:T(8,128)(2,1)S(1)} %get-tuple-element.81.qkv_ref, bf16[2,512,384]{2,1,0:T(8,128)(2,1)S(1)} %get-tuple-element.82.att_ref, ...), custom_call_target="tpu_custom_call" | custom-call | flops 1000 | bytes 1000 | tf_op jit(solution)/shard_map/attend_back/pallas_call | solution.py:213
  71.9 2.8 %first_back.1 = (f32[512,768]{1,0:T(8,128)S(1)}, bf16[512,768]{1,0:T(8,128)(2,1)S(1)}) custom-call(s32[13]{0:T(128)S(1)} %stack.37.at_ref, bf16[3,768,384]{2,1,0:T(8,128)(2,1)S(1)} %copy-done.4, bf16[3,2,512,128]{3,2,1,0:T(8,128)(2,1)S(1)} %get-tuple-element.86.refs_2_.refs_0_, bf16[3,2,512,128]{3,2,1,0:T(8,128)(2,1)S(1)} %get-tuple-element.89.refs_0_.refs_1_, ...), custom_call_target="tpu_custom_call" | custom-call | flops 1000 | bytes 1000 | tf_op jit(solution)/shard_map/first_back/pallas_call | solution.py:213
  75.5 2.1 %collective-permute-start.13 = (bf16[2,192,768]{2,1,0:T(8,128)(2,1)S(1)}, bf16[2,192,768]{2,1,0:T(8,128)(2,1)S(1)}, u32[]{:S(2)}, u32[]{:S(2)}) collective-permute-start(bf16[2,192,768]{2,1,0:T(8,128)(2,1)S(1)} %get-tuple-element.107), channel_id=1, source_target_pairs={{0,2},{1,9},{2,0},{3,11},{4,6},{5,13},{6,4},{7,15},{8,10},{9,1},{1... | collective-permute-start | bytes 1769480 | tf_op jit(solution)/shard_map/ppermute | solution.py:769
  78.3 3.1 %block.1 = (f32[512,768]{1,0:T(8,128)S(1)}, bf16[512,768]{1,0:T(8,128)(2,1)S(1)}) custom-call(s32[13]{0:T(128)S(1)} %stack.37.at_ref, bf16[2,512,1536]{2,1,0:T(8,128)(2,1)S(1)} %get-tuple-element.79.refs_0_.rows_ref, bf16[1536,768]{1,0:T(8,128)(2,1)S(1)} %copy-done.2, bf16[2,128,768]{2,1,0:T(8,128)(2,1)S(1)} %get-tuple-element.101.refs_0_.kept_ref), custom_call_target="tpu_custom_call" | custom-call | flops 1000 | bytes 1000 | tf_op jit(solution)/shard_map/block/pallas_call | solution.py:213
  84.3 3.0 %collective-permute-done.13.came_ref = bf16[2,192,768]{2,1,0:T(8,128)(2,1)S(1)} collective-permute-done((bf16[2,192,768]{2,1,0:T(8,128)(2,1)S(1)}, bf16[2,192,768]{2,1,0:T(8,128)(2,1)S(1)}, u32[]{:S(2)}, u32[]{:S(2)}) %collective-permute-start.13) | collective-permute-done | bytes 589856 | tf_op jit(solution)/shard_map/ppermute | solution.py:769
  88.0 2.1 %collective-permute-start.15 = (bf16[1,192,768]{2,1,0:T(8,128)(2,1)S(1)}, bf16[1,192,768]{2,1,0:T(8,128)(2,1)S(1)}, u32[]{:S(2)}, u32[]{:S(2)}) collective-permute-start(bf16[1,192,768]{2,1,0:T(8,128)(2,1)S(1)} %get-tuple-element.111), channel_id=1, source_target_pairs={{0,4},{1,3},{2,6},{3,1},{4,0},{5,7},{6,2},{7,5},{8,12},{9,11},{10,... | collective-permute-start | bytes 884744 | tf_op jit(solution)/shard_map/ppermute | solution.py:769
  92.8 2.0 %collective-permute-done.15.came_ref = bf16[1,192,768]{2,1,0:T(8,128)(2,1)S(1)} collective-permute-done((bf16[1,192,768]{2,1,0:T(8,128)(2,1)S(1)}, bf16[1,192,768]{2,1,0:T(8,128)(2,1)S(1)}, u32[]{:S(2)}, u32[]{:S(2)}) %collective-permute-start.15) | collective-permute-done | bytes 294944 | tf_op jit(solution)/shard_map/ppermute | solution.py:769
  94.8 3.1 %collective-permute-start.19 = (bf16[1,192,768]{2,1,0:T(8,128)(2,1)S(1)}, bf16[1,192,768]{2,1,0:T(8,128)(2,1)S(1)}, u32[]{:S(2)}, u32[]{:S(2)}) collective-permute-start(bf16[1,192,768]{2,1,0:T(8,128)(2,1)S(1)} %add.6.refs_0_.mine_ref), channel_id=1, source_target_pairs={{0,16},{1,17},{2,18},{3,19},{4,20},{5,21},{6,22},{7,23},{8,24},{9,... | collective-permute-start | bytes 884744 | tf_op jit(solution)/shard_map/ppermute | solution.py:769
  99.7 2.2 %collective-permute-start.18 = (bf16[1,128,768]{2,1,0:T(8,128)(2,1)S(1)}, bf16[1,128,768]{2,1,0:T(8,128)(2,1)S(1)}, u32[]{:S(2)}, u32[]{:S(2)}) collective-permute-start(bf16[1,128,768]{2,1,0:T(8,128)(2,1)S(1)} %get-tuple-element.118), channel_id=1, source_target_pairs={{0,8},{1,3},{2,10},{3,1},{4,12},{5,7},{6,14},{7,5},{8,0},{9,11},{1... | collective-permute-start | bytes 589832 | tf_op jit(solution)/shard_map/ppermute | solution.py:769
  104.1 2.6 %collective-permute-start.24 = (bf16[1,192,768]{2,1,0:T(8,128)(2,1)S(1)}, bf16[1,192,768]{2,1,0:T(8,128)(2,1)S(1)}, u32[]{:S(2)}, u32[]{:S(2)}) collective-permute-start(bf16[1,192,768]{2,1,0:T(8,128)(2,1)S(1)} %add.7.refs_0_.mine_ref), channel_id=1, source_target_pairs={{0,16},{1,17},{2,18},{3,19},{4,20},{5,21},{6,22},{7,23},{8,24},{9,... | collective-permute-start | bytes 884744 | tf_op jit(solution)/shard_map/ppermute | solution.py:769
  106.7 7.1 %unmix.1 = (bf16[8,512,768]{2,1,0:T(8,128)(2,1)}, bf16[512,768]{1,0:T(8,128)(2,1)}, f32[32,768]{1,0:T(8,128)S(1)}) custom-call(f32[8]{0:T(128)S(1)} %copy-done.9, f32[1,768]{1,0:T(1,128)S(1)} %copy-done.8, f32[512,768]{1,0:T(8,128)S(1)} %copy-done.5, f32[512,768]{1,0:T(8,128)S(1)} %get-tuple-element.80.middle_ref, ...), custom_call_target="tpu_custom_call" | custom-call | flops 1000 | bytes 1000 | tf_op jit(solution)/shard_map/unmix/pallas_call | solution.py:163
  113.8 6.6 %collective-permute-done.19.came_ref = bf16[1,192,768]{2,1,0:T(8,128)(2,1)S(1)} collective-permute-done((bf16[1,192,768]{2,1,0:T(8,128)(2,1)S(1)}, bf16[1,192,768]{2,1,0:T(8,128)(2,1)S(1)}, u32[]{:S(2)}, u32[]{:S(2)}) %collective-permute-start.19) | collective-permute-done | bytes 294944 | tf_op jit(solution)/shard_map/ppermute | solution.py:769
  121.0 2.0 %collective-permute-start.27 = (bf16[1,192,768]{2,1,0:T(8,128)(2,1)S(1)}, bf16[1,192,768]{2,1,0:T(8,128)(2,1)S(1)}, u32[]{:S(2)}, u32[]{:S(2)}) collective-permute-start(bf16[1,192,768]{2,1,0:T(8,128)(2,1)S(1)} %again.4.refs_0_.mine_ref), channel_id=1, source_target_pairs={{0,4},{1,9},{2,6},{3,11},{4,0},{5,13},{6,2},{7,15},{8,12},{9,1},{1... | collective-permute-start | bytes 884744 | tf_op jit(solution)/shard_map/ppermute | solution.py:769
  124.5 6.7 %collective-permute-done.20.came_ref = bf16[1,64,768]{2,1,0:T(8,128)(2,1)S(1)} collective-permute-done((bf16[1,64,768]{2,1,0:T(8,128)(2,1)S(1)}, bf16[1,64,768]{2,1,0:T(8,128)(2,1)S(1)}, u32[]{:S(2)}, u32[]{:S(2)}) %collective-permute-start.20) | collective-permute-done | bytes 98336 | tf_op jit(solution)/shard_map/ppermute | solution.py:769
  135.6 5.1 %collective-permute-done.26.came_ref = bf16[1,192,768]{2,1,0:T(8,128)(2,1)S(1)} collective-permute-done((bf16[1,192,768]{2,1,0:T(8,128)(2,1)S(1)}, bf16[1,192,768]{2,1,0:T(8,128)(2,1)S(1)}, u32[]{:S(2)}, u32[]{:S(2)}) %collective-permute-start.26) | collective-permute-done | bytes 294944 | tf_op jit(solution)/shard_map/ppermute | solution.py:769
  141.4 4.1 %collective-permute-done.25.came_ref = bf16[1,128,768]{2,1,0:T(8,128)(2,1)S(1)} collective-permute-done((bf16[1,128,768]{2,1,0:T(8,128)(2,1)S(1)}, bf16[1,128,768]{2,1,0:T(8,128)(2,1)S(1)}, u32[]{:S(2)}, u32[]{:S(2)}) %collective-permute-start.25) | collective-permute-done | bytes 196640 | tf_op jit(solution)/shard_map/ppermute | solution.py:769
  147.0 2.3 %collective-permute-start.34 = (bf16[2,128,768]{2,1,0:T(8,128)(2,1)S(1)}, bf16[2,128,768]{2,1,0:T(8,128)(2,1)S(1)}, u32[]{:S(2)}, u32[]{:S(2)}) collective-permute-start(bf16[2,128,768]{2,1,0:T(8,128)(2,1)S(1)} %join.10.refs_0_.mine_ref), channel_id=1, source_target_pairs={{0,4},{1,9},{2,6},{3,11},{4,0},{5,13},{6,2},{7,15},{8,12},{9,1},{1... | collective-permute-start | bytes 1179656 | tf_op jit(solution)/shard_map/ppermute | solution.py:769
  149.3 4.7 %collective-permute-done.28.came_ref = bf16[2,64,768]{2,1,0:T(8,128)(2,1)S(1)} collective-permute-done((bf16[2,64,768]{2,1,0:T(8,128)(2,1)S(1)}, bf16[2,64,768]{2,1,0:T(8,128)(2,1)S(1)}, u32[]{:S(2)}, u32[]{:S(2)}) %collective-permute-start.28) | collective-permute-done | bytes 196640 | tf_op jit(solution)/shard_map/ppermute | solution.py:769
  157.6 7.0 %collective-permute-done.29.came_ref = bf16[3,64,768]{2,1,0:T(8,128)(2,1)S(1)} collective-permute-done((bf16[3,64,768]{2,1,0:T(8,128)(2,1)S(1)}, bf16[3,64,768]{2,1,0:T(8,128)(2,1)S(1)}, u32[]{:S(2)}, u32[]{:S(2)}) %collective-permute-start.29) | collective-permute-done | bytes 294944 | tf_op jit(solution)/shard_map/ppermute | solution.py:769
  169.1 8.3 %collective-permute-done.32.came_ref = bf16[4,192,768]{2,1,0:T(8,128)(2,1)S(1)} collective-permute-done((bf16[4,192,768]{2,1,0:T(8,128)(2,1)S(1)}, bf16[4,192,768]{2,1,0:T(8,128)(2,1)S(1)}, u32[]{:S(2)}, u32[]{:S(2)}) %collective-permute-start.32) | collective-permute-done | bytes 1179680 | tf_op jit(solution)/shard_map/ppermute | solution.py:769
  177.4 2.9 %finish_mlp.2 = (f32[768,1536]{1,0:T(8,128)}, f32[1536,768]{1,0:T(8,128)}, f32[32,768]{1,0:T(8,128)S(1)}) custom-call(s32[13]{0:T(128)S(1)} %stack.37.at_ref, bf16[4,192,768]{2,1,0:T(8,128)(2,1)S(1)} %join.12.refs_0_.mine_ref, bf16[4,192,768]{2,1,0:T(8,128)(2,1)S(1)} %collective-permute-done.32.came_ref, bf16[4,192,768]{2,1,0:T(8,128)(2,1)S(1)} %join.15.refs_0_.mine_ref), custom_call_target="tpu_custom_call" | custom-call | flops 1000 | bytes 1000 | tf_op jit(solution)/shard_map/finish_mlp/pallas_call | solution.py:720
  180.3 4.0 %collective-permute-done.31.came_ref = bf16[5,64,768]{2,1,0:T(8,128)(2,1)S(1)} collective-permute-done((bf16[5,64,768]{2,1,0:T(8,128)(2,1)S(1)}, bf16[5,64,768]{2,1,0:T(8,128)(2,1)S(1)}, u32[]{:S(2)}, u32[]{:S(2)}) %collective-permute-start.31) | collective-permute-done | bytes 491552 | tf_op jit(solution)/shard_map/ppermute | solution.py:769
  186.1 2.3 %finish_attend.3 = (f32[3,768,384]{2,1,0:T(8,128)}, f32[384,768]{1,0:T(8,128)}, f32[32,768]{1,0:T(8,128)S(1)}) custom-call(s32[13]{0:T(128)S(1)} %stack.37.at_ref, bf16[4,128,768]{2,1,0:T(8,128)(2,1)S(1)} %join.14.refs_0_.mine_ref, bf16[4,128,768]{2,1,0:T(8,128)(2,1)S(1)} %collective-permute-done.35.came_ref, ...), custom_call_target="tpu_custom_call", output_to_operand_aliasing={{0}: (3, {}), {1}: (4, {})} | custom-call | flops 1000 | bytes 1000 | tf_op jit(solution)/shard_map/finish_attend/pallas_call | solution.py:720
  190.0 3.5 %finish_mlp.3 = (f32[768,1536]{1,0:T(8,128)}, f32[1536,768]{1,0:T(8,128)}, f32[32,768]{1,0:T(8,128)}) custom-call(s32[13]{0:T(128)S(1)} %stack.37.at_ref, bf16[4,192,768]{2,1,0:T(8,128)(2,1)S(1)} %join.15.refs_0_.mine_ref, bf16[4,192,768]{2,1,0:T(8,128)(2,1)S(1)} %collective-permute-done.36.came_ref, ...), custom_call_target="tpu_custom_call", output_to_operand_aliasing={{0}: (3, {}), {1}: (4, {})} | custom-call | flops 1000 | bytes 1000 | tf_op jit(solution)/shard_map/finish_mlp/pallas_call | solution.py:720
  (113 shorter events, 45.7 us)
Async XLA Ops:
  23.7 3.5 %collective-permute-start.3 = (bf16[512,768]{1,0:T(8,128)(2,1)S(1)}, bf16[512,768]{1,0:T(8,128)(2,1)S(1)}, u32[]{:S(2)}, u32[]{:S(2)}) collective-permute-start(bf16[512,768]{1,0:T(8,128)(2,1)S(1)} %copy-done.6), channel_id=1, source_target_pairs={{0,1},{1,0},{2,3},{3,2},{4,5},{5,4},{6,7},{7,6},{8,9},{9,8},{10,11... | collective-permute-start | bytes 2359304 | tf_op jit(solution)/shard_map/ppermute | solution.py:755
  44.1 20.6 %collective-permute-start.6 = (bf16[4,192,768]{2,1,0:T(8,128)(2,1)S(1)}, bf16[4,192,768]{2,1,0:T(8,128)(2,1)S(1)}, u32[]{:S(2)}, u32[]{:S(2)}) collective-permute-start(bf16[4,192,768]{2,1,0:T(8,128)(2,1)S(1)} %get-tuple-element.91), channel_id=1, source_target_pairs={{0,8},{1,3},{2,10},{3,1},{4,12},{5,7},{6,14},{7,5},{8,0},{9,11},{1... | collective-permute-start | bytes 3538952 | tf_op jit(solution)/shard_map/ppermute | solution.py:769
  48.7 26.0 %collective-permute-start.9 = (bf16[4,192,768]{2,1,0:T(8,128)(2,1)S(1)}, bf16[4,192,768]{2,1,0:T(8,128)(2,1)S(1)}, u32[]{:S(2)}, u32[]{:S(2)}) collective-permute-start(bf16[4,192,768]{2,1,0:T(8,128)(2,1)S(1)} %get-tuple-element.99), channel_id=1, source_target_pairs={{0,8},{1,5},{2,10},{3,7},{4,12},{5,1},{6,14},{7,3},{8,0},{9,13},{1... | collective-permute-start | bytes 3538952 | tf_op jit(solution)/shard_map/ppermute | solution.py:769
  62.6 15.0 %collective-permute-start.8 = (bf16[4,128,768]{2,1,0:T(8,128)(2,1)S(1)}, bf16[4,128,768]{2,1,0:T(8,128)(2,1)S(1)}, u32[]{:S(2)}, u32[]{:S(2)}) collective-permute-start(bf16[4,128,768]{2,1,0:T(8,128)(2,1)S(1)} %get-tuple-element.97), channel_id=1, source_target_pairs={{0,2},{1,5},{2,0},{3,7},{4,6},{5,1},{6,4},{7,3},{8,10},{9,13},{10,... | collective-permute-start | bytes 2359304 | tf_op jit(solution)/shard_map/ppermute | solution.py:769
  65.6 16.5 %collective-permute-start.14 = (bf16[2,192,768]{2,1,0:T(8,128)(2,1)S(1)}, bf16[2,192,768]{2,1,0:T(8,128)(2,1)S(1)}, u32[]{:S(2)}, u32[]{:S(2)}) collective-permute-start(bf16[2,192,768]{2,1,0:T(8,128)(2,1)S(1)} %get-tuple-element.108), channel_id=1, source_target_pairs={{0,2},{1,5},{2,0},{3,7},{4,6},{5,1},{6,4},{7,3},{8,10},{9,13},{10,... | collective-permute-start | bytes 1769480 | tf_op jit(solution)/shard_map/ppermute | solution.py:769
  75.5 11.8 %collective-permute-start.13 = (bf16[2,192,768]{2,1,0:T(8,128)(2,1)S(1)}, bf16[2,192,768]{2,1,0:T(8,128)(2,1)S(1)}, u32[]{:S(2)}, u32[]{:S(2)}) collective-permute-start(bf16[2,192,768]{2,1,0:T(8,128)(2,1)S(1)} %get-tuple-element.107), channel_id=1, source_target_pairs={{0,2},{1,9},{2,0},{3,11},{4,6},{5,13},{6,4},{7,15},{8,10},{9,1},{1... | collective-permute-start | bytes 1769480 | tf_op jit(solution)/shard_map/ppermute | solution.py:769
  77.6 26.5 %collective-permute-start.7 = (bf16[512,768]{1,0:T(8,128)(2,1)S(1)}, bf16[512,768]{1,0:T(8,128)(2,1)S(1)}, u32[]{:S(2)}, u32[]{:S(2)}) collective-permute-start(bf16[512,768]{1,0:T(8,128)(2,1)S(1)} %get-tuple-element.95), channel_id=1, source_target_pairs={{0,1},{1,0},{2,3},{3,2},{4,5},{5,4},{6,7},{7,6},{8,9},{9,8},{10,11... | collective-permute-start | bytes 2359304 | tf_op jit(solution)/shard_map/ppermute | solution.py:755
  81.5 25.2 %collective-permute-start.10 = (bf16[512,768]{1,0:T(8,128)(2,1)S(1)}, bf16[512,768]{1,0:T(8,128)(2,1)S(1)}, u32[]{:S(2)}, u32[]{:S(2)}) collective-permute-start(bf16[512,768]{1,0:T(8,128)(2,1)S(1)} %get-tuple-element.103), channel_id=1, source_target_pairs={{0,1},{1,0},{2,3},{3,2},{4,5},{5,4},{6,7},{7,6},{8,9},{9,8},{10,11... | collective-permute-start | bytes 2359304 | tf_op jit(solution)/shard_map/ppermute | solution.py:755
  82.8 7.5 %collective-permute-start.16 = (bf16[1,192,768]{2,1,0:T(8,128)(2,1)S(1)}, bf16[1,192,768]{2,1,0:T(8,128)(2,1)S(1)}, u32[]{:S(2)}, u32[]{:S(2)}) collective-permute-start(bf16[1,192,768]{2,1,0:T(8,128)(2,1)S(1)} %get-tuple-element.112), channel_id=1, source_target_pairs={{0,4},{1,9},{2,6},{3,11},{4,0},{5,13},{6,2},{7,15},{8,12},{9,1},{1... | collective-permute-start | bytes 884744 | tf_op jit(solution)/shard_map/ppermute | solution.py:769
  88.0 6.8 %collective-permute-start.15 = (bf16[1,192,768]{2,1,0:T(8,128)(2,1)S(1)}, bf16[1,192,768]{2,1,0:T(8,128)(2,1)S(1)}, u32[]{:S(2)}, u32[]{:S(2)}) collective-permute-start(bf16[1,192,768]{2,1,0:T(8,128)(2,1)S(1)} %get-tuple-element.111), channel_id=1, source_target_pairs={{0,4},{1,3},{2,6},{3,1},{4,0},{5,7},{6,2},{7,5},{8,12},{9,11},{10,... | collective-permute-start | bytes 884744 | tf_op jit(solution)/shard_map/ppermute | solution.py:769
  90.1 8.9 %collective-permute-start.12 = (bf16[2,128,768]{2,1,0:T(8,128)(2,1)S(1)}, bf16[2,128,768]{2,1,0:T(8,128)(2,1)S(1)}, u32[]{:S(2)}, u32[]{:S(2)}) collective-permute-start(bf16[2,128,768]{2,1,0:T(8,128)(2,1)S(1)} %get-tuple-element.106), channel_id=1, source_target_pairs={{0,4},{1,9},{2,6},{3,11},{4,0},{5,13},{6,2},{7,15},{8,12},{9,1},{1... | collective-permute-start | bytes 1179656 | tf_op jit(solution)/shard_map/ppermute | solution.py:769
  90.2 11.6 %collective-permute-start.11 = (bf16[4,64,768]{2,1,0:T(8,128)(2,1)S(1)}, bf16[4,64,768]{2,1,0:T(8,128)(2,1)S(1)}, u32[]{:S(2)}, u32[]{:S(2)}) collective-permute-start(bf16[4,64,768]{2,1,0:T(8,128)(2,1)S(1)} %get-tuple-element.105), channel_id=1, source_target_pairs={{0,2},{1,9},{2,0},{3,11},{4,6},{5,13},{6,4},{7,15},{8,10},{9,1},{1... | collective-permute-start | bytes 1179656 | tf_op jit(solution)/shard_map/ppermute | solution.py:769
  94.8 25.5 %collective-permute-start.19 = (bf16[1,192,768]{2,1,0:T(8,128)(2,1)S(1)}, bf16[1,192,768]{2,1,0:T(8,128)(2,1)S(1)}, u32[]{:S(2)}, u32[]{:S(2)}) collective-permute-start(bf16[1,192,768]{2,1,0:T(8,128)(2,1)S(1)} %add.6.refs_0_.mine_ref), channel_id=1, source_target_pairs={{0,16},{1,17},{2,18},{3,19},{4,20},{5,21},{6,22},{7,23},{8,24},{9,... | collective-permute-start | bytes 884744 | tf_op jit(solution)/shard_map/ppermute | solution.py:769
  99.7 23.3 %collective-permute-start.18 = (bf16[1,128,768]{2,1,0:T(8,128)(2,1)S(1)}, bf16[1,128,768]{2,1,0:T(8,128)(2,1)S(1)}, u32[]{:S(2)}, u32[]{:S(2)}) collective-permute-start(bf16[1,128,768]{2,1,0:T(8,128)(2,1)S(1)} %get-tuple-element.118), channel_id=1, source_target_pairs={{0,8},{1,3},{2,10},{3,1},{4,12},{5,7},{6,14},{7,5},{8,0},{9,11},{1... | collective-permute-start | bytes 589832 | tf_op jit(solution)/shard_map/ppermute | solution.py:769
  102.5 21.2 %collective-permute-start.17 = (bf16[2,64,768]{2,1,0:T(8,128)(2,1)S(1)}, bf16[2,64,768]{2,1,0:T(8,128)(2,1)S(1)}, u32[]{:S(2)}, u32[]{:S(2)}) collective-permute-start(bf16[2,64,768]{2,1,0:T(8,128)(2,1)S(1)} %get-tuple-element.117), channel_id=1, source_target_pairs={{0,4},{1,3},{2,6},{3,1},{4,0},{5,7},{6,2},{7,5},{8,12},{9,11},{10,... | collective-permute-start | bytes 589832 | tf_op jit(solution)/shard_map/ppermute | solution.py:769
  104.1 27.7 %collective-permute-start.24 = (bf16[1,192,768]{2,1,0:T(8,128)(2,1)S(1)}, bf16[1,192,768]{2,1,0:T(8,128)(2,1)S(1)}, u32[]{:S(2)}, u32[]{:S(2)}) collective-permute-start(bf16[1,192,768]{2,1,0:T(8,128)(2,1)S(1)} %add.7.refs_0_.mine_ref), channel_id=1, source_target_pairs={{0,16},{1,17},{2,18},{3,19},{4,20},{5,21},{6,22},{7,23},{8,24},{9,... | collective-permute-start | bytes 884744 | tf_op jit(solution)/shard_map/ppermute | solution.py:769
  121.0 13.8 %collective-permute-start.27 = (bf16[1,192,768]{2,1,0:T(8,128)(2,1)S(1)}, bf16[1,192,768]{2,1,0:T(8,128)(2,1)S(1)}, u32[]{:S(2)}, u32[]{:S(2)}) collective-permute-start(bf16[1,192,768]{2,1,0:T(8,128)(2,1)S(1)} %again.4.refs_0_.mine_ref), channel_id=1, source_target_pairs={{0,4},{1,9},{2,6},{3,11},{4,0},{5,13},{6,2},{7,15},{8,12},{9,1},{1... | collective-permute-start | bytes 884744 | tf_op jit(solution)/shard_map/ppermute | solution.py:769
  123.6 10.6 %collective-permute-start.23 = (bf16[1,128,768]{2,1,0:T(8,128)(2,1)S(1)}, bf16[1,128,768]{2,1,0:T(8,128)(2,1)S(1)}, u32[]{:S(2)}, u32[]{:S(2)}) collective-permute-start(bf16[1,128,768]{2,1,0:T(8,128)(2,1)S(1)} %add.8.refs_0_.mine_ref), channel_id=1, source_target_pairs={{0,16},{1,17},{2,18},{3,19},{4,20},{5,21},{6,22},{7,23},{8,24},{9,... | collective-permute-start | bytes 589832 | tf_op jit(solution)/shard_map/ppermute | solution.py:769
  124.3 6.9 %collective-permute-start.20 = (bf16[1,64,768]{2,1,0:T(8,128)(2,1)S(1)}, bf16[1,64,768]{2,1,0:T(8,128)(2,1)S(1)}, u32[]{:S(2)}, u32[]{:S(2)}) collective-permute-start(bf16[1,64,768]{2,1,0:T(8,128)(2,1)S(1)} %get-tuple-element.121), channel_id=1, source_target_pairs={{0,8},{1,5},{2,10},{3,7},{4,12},{5,1},{6,14},{7,3},{8,0},{9,13},{1... | collective-permute-start | bytes 294920 | tf_op jit(solution)/shard_map/ppermute | solution.py:769
  124.4 6.8 %collective-permute-start.21 = (f32[32,768]{1,0:T(8,128)S(1)}, f32[32,768]{1,0:T(8,128)S(1)}, u32[]{:S(2)}, u32[]{:S(2)}) collective-permute-start(f32[32,768]{1,0:T(8,128)S(1)} %get-tuple-element.119.refs_0_.mine_ref), channel_id=1, source_target_pairs={{0,1},{1,0},{2,3},{3,2},{4,5},{5,4},{6,7},{7,6},{8,9},{9,8},{10,11... | collective-permute-start | bytes 294920 | tf_op jit(solution)/shard_map/ppermute | solution.py:755
  132.4 8.3 %collective-permute-start.26 = (bf16[1,192,768]{2,1,0:T(8,128)(2,1)S(1)}, bf16[1,192,768]{2,1,0:T(8,128)(2,1)S(1)}, u32[]{:S(2)}, u32[]{:S(2)}) collective-permute-start(bf16[1,192,768]{2,1,0:T(8,128)(2,1)S(1)} %again.5.refs_0_.mine_ref), channel_id=1, source_target_pairs={{0,4},{1,3},{2,6},{3,1},{4,0},{5,7},{6,2},{7,5},{8,12},{9,11},{10,... | collective-permute-start | bytes 884744 | tf_op jit(solution)/shard_map/ppermute | solution.py:769
  135.4 20.5 %collective-permute-start.30 = (bf16[2,192,768]{2,1,0:T(8,128)(2,1)S(1)}, bf16[2,192,768]{2,1,0:T(8,128)(2,1)S(1)}, u32[]{:S(2)}, u32[]{:S(2)}) collective-permute-start(bf16[2,192,768]{2,1,0:T(8,128)(2,1)S(1)} %join.8.refs_0_.mine_ref), channel_id=1, source_target_pairs={{0,2},{1,5},{2,0},{3,7},{4,6},{5,1},{6,4},{7,3},{8,10},{9,13},{10,... | collective-permute-start | bytes 1769480 | tf_op jit(solution)/shard_map/ppermute | solution.py:769
  135.5 10.0 %collective-permute-start.25 = (bf16[1,128,768]{2,1,0:T(8,128)(2,1)S(1)}, bf16[1,128,768]{2,1,0:T(8,128)(2,1)S(1)}, u32[]{:S(2)}, u32[]{:S(2)}) collective-permute-start(bf16[1,128,768]{2,1,0:T(8,128)(2,1)S(1)} %again.6.refs_0_.mine_ref), channel_id=1, source_target_pairs={{0,8},{1,3},{2,10},{3,1},{4,12},{5,7},{6,14},{7,5},{8,0},{9,11},{1... | collective-permute-start | bytes 589832 | tf_op jit(solution)/shard_map/ppermute | solution.py:769
  135.5 10.5 %collective-permute-start.22 = (bf16[2,64,768]{2,1,0:T(8,128)(2,1)S(1)}, bf16[2,64,768]{2,1,0:T(8,128)(2,1)S(1)}, u32[]{:S(2)}, u32[]{:S(2)}) collective-permute-start(bf16[2,64,768]{2,1,0:T(8,128)(2,1)S(1)} %add.9.refs_0_.mine_ref), channel_id=1, source_target_pairs={{0,16},{1,17},{2,18},{3,19},{4,20},{5,21},{6,22},{7,23},{8,24},{9,... | collective-permute-start | bytes 589832 | tf_op jit(solution)/shard_map/ppermute | solution.py:769
  141.3 24.5 %collective-permute-start.33 = (bf16[2,192,768]{2,1,0:T(8,128)(2,1)S(1)}, bf16[2,192,768]{2,1,0:T(8,128)(2,1)S(1)}, u32[]{:S(2)}, u32[]{:S(2)}) collective-permute-start(bf16[2,192,768]{2,1,0:T(8,128)(2,1)S(1)} %join.9.refs_0_.mine_ref), channel_id=1, source_target_pairs={{0,2},{1,9},{2,0},{3,11},{4,6},{5,13},{6,4},{7,15},{8,10},{9,1},{1... | collective-permute-start | bytes 1769480 | tf_op jit(solution)/shard_map/ppermute | solution.py:769
  146.7 7.3 %collective-permute-start.28 = (bf16[2,64,768]{2,1,0:T(8,128)(2,1)S(1)}, bf16[2,64,768]{2,1,0:T(8,128)(2,1)S(1)}, u32[]{:S(2)}, u32[]{:S(2)}) collective-permute-start(bf16[2,64,768]{2,1,0:T(8,128)(2,1)S(1)} %again.7.mine_ref.refs_0_), channel_id=1, source_target_pairs={{0,8},{1,5},{2,10},{3,7},{4,12},{5,1},{6,14},{7,3},{8,0},{9,13},{1... | collective-permute-start | bytes 589832 | tf_op jit(solution)/shard_map/ppermute | solution.py:769
  147.0 18.2 %collective-permute-start.34 = (bf16[2,128,768]{2,1,0:T(8,128)(2,1)S(1)}, bf16[2,128,768]{2,1,0:T(8,128)(2,1)S(1)}, u32[]{:S(2)}, u32[]{:S(2)}) collective-permute-start(bf16[2,128,768]{2,1,0:T(8,128)(2,1)S(1)} %join.10.refs_0_.mine_ref), channel_id=1, source_target_pairs={{0,4},{1,9},{2,6},{3,11},{4,0},{5,13},{6,2},{7,15},{8,12},{9,1},{1... | collective-permute-start | bytes 1179656 | tf_op jit(solution)/shard_map/ppermute | solution.py:769
  154.6 9.9 %collective-permute-start.29 = (bf16[3,64,768]{2,1,0:T(8,128)(2,1)S(1)}, bf16[3,64,768]{2,1,0:T(8,128)(2,1)S(1)}, u32[]{:S(2)}, u32[]{:S(2)}) collective-permute-start(bf16[3,64,768]{2,1,0:T(8,128)(2,1)S(1)} %join.11.refs_0_.mine_ref), channel_id=1, source_target_pairs={{0,4},{1,3},{2,6},{3,1},{4,0},{5,7},{6,2},{7,5},{8,12},{9,11},{10,... | collective-permute-start | bytes 884744 | tf_op jit(solution)/shard_map/ppermute | solution.py:769
  156.5 20.8 %collective-permute-start.32 = (bf16[4,192,768]{2,1,0:T(8,128)(2,1)S(1)}, bf16[4,192,768]{2,1,0:T(8,128)(2,1)S(1)}, u32[]{:S(2)}, u32[]{:S(2)}) collective-permute-start(bf16[4,192,768]{2,1,0:T(8,128)(2,1)S(1)} %join.12.refs_0_.mine_ref), channel_id=1, source_target_pairs={{0,8},{1,3},{2,10},{3,1},{4,12},{5,7},{6,14},{7,5},{8,0},{9,11},{1... | collective-permute-start | bytes 3538952 | tf_op jit(solution)/shard_map/ppermute | solution.py:769
  166.4 23.6 %collective-permute-start.36 = (bf16[4,192,768]{2,1,0:T(8,128)(2,1)S(1)}, bf16[4,192,768]{2,1,0:T(8,128)(2,1)S(1)}, u32[]{:S(2)}, u32[]{:S(2)}) collective-permute-start(bf16[4,192,768]{2,1,0:T(8,128)(2,1)S(1)} %join.15.refs_0_.mine_ref), channel_id=1, source_target_pairs={{0,8},{1,5},{2,10},{3,7},{4,12},{5,1},{6,14},{7,3},{8,0},{9,13},{1... | collective-permute-start | bytes 3538952 | tf_op jit(solution)/shard_map/ppermute | solution.py:769
  167.1 19.1 %collective-permute-start.35 = (bf16[4,128,768]{2,1,0:T(8,128)(2,1)S(1)}, bf16[4,128,768]{2,1,0:T(8,128)(2,1)S(1)}, u32[]{:S(2)}, u32[]{:S(2)}) collective-permute-start(bf16[4,128,768]{2,1,0:T(8,128)(2,1)S(1)} %join.14.refs_0_.mine_ref), channel_id=1, source_target_pairs={{0,2},{1,5},{2,0},{3,7},{4,6},{5,1},{6,4},{7,3},{8,10},{9,13},{10,... | collective-permute-start | bytes 2359304 | tf_op jit(solution)/shard_map/ppermute | solution.py:769
  167.8 16.6 %collective-permute-start.31 = (bf16[5,64,768]{2,1,0:T(8,128)(2,1)S(1)}, bf16[5,64,768]{2,1,0:T(8,128)(2,1)S(1)}, u32[]{:S(2)}, u32[]{:S(2)}) collective-permute-start(bf16[5,64,768]{2,1,0:T(8,128)(2,1)S(1)} %join.13.refs_0_.mine_ref), channel_id=1, source_target_pairs={{0,2},{1,9},{2,0},{3,11},{4,6},{5,13},{6,4},{7,15},{8,10},{9,1},{1... | collective-permute-start | bytes 1474568 | tf_op jit(solution)/shard_map/ppermute | solution.py:769
  (18 other events, 179.8 us)
